TPU v7x, 32 devices: a whole 2x2x4 slice. The times are simulated.
32 devices in a mesh: rows: 4 (over y, x), seq: 8 (over z, core).
Axes of the slice: x: 2, y: 2, z: 4, core: 2. Of those that a mesh axis runs over, the one named last changes fastest.
Arguments:
- tokens: bfloat16 [4, 1024, 1024], P('rows', 'seq'), may hold values from -6 to 6
- cotangent: bfloat16 [4, 1024, 1024], P('rows', 'seq'), may hold values from -6 to 6
- doc_lengths: int32 [4, 8], P('rows'), may hold values from 1 to 512, 1024 in all within a row
- norm_gain: float32 [1024], replicated, may hold values from 0.5 to 1.5
- in_proj: bfloat16 [1024, 4096], replicated, may hold values from -0.1875 to 0.1875
- conv_weight: float32 [4, 2048], replicated, may hold values from -3 to 3
- conv_bias: float32 [2048], replicated, may hold values from -3 to 3
- x_proj: bfloat16 [2048, 96], replicated, may hold values from -0.125 to 0.125
- dt_proj: bfloat16 [64, 2048], replicated, may hold values from -0.75 to 0.75
- dt_bias: float32 [2048], replicated, may hold values from -6.5 to -2.5
- a_log: float32 [16, 2048], replicated, may hold values from 0 to 2.77
- d_skip: float32 [2048], replicated, may hold values from 0.5 to 1.5
- out_proj: bfloat16 [2048, 1024], replicated, may hold values from -0.25 to 0.25
- moment_norm_gain: float32 [1024], P('seq'), may hold values from -0.0024414062 to 0.0024414062
- moment_in_proj: float32 [1024, 4096], P('seq'), may hold values from -0.0024414062 to 0.0024414062
- moment_conv_weight: float32 [4, 2048], P(None, 'seq'), may hold values from -0.0024414062 to 0.0024414062
- moment_conv_bias: float32 [2048], P('seq'), may hold values from -0.0024414062 to 0.0024414062
- moment_x_proj: float32 [2048, 96], P('seq'), may hold values from -0.0024414062 to 0.0024414062
- moment_dt_proj: float32 [64, 2048], P(None, 'seq'), may hold values from -0.0024414062 to 0.0024414062
- moment_dt_bias: float32 [2048], P('seq'), may hold values from -0.0024414062 to 0.0024414062
- moment_a_log: float32 [16, 2048], P(None, 'seq'), may hold values from -0.0024414062 to 0.0024414062
- moment_d_skip: float32 [2048], P('seq'), may hold values from -0.0024414062 to 0.0024414062
- moment_out_proj: float32 [2048, 1024], P('seq'), may hold values from -0.0024414062 to 0.0024414062
- average_norm_gain: float32 [1024], P('seq'), may hold values from 0.5 to 1.5
- average_in_proj: float32 [1024, 4096], P('seq'), may hold values from -0.1875 to 0.1875
- average_conv_weight: float32 [4, 2048], P(None, 'seq'), may hold values from -3 to 3
- average_conv_bias: float32 [2048], P('seq'), may hold values from -3 to 3
- average_x_proj: float32 [2048, 96], P('seq'), may hold values from -0.125 to 0.125
- average_dt_proj: float32 [64, 2048], P(None, 'seq'), may hold values from -0.75 to 0.75
- average_dt_bias: float32 [2048], P('seq'), may hold values from -6.5 to 1.5
- average_a_log: float32 [16, 2048], P(None, 'seq'), may hold values from 0 to 2.77
- average_d_skip: float32 [2048], P('seq'), may hold values from 0.5 to 1.5
- average_out_proj: float32 [2048, 1024], P('seq'), may hold values from -0.25 to 0.25
Outputs:
- block_output: float32 [4, 1024, 1024], P('rows', 'seq')
- input_grad: float32 [4, 1024, 1024], P('rows', 'seq')
- grad_norm: float32 [], replicated
- new_moment_norm_gain: float32 [1024], P('seq')
- new_weight_norm_gain: float32 [1024], P('seq')
- new_average_norm_gain: float32 [1024], P('seq')
- new_moment_in_proj: float32 [1024, 4096], P('seq')
- new_weight_in_proj: float32 [1024, 4096], P('seq')
- new_average_in_proj: float32 [1024, 4096], P('seq')
- new_moment_conv_weight: float32 [4, 2048], P(None, 'seq')
- new_weight_conv_weight: float32 [4, 2048], P(None, 'seq')
- new_average_conv_weight: float32 [4, 2048], P(None, 'seq')
- new_moment_conv_bias: float32 [2048], P('seq')
- new_weight_conv_bias: float32 [2048], P('seq')
- new_average_conv_bias: float32 [2048], P('seq')
- new_moment_x_proj: float32 [2048, 96], P('seq')
- new_weight_x_proj: float32 [2048, 96], P('seq')
- new_average_x_proj: float32 [2048, 96], P('seq')
- new_moment_dt_proj: float32 [64, 2048], P(None, 'seq')
- new_weight_dt_proj: float32 [64, 2048], P(None, 'seq')
- new_average_dt_proj: float32 [64, 2048], P(None, 'seq')
- new_moment_dt_bias: float32 [2048], P('seq')
- new_weight_dt_bias: float32 [2048], P('seq')
- new_average_dt_bias: float32 [2048], P('seq')
- new_moment_a_log: float32 [16, 2048], P(None, 'seq')
- new_weight_a_log: float32 [16, 2048], P(None, 'seq')
- new_average_a_log: float32 [16, 2048], P(None, 'seq')
- new_moment_d_skip: float32 [2048], P('seq')
- new_weight_d_skip: float32 [2048], P('seq')
- new_average_d_skip: float32 [2048], P('seq')
- new_moment_out_proj: float32 [2048, 1024], P('seq')
- new_weight_out_proj: float32 [2048, 1024], P('seq')
- new_average_out_proj: float32 [2048, 1024], P('seq')
All inputs are finite; a program needn't handle non-finite values.
Results may differ from a plain program's by a relative error of at most 0.008.
The roundings to bfloat16 on the way count: a program that leaves them out, or rounds other values in their place, can miss the bound.
Values may be sent and summed in bfloat16 or wider, within the bound.
A program may use at most 384 MiB of HBM per device.

v0:
```python
import math

import jax
import jax.numpy as jnp
from jax import lax
from jax.experimental import pallas as pl
from jax.experimental.pallas import tpu as pltpu
from jax.sharding import PartitionSpec as P

D = 1024
E = 2048
N = 16
R = 64
K = 4
PARAMS = 6667264

LANES = 128
RESET = 1e30


EPS = 1e-05
MOMENTUM = 0.9
AVERAGE = 0.9
RATES = (0.1, 0.03, 0.1, 0.1, 0.03, 0.03, 0.3, 0.3, 0.1, 0.03)


def silu(values):
    return values * jax.nn.sigmoid(values)


def silu_slope(values):
    sigmoid_of = jax.nn.sigmoid(values)
    return sigmoid_of * (1.0 + values * (1.0 - sigmoid_of))


def doc_tables(lengths_row, positions):
    ends = jnp.cumsum(lengths_row)
    starts = ends - lengths_row
    docid = jnp.sum((positions[None, :] >= starts[:, None]).astype(jnp.int32), axis=0)
    first = jnp.sum((positions[None, :] == starts[:, None]).astype(jnp.int32), axis=0)
    return (docid, first > 0)


def ends_kernel(ddec_ref, drive_ref, grady_ref, inb_ref, outb_ref, rates_ref, ends_ref):
    groups, steps = ddec_ref.shape[:2]
    columns = [pl.ds(group * LANES, LANES) for group in range(groups)]

    def step(t, carry):
        hidden, decayed, pulled = carry
        in_row, out_row = inb_ref[t], outb_ref[t]
        new = ([], [], [])
        for group in range(groups):
            here = (group, pl.ds(t, 1))
            decay = jnp.exp2(ddec_ref[here] * rates_ref[:, columns[group]])
            new[0].append(decay * hidden[group] + drive_ref[here] * in_row)
            product = decay * decayed[group]
            new[1].append(product)
            new[2].append(pulled[group] + product * (grady_ref[here] * out_row))
        return new

    zeros = [jnp.zeros((N, LANES), jnp.float32) for _ in range(groups)]
    ones = [jnp.ones((N, LANES), jnp.float32) for _ in range(groups)]
    hidden, _, pulled = lax.fori_loop(0, steps, step, (zeros, ones, zeros), unroll=4)
    for group in range(groups):
        ends_ref[:N, columns[group]] = hidden[group]
        ends_ref[N : 2 * N, columns[group]] = pulled[group]
        total = jnp.sum(ddec_ref[group], axis=0, keepdims=True)
        ends_ref[2 * N :, columns[group]] = jnp.broadcast_to(total, (8, LANES))


def scan_kernel(
    member_ref,
    ddec_ref,
    drive_ref,
    grady_ref,
    inb_ref,
    outb_ref,
    rates_ref,
    all_ref,
    scanned_ref,
    along_ref,
    decayed_ref,
    gin_ref,
    gout_ref,
    grates_ref,
    kept,
    first,
    second,
):
    groups, steps = ddec_ref.shape[:2]
    devices = all_ref.shape[0]
    member = member_ref[0]
    columns = [pl.ds(group * LANES, LANES) for group in range(groups)]
    half = N // 2

    @pl.when(pl.program_id(0) == 0)
    def _():
        gin_ref[...] = jnp.zeros_like(gin_ref)
        gout_ref[...] = jnp.zeros_like(gout_ref)

    def through(device, state, offset):
        factor = jnp.exp2(all_ref[device, 2 * N : 2 * N + 1, :] * rates_ref[...])
        return factor * state + all_ref[device, offset : offset + N, :]

    nothing = jnp.zeros(rates_ref.shape, jnp.float32)
    entering = lax.fori_loop(0, member, lambda d, s: through(d, s, 0), nothing)
    leaving = lax.fori_loop(
        0, devices - 1 - member, lambda d, s: through(devices - 1 - d, s, N), nothing
    )

    def fold(values):
        return values[:half] + values[half:]

    def forward(t, hidden):
        in_row, out_row = inb_ref[t], outb_ref[t]
        new = []
        for group in range(groups):
            here = (group, pl.ds(t, 1))
            decay = jnp.exp2(ddec_ref[here] * rates_ref[:, columns[group]])
            state = decay * hidden[group] + drive_ref[here] * in_row
            kept[t + 1, :, columns[group]] = state
            first[group, pl.ds(pl.multiple_of(t * half, half), half), :] = fold(state * out_row)
            new.append(state)
        return new

    kept[0] = entering
    begin = [entering[:, group * LANES : (group + 1) * LANES] for group in range(groups)]
    lax.fori_loop(0, steps, forward, begin, unroll=4)

    def collapse(source, target_ref):
        for group in range(groups):
            total = source[group, pl.ds(0, steps, stride=half), :]
            for place in range(1, half):
                total = total + source[group, pl.ds(place, steps, stride=half), :]
            target_ref[group] = total

    collapse(first, scanned_ref)

    def backward(back, carry):
        later, grates = carry
        t = steps - 1 - back
        in_row, out_row = inb_ref[t], outb_ref[t]
        gin, gout = gin_ref[t], gout_ref[t]
        new = ([], [])
        rows = pl.ds(pl.multiple_of(t * half, half), half)
        for group in range(groups):
            here = (group, pl.ds(t, 1))
            grady = grady_ref[here]
            delta = ddec_ref[here]
            rates = rates_ref[:, columns[group]]
            adjoint = grady * out_row + later[group]
            gout = gout + grady * kept[t + 1, :, columns[group]]
            gin = gin + adjoint * drive_ref[here]
            first[group, rows, :] = fold(adjoint * in_row)
            passed = jnp.exp2(delta * rates) * adjoint
            pulled = passed * kept[t, :, columns[group]]
            second[group, rows, :] = fold(pulled * rates)
            new[0].append(passed)
            new[1].append(grates[group] + pulled * delta)
        gin_ref[t] = gin
        gout_ref[t] = gout
        return new

    end = [leaving[:, group * LANES : (group + 1) * LANES] for group in range(groups)]
    zeros = [jnp.zeros((N, LANES), jnp.float32) for _ in range(groups)]
    _, grates = lax.fori_loop(0, steps, backward, (end, zeros), unroll=4)
    collapse(first, along_ref)
    collapse(second, decayed_ref)
    for group in range(groups):
        grates_ref[:, columns[group]] = grates[group]


def ends_of(ddec, drive, grady, inb, outb, rates, block):
    steps = ddec.shape[1]
    wide = pl.BlockSpec((block // LANES, steps, LANES), lambda b: (b, 0, 0))
    whole = pl.BlockSpec((steps, N, LANES), lambda b: (0, 0, 0))
    return pl.pallas_call(
        ends_kernel,
        grid=(E // block,),
        in_specs=[wide, wide, wide, whole, whole, pl.BlockSpec((N, block), lambda b: (0, b))],
        out_specs=pl.BlockSpec((2 * N + 8, block), lambda b: (0, b)),
        out_shape=jax.ShapeDtypeStruct((2 * N + 8, E), jnp.float32),
        compiler_params=pltpu.CompilerParams(vmem_limit_bytes=48 * 2**20),
        name="ends",
    )(ddec, drive, grady, inb, outb, rates)


def scan_of(member, ddec, drive, grady, inb, outb, rates, everyone, block):
    steps = ddec.shape[1]
    devices = everyone.shape[0]
    groups = block // LANES
    wide = pl.BlockSpec((block // LANES, steps, LANES), lambda b: (b, 0, 0))
    whole = pl.BlockSpec((steps, N, LANES), lambda b: (0, 0, 0))
    narrow = pl.BlockSpec((N, block), lambda b: (0, b))
    full = jax.ShapeDtypeStruct((E // LANES, steps, LANES), jnp.float32)
    spread = jax.ShapeDtypeStruct((steps, N, LANES), jnp.float32)
    return pl.pallas_call(
        scan_kernel,
        grid=(E // block,),
        in_specs=[
            pl.BlockSpec(memory_space=pltpu.SMEM),
            wide,
            wide,
            wide,
            whole,
            whole,
            narrow,
            pl.BlockSpec((devices, 2 * N + 8, block), lambda b: (0, 0, b)),
        ],
        out_specs=[wide, wide, wide, whole, whole, narrow],
        out_shape=[full, full, full, spread, spread, jax.ShapeDtypeStruct((N, E), jnp.float32)],
        scratch_shapes=[
            pltpu.VMEM((steps + 1, N, block), jnp.float32),
            pltpu.VMEM((groups, steps * N // 2, LANES), jnp.float32),
            pltpu.VMEM((groups, steps * N // 2, LANES), jnp.float32),
        ],
        compiler_params=pltpu.CompilerParams(vmem_limit_bytes=48 * 2**20),
        name="scan",
    )(member, ddec, drive, grady, inb, outb, rates, everyone)


def local(
    tokens,
    cotangent,
    doc_lengths,
    norm_gain,
    in_proj,
    conv_weight,
    conv_bias,
    x_proj,
    dt_proj,
    dt_bias,
    a_log,
    d_skip,
    out_proj,
    moment_norm_gain,
    moment_in_proj,
    moment_conv_weight,
    moment_conv_bias,
    moment_x_proj,
    moment_dt_proj,
    moment_dt_bias,
    moment_a_log,
    moment_d_skip,
    moment_out_proj,
    average_norm_gain,
    average_in_proj,
    average_conv_weight,
    average_conv_bias,
    average_x_proj,
    average_dt_proj,
    average_dt_bias,
    average_a_log,
    average_d_skip,
    average_out_proj,
):
    devices = lax.axis_size("seq")
    member_id = lax.axis_index("seq")
    channels = E // devices
    begin = member_id * channels
    stream = tokens[0].astype(jnp.float32)
    steps = stream.shape[0]
    length = steps * devices
    cot_low = cotangent[0]
    inverse = lax.rsqrt(jnp.mean(stream * stream, axis=1, keepdims=True) + EPS)
    normed = (stream * inverse * norm_gain[None, :]).astype(jnp.bfloat16)
    normed_all = lax.all_gather(normed, "seq", axis=0, tiled=True)
    cot_all = lax.all_gather(cot_low, "seq", axis=0, tiled=True)
    xz = jnp.dot(normed, in_proj, preferred_element_type=jnp.float32).astype(jnp.bfloat16)
    halo = lax.ppermute(
        xz[steps - 8 :, :E], "seq", [(i, i + 1) for i in range(devices - 1)]
    )
    back_gated = lax.dot_general(
        cot_low, out_proj, (((1,), (1,)), ((), ())), preferred_element_type=jnp.float32
    ).astype(jnp.bfloat16)
    positions = member_id * steps + jnp.arange(-8, steps + 8, dtype=jnp.int32)
    docid, starting = doc_tables(doc_lengths[0], positions)
    reset = starting[8 : 8 + steps, None]
    masks = []
    for offset in range(K):
        linked = (docid[8:] == docid[8 - offset : steps + 16 - offset]) & (
            positions[8 - offset : steps + 16 - offset] >= 0
        )
        masks.append((linked & (positions[8:] < length)).astype(jnp.float32)[:, None])
    padded = jnp.concatenate([halo, xz[:, :E]], axis=0).astype(jnp.float32)
    gates = xz[:, E:].astype(jnp.float32)
    pre_act = jnp.broadcast_to(conv_bias[None, :], (steps, E))
    for offset in range(K):
        pre_act = (
            pre_act
            + conv_weight[offset][None, :]
            * padded[8 - offset : 8 - offset + steps]
            * masks[offset][:steps]
        )
    act = silu(pre_act)
    act_low = act.astype(jnp.bfloat16)
    proj = jnp.dot(act_low, x_proj, preferred_element_type=jnp.float32)
    rank_low = proj[:, :R].astype(jnp.bfloat16)
    in_mat = proj[:, R : R + N]
    out_mat = proj[:, R + N :]
    delta_pre = (
        jnp.dot(rank_low, dt_proj, preferred_element_type=jnp.float32) + dt_bias[None, :]
    )
    delta = jax.nn.softplus(delta_pre)
    rates = -jnp.exp(a_log)
    scaled_rates = rates * (1.0 / math.log(2.0))
    ddec = jnp.where(reset, RESET, delta)
    drive = delta * act
    silu_gate = silu(gates)
    chan_back = back_gated.astype(jnp.float32)
    grad_y = chan_back * silu_gate
    inb = jnp.broadcast_to(in_mat[:, :, None], (steps, N, LANES))
    outb = jnp.broadcast_to(out_mat[:, :, None], (steps, N, LANES))
    def grouped(values):
        return jnp.transpose(values.reshape(steps, E // LANES, LANES), (1, 0, 2))

    def flat(values):
        return jnp.transpose(values, (1, 0, 2)).reshape(steps, E)

    ddec, drive, grady_rows = grouped(ddec), grouped(drive), grouped(grad_y)
    ends = ends_of(ddec, drive, grady_rows, inb, outb, scaled_rates, 512)
    everyone = lax.all_gather(ends, "seq", axis=0)
    member_word = jnp.reshape(member_id, (1,)).astype(jnp.int32)
    scanned, along_in, pulled_sum, gin, gout, grad_rates = scan_of(
        member_word, ddec, drive, grady_rows, inb, outb, scaled_rates, everyone, 512
    )
    scanned, along_in, pulled_sum = flat(scanned), flat(along_in), flat(pulled_sum)
    y_full = scanned + d_skip[None, :] * act
    gated = (y_full * silu_gate).astype(jnp.bfloat16)
    block_output = (
        stream + jnp.dot(gated, out_proj, preferred_element_type=jnp.float32)
    )[None]
    gated_mine = lax.all_to_all(gated, "seq", split_axis=1, concat_axis=0, tiled=True)
    grad_out_proj = lax.dot_general(
        gated_mine, cot_all, (((0,), (0,)), ((), ())), preferred_element_type=jnp.float32
    )
    grad_gates = chan_back * y_full * silu_slope(gates)
    grad_dskip = jnp.sum(grad_y * act, axis=0)
    grad_in_mat = jnp.sum(gin, axis=2)
    grad_out_mat = jnp.sum(gout, axis=2)
    grad_delta = along_in * act + pulled_sum * math.log(2.0)
    grad_alog = grad_rates * rates
    grad_pre = (grad_delta * jax.nn.sigmoid(delta_pre)).astype(jnp.bfloat16)
    grad_dtbias = jnp.sum(grad_pre.astype(jnp.float32), axis=0)
    grad_dtproj = lax.dot_general(
        rank_low, grad_pre, (((0,), (0,)), ((), ())), preferred_element_type=jnp.float32
    )
    rank_back = lax.dot_general(
        grad_pre, dt_proj, (((1,), (1,)), ((), ())), preferred_element_type=jnp.float32
    )
    proj_back = jnp.concatenate([rank_back, grad_in_mat, grad_out_mat], axis=1).astype(jnp.bfloat16)
    grad_xproj = lax.dot_general(
        act_low, proj_back, (((0,), (0,)), ((), ())), preferred_element_type=jnp.float32
    )
    grad_act = (
        grad_y * d_skip[None, :]
        + along_in * delta
        + lax.dot_general(
            proj_back, x_proj, (((1,), (1,)), ((), ())), preferred_element_type=jnp.float32
        )
    )
    grad_pre_act = grad_act * silu_slope(pre_act)
    ahead = lax.ppermute(
        grad_pre_act[:8], "seq", [(i + 1, i) for i in range(devices - 1)]
    )
    extended = jnp.concatenate([grad_pre_act, ahead], axis=0)
    grad_conv_bias = jnp.sum(grad_pre_act, axis=0)
    grad_inner = jnp.zeros_like(gates)
    conv_rows = []
    for offset in range(K):
        masked = extended * masks[offset]
        conv_rows.append(
            jnp.sum(masked[:steps] * padded[8 - offset : 8 - offset + steps], axis=0)
        )
        grad_inner = grad_inner + conv_weight[offset][None, :] * masked[offset : offset + steps]
    grad_convw = jnp.stack(conv_rows)
    back_xz = jnp.stack([grad_inner, grad_gates]).astype(jnp.bfloat16)
    back_mine = lax.all_to_all(back_xz, "seq", split_axis=2, concat_axis=1, tiled=True)
    grad_normed = lax.dot_general(
        back_xz[0], in_proj[:, :E], (((1,), (1,)), ((), ())), preferred_element_type=jnp.float32
    ) + lax.dot_general(
        back_xz[1], in_proj[:, E:], (((1,), (1,)), ((), ())), preferred_element_type=jnp.float32
    )
    grad_in_proj = jnp.einsum(
        "td,ktc->dkc", normed_all, back_mine, preferred_element_type=jnp.float32
    )
    grad_gain = jnp.sum(grad_normed * stream * inverse, axis=0)
    scaled = grad_normed * norm_gain[None, :]
    input_grad = (
        cot_low.astype(jnp.float32)
        + inverse * scaled
        - stream * inverse * inverse * inverse * jnp.mean(scaled * stream, axis=1, keepdims=True)
    )
    summed = lax.psum((grad_in_proj, grad_out_proj), "rows")
    in_share = lax.all_to_all(summed[0], "seq", split_axis=0, concat_axis=2, tiled=True)
    small = jnp.concatenate(
        [
            grad_xproj.T,
            grad_dtproj,
            grad_alog,
            grad_convw,
            grad_conv_bias[None],
            grad_dtbias[None],
            grad_dskip[None],
            jnp.pad(
                grad_gain.reshape(devices, D // devices),
                ((0, 0), (0, channels - D // devices)),
            ).reshape(1, E),
        ],
        axis=0,
    )
    small = lax.psum(small, "rows")
    small = lax.psum_scatter(small, "seq", scatter_dimension=1, tiled=True)
    parts = []
    at = 0
    for count in (R + 2 * N, R, N, K, 1, 1, 1, 1):
        parts.append(small[at : at + count])
        at += count
    owner_grads = (
        parts[7][0, : D // devices],
        in_share.reshape(D // devices, 2 * E),
        parts[3],
        parts[4][0],
        parts[0].T,
        parts[1],
        parts[5][0],
        parts[2],
        parts[6][0],
        summed[1],
    )
    conv_mine = lax.dynamic_slice_in_dim(conv_weight, begin, channels, 1)
    cbias_mine = lax.dynamic_slice_in_dim(conv_bias, begin, channels, 0)
    xproj_mine = lax.dynamic_slice_in_dim(x_proj, begin, channels, 0)
    dtproj_mine = lax.dynamic_slice_in_dim(dt_proj, begin, channels, 1)
    dtbias_mine = lax.dynamic_slice_in_dim(dt_bias, begin, channels, 0)
    alog_mine = lax.dynamic_slice_in_dim(a_log, begin, channels, 1)
    dskip_mine = lax.dynamic_slice_in_dim(d_skip, begin, channels, 0)
    squares = jnp.float32(0.0)
    for member in owner_grads:
        squares = squares + jnp.sum(member * member)
    squares_all = lax.psum(squares, "seq")
    grad_norm = jnp.sqrt(squares_all)
    shrink_by = 1.0 / jnp.maximum(grad_norm, 1.0)
    gain_rows = D // devices
    outer_rows = E // devices
    mine_weights = (
        lax.dynamic_slice_in_dim(norm_gain, member_id * gain_rows, gain_rows, 0),
        lax.dynamic_slice_in_dim(in_proj, member_id * gain_rows, gain_rows, 0).astype(jnp.float32),
        conv_mine,
        cbias_mine,
        xproj_mine.astype(jnp.float32),
        dtproj_mine.astype(jnp.float32),
        dtbias_mine,
        alog_mine,
        dskip_mine,
        lax.dynamic_slice_in_dim(out_proj, member_id * outer_rows, outer_rows, 0).astype(
            jnp.float32
        ),
    )
    moments = (
        moment_norm_gain,
        moment_in_proj,
        moment_conv_weight,
        moment_conv_bias,
        moment_x_proj,
        moment_dt_proj,
        moment_dt_bias,
        moment_a_log,
        moment_d_skip,
        moment_out_proj,
    )
    averages = (
        average_norm_gain,
        average_in_proj,
        average_conv_weight,
        average_conv_bias,
        average_x_proj,
        average_dt_proj,
        average_dt_bias,
        average_a_log,
        average_d_skip,
        average_out_proj,
    )
    results = [block_output, input_grad[None], grad_norm]
    for ordinal in range(10):
        clipped = owner_grads[ordinal] * shrink_by
        momentum_new = MOMENTUM * moments[ordinal] + clipped
        renewed = mine_weights[ordinal] - RATES[ordinal] * math.sqrt(PARAMS) * (
            clipped + MOMENTUM * momentum_new
        )
        results += [momentum_new, renewed, AVERAGE * averages[ordinal] + (1.0 - AVERAGE) * renewed]
    return tuple(results)


def solution(mesh):
    return jax.shard_map(
        local,
        mesh=mesh,
        in_specs=(
            P("rows", "seq", None),
            P("rows", "seq", None),
            P("rows", None),
            P(),
            P(),
            P(),
            P(),
            P(),
            P(),
            P(),
            P(),
            P(),
            P(),
            P("seq"),
            P("seq", None),
            P(None, "seq"),
            P("seq"),
            P("seq", None),
            P(None, "seq"),
            P("seq"),
            P(None, "seq"),
            P("seq"),
            P("seq", None),
            P("seq"),
            P("seq", None),
            P(None, "seq"),
            P("seq"),
            P("seq", None),
            P(None, "seq"),
            P("seq"),
            P(None, "seq"),
            P("seq"),
            P("seq", None),
        ),
        out_specs=(
            P("rows", "seq", None),
            P("rows", "seq", None),
            P(),
            P("seq"),
            P("seq"),
            P("seq"),
            P("seq", None),
            P("seq", None),
            P("seq", None),
            P(None, "seq"),
            P(None, "seq"),
            P(None, "seq"),
            P("seq"),
            P("seq"),
            P("seq"),
            P("seq", None),
            P("seq", None),
            P("seq", None),
            P(None, "seq"),
            P(None, "seq"),
            P(None, "seq"),
            P("seq"),
            P("seq"),
            P("seq"),
            P(None, "seq"),
            P(None, "seq"),
            P(None, "seq"),
            P("seq"),
            P("seq"),
            P("seq"),
            P("seq", None),
            P("seq", None),
            P("seq", None),
        ),
        check_vma=False,
    )
```

profile of v0, /device:TPU:0, one launch (start us, length us, event | category | flops | bytes accessed | tf_op | source)
XLA Modules:
  0.0 408.2 jit_solution(17956215286865347650)
XLA Ops:
  8.4 1.1 fusion.36
  9.5 4.8 %convolution_convert_fusion = bf16[128,4096]{1,0:T(8,128)(2,1)S(1)} fusion(bf16[128,1024]{1,0:T(8,128)(2,1)S(1)} %fusion.36, bf16[1024,4096]{1,0:T(8,128)(2,1)} %param.37), kind=kOutput, calls=%fused_computation | convolution fusion | flops 1074266112 | bytes 9699328 | tf_op jit(solution)/shard_map/dot_general | solution.py:269
  14.3 2.5 collective-permute-start
  17.8 6.7 %multiply_reduce_fusion.2 = (f32[2048]{0:T(1024)}, f32[128,2048]{1,0:T(8,128)}, f32[128,2048]{1,0:T(8,128)S(1)}, f32[128,2048]{1,0:T(8,128)}) fusion(bf16[128,4096]{1,0:T(8,128)(2,1)S(1)} %convolution_convert_fusion, f32[128]{0:T(128)S(1)} %slice.183, f32[136,2048]{1,0:T(8,128)S(1)} %maximum_convert_fusion, f32[2048]{0:T(1024)S(1)} %bitcast.157, ...), kind=kOutput, calls=%fused_computation.61 | convolution fusion | flops 543684608 | bytes 12371968 | tf_op jit(solution)/shard_map/dot_general | solution.py:273
  25.8 2.3 fusion.55
  28.8 1.9 copy.115
  31.1 2.9 copy.117
  34.0 1.6 copy.118
  37.1 7.3 %ends.1 = f32[40,2048]{1,0:T(8,128)} custom-call(f32[16,128,128]{2,1,0:T(8,128)S(1)} %bitcast.117, f32[16,128,128]{2,1,0:T(8,128)S(1)} %bitcast.119, f32[16,128,128]{2,1,0:T(8,128)S(1)} %bitcast.121, f32[128,16,128]{2,1,0:T(8,128)S(1)} %broadcast_in_dim.31.inb_ref, f32[128,16,128]{2,1,0:T(8,128)S(1)} %broadcast_in_dim.32.outb_ref, ...), custom_call_target="tpu_custom_call" | custom-call | tf_op jit(solution)/shard_map/ends/pallas_call | solution.py:177
  46.9 37.3 %all-gather.8.cloned.1.call-done = f32[320,2048]{1,0:T(8,128)} async-done(((f32[40,2048]{1,0:T(8,128)}), f32[320,2048]{1,0:T(8,128)}) %all-gather.8.cloned.1.call-update) | async-done | bytes 2621456 | tf_op jit(solution)/shard_map/all_gather | solution.py:322
  84.1 21.1 %scan.1 = (f32[16,128,128]{2,1,0:T(8,128)S(1)}, f32[16,128,128]{2,1,0:T(8,128)S(1)}, f32[16,128,128]{2,1,0:T(8,128)S(1)}, f32[128,16,128]{2,1,0:T(8,128)S(1)}, f...) custom-call(s32[1]{0:T(128)} %bitcast.1.member_ref, f32[16,128,128]{2,1,0:T(8,128)} %bitcast.118, ...), custom_call_target="tpu_custom_call" | custom-call | tf_op jit(solution)/shard_map/scan/pallas_call | solution.py:197
  107.3 2.5 copy.126
  109.8 2.5 copy.127
  112.3 2.5 copy.123
  114.9 2.6 copy.124
  117.4 1.3 copy.121
  118.7 2.6 copy.122
  122.3 4.4 %convert_reduce_fusion = (f32[2048]{0:T(1024)S(1)}, bf16[128,2048]{1,0:T(8,128)(2,1)S(1)}, bf16[128,2048]{1,0:T(8,128)(2,1)S(1)}, bf16[128,2048]{1,0:T(8,128)(2,1)S(1)}) fusion(f32[128,2048]{1,0:T(8,128)} %get-tuple-element.119, f32[128,2048]{1,0:T(8,128)} %copy.127, f32[128,2048]{1,0:T(8,128)} %copy.124, f32[128,2048]{1,0:T(8,128)} %copy-done.22, ...), kind=kLoop, calls=%fused_computation.62 | loop fusion | flops 7600128 | bytes 8404992 | tf_op jit(solution)/shard_map/reduce_sum | solution.py:344
  127.0 1.1 fusion.4
  128.2 1.4 collective-permute-start.1
  129.6 1.4 fusion.47
  131.0 2.3 fusion
  135.2 4.8 %all-to-all-start.2 = ((bf16[128,8,256]{2,0,1:T(8,128)(2,1)}), bf16[128,8,256]{2,0,1:T(8,128)(2,1)S(1)}, u32[]{:S(2)}, u32[]{:S(2)}) async-start(bf16[128,8,256]{2,0,1:T(8,128)(2,1)} %bitcast.142), calls=%async_computation.2 | async-start | bytes 1048576 | tf_op jit(solution)/shard_map/all_to_all | solution.py:333
  142.1 4.7 %fusion.44 = (f32[1024]{0:T(1024)S(1)}, f32[128]{0:T(128)S(1)}, f32[128,1024]{1,0:T(8,128)}) fusion(bf16[1,128,1024]{2,1,0:T(8,128)(2,1)S(1)} %copy-done.12, f32[128]{0:T(128)S(1)} %copy-done.58, f32[1024]{0:T(1024)S(1)} %copy-done.41, f32[128,1024]{1,0:T(8,128)S(1)} %copy-done.73, bf16[128,2048]{1,0:T(8,128)(2,1)S(1)} %fusion.27, bf16[1024,4096]{1,0:T(8,128)(2,1)} %param.37), kind=kOutput, calls=%fused_computation.85 | convolution fusion | flops 537918336 | bytes 6038528 | tf_op jit(solution)/shard_map/dot_general | solution.py:379
  147.5 6.0 %concatenate.16 = f32[184,2048]{1,0:T(8,128)} concatenate(f32[96,2048]{1,0:T(8,128)} %fusion.47, f32[64,2048]{1,0:T(8,128)} %fusion.56, f32[16,2048]{1,0:T(8,128)S(1)} %fusion.51, f32[1,2048]{1,0:T(1,128)S(1)} %bitcast.148, f32[1,2048]{1,0:T(1,128)S(1)} %bitcast.147, f32[1,2048]{1,0:T(1,128)S(1)} %bitcast.146, f32[1,2048]{1,0:T(1,128)S(1)} %bitcast.145, f32[1,2048]{1,0:T(1,128)S(1)} %bitcast.149, ...), dimensions={0} | concatenate | bytes 3014656 | tf_op jit(solution)/shard_map/concatenate | solution.py:396
  153.5 1.1 pad_maximum_fusion.1
  154.7 2.0 copy.130
  156.7 5.1 %all-to-all-start = ((bf16[2,128,2048]{1,0,2:T(2,128)(2,1)}), bf16[2,128,2048]{1,0,2:T(2,128)(2,1)S(1)}, u32[]{:S(2)}, u32[]{:S(2)}) async-start(bf16[2,128,2048]{1,0,2:T(2,128)(2,1)} %copy.130), calls=%async_computation | async-start | bytes 2097152 | tf_op jit(solution)/shard_map/all_to_all | solution.py:378
  162.0 3.3 fusion.6
  165.3 34.8 %all-to-all-done = bf16[2,128,2048]{1,0,2:T(2,128)(2,1)S(1)} async-done(((bf16[2,128,2048]{1,0,2:T(2,128)(2,1)}), bf16[2,128,2048]{1,0,2:T(2,128)(2,1)S(1)}, u32[]{:S(2)}, u32[]{:S(2)}) %all-to-all-start) | async-done | bytes 1048608 | tf_op jit(solution)/shard_map/all_to_all | solution.py:378
  200.9 4.2 %fusion.8 = f32[1024,2,256]{2,0,1:T(8,128)} fusion(bf16[2,1024,256]{2,1,0:T(8,128)(2,1)S(1)} %bitcast.144, bf16[1024,1024]{1,0:T(8,128)(2,1)} %all-gather.6.cloned.1.call-done), kind=kOutput, calls=%fused_computation.13 | convolution fusion | flops 1073741824 | bytes 5242880 | tf_op jit(solution)/shard_map/td,ktc->dkc/dot_general | solution.py:384
  205.2 90.7 %all-reduce.4.cloned.1.call-done = (f32[184,256]{1,0:T(8,128)}, f32[1024,2,256]{2,0,1:T(8,128)}, f32[256,1024]{1,0:T(8,128)}) async-done(((f32[184,256]{1,0:T(8,128)}, f32[1024,2,256]{2,0,1:T(8,128)}, f32[256,1024]{1,0:T(8,128)}), (f32[184,256]{1,0:T(8,128)}, f32[1024,2,256]{2,0,1:T(8,128)}, f32[256,1024]{1,0:T(8,128)})) %all-reduce.4.cloned.1.call-update) | async-done | bytes 3334160 | tf_op jit(solution)/shard_map/psum | solution.py:412
  295.9 4.5 %copy.133 = f32[1024,2,256]{2,1,0:T(2,128)} copy(f32[1024,2,256]{2,0,1:T(8,128)} %get-tuple-element.58) | data formatting | bytes 4194304 | tf_op jit(solution)/shard_map/psum | solution.py:394
  300.4 4.6 %all-to-all-start.1 = ((f32[1024,2,256]{2,1,0:T(2,128)}), f32[1024,2,256]{2,1,0:T(2,128)S(1)}, u32[]{:S(2)}, u32[]{:S(2)}) async-start(f32[1024,2,256]{2,1,0:T(2,128)} %copy.133), calls=%async_computation.1 | async-start | bytes 4194304 | tf_op jit(solution)/shard_map/all_to_all | solution.py:395
  305.0 3.8 fusion.10
  313.4 40.7 %all-to-all-done.1 = f32[1024,2,256]{2,1,0:T(2,128)S(1)} async-done(((f32[1024,2,256]{2,1,0:T(2,128)}), f32[1024,2,256]{2,1,0:T(2,128)S(1)}, u32[]{:S(2)}, u32[]{:S(2)}) %all-to-all-start.1) | async-done | bytes 2097184 | tf_op jit(solution)/shard_map/all_to_all | solution.py:395
  354.1 2.8 multiply_reduce_fusion
  363.3 2.1 fusion.40
  365.4 15.0 %psum.31 = f32[]{:T(128)} all-reduce(f32[]{:T(128)S(6)} %add.281), channel_id=1, replica_groups=mesh['rows'=4,'seq'=8] {'seq'}, use_global_device_ids=true, to_apply=%region_29.30 | all-reduce | flops 1 | bytes 8 | tf_op jit(solution)/shard_map/psum | solution.py:441
  381.3 1.2 copy.135
  382.7 1.7 copy.140
  384.4 1.3 multiply_add_fusion.11
  385.7 1.5 multiply_add_fusion.6
  387.2 1.5 multiply_add_fusion.7
  389.3 3.2 multiply_add_fusion.2
  393.2 4.6 %multiply_add_fusion = (f32[128,4096]{1,0:T(8,128)}, f32[128,4096]{1,0:T(8,128)}, f32[128,4096]{1,0:T(8,128)}) fusion(f32[128,4096]{1,0:T(8,128)S(1)} %copy-done.15, f32[128,4096]{1,0:T(8,128)S(1)} %bitcast.130, bf16[1024,4096]{1,0:T(8,128)(2,1)} %param.37, s32[]{:T(128)S(6)} %select_n.24, f32[128,4096]{1,0:T(8,128)S(1)} %copy-done.16), kind=kLoop, calls=%fused_computation.15 | loop fusion | flops 5242880 | bytes 13631492 | tf_op jit(solution)/shard_map/add | solution.py:491
  397.8 1.3 multiply_add_fusion.17
  399.2 1.4 multiply_add_fusion.13
  (225 shorter events, 23.3 us)
Async XLA Ops:
  7.2 76.9 %all-gather.8.cloned.1.call-start = ((), (), s32[]{:S(2)}) async-start(), calls=%async_computation.5 | async-start | bytes 2949120 | tf_op jit(solution)/shard_map/all_gather | solution.py:322
  9.4 4.8 %copy-start.13 = (bf16[128,1024]{1,0:T(8,128)(2,1)}, bf16[128,1024]{1,0:T(8,128)(2,1)S(1)}, u32[]{:S(2)}) copy-start(bf16[128,1024]{1,0:T(8,128)(2,1)S(1)} %fusion.36) | copy-start | bytes 786436
  9.5 7.5 %copy-start.72 = (s32[1,8]{1,0:T(1,128)S(1)}, s32[1,8]{1,0:T(1,128)}, u32[]{:S(2)}) copy-start(s32[1,8]{1,0:T(1,128)} %param.35) | copy-start | bytes 100
  9.5 7.7 %copy-start.36 = (f32[4,2048]{1,0:T(4,128)S(1)}, f32[4,2048]{1,0:T(4,128)}, u32[]{:S(2)}) copy-start(f32[4,2048]{1,0:T(4,128)} %param.38) | copy-start | bytes 98308
  9.5 7.8 %copy-start.26 = (f32[16,2048]{1,0:T(8,128)S(1)}, f32[16,2048]{1,0:T(8,128)}, u32[]{:S(2)}) copy-start(f32[16,2048]{1,0:T(8,128)} %param.43) | copy-start | bytes 393220
  14.3 10.3 %copy-start.8 = (bf16[128,4096]{1,0:T(8,128)(2,1)}, bf16[128,4096]{1,0:T(8,128)(2,1)S(1)}, u32[]{:S(2)}) copy-start(bf16[128,4096]{1,0:T(8,128)(2,1)S(1)} %convolution_convert_fusion) | copy-start | bytes 3145732
  14.3 3.3 collective-permute-start
  17.3 7.3 %copy-start.37 = (f32[1,2048]{1,0:T(1,128)}, f32[1,2048]{1,0:T(1,128)S(1)}, u32[]{:S(2)}) copy-start(f32[1,2048]{1,0:T(1,128)S(1)} %get-tuple-element.113) | copy-start | bytes 24580
  17.3 7.3 %copy-start.39 = (f32[1,2048]{1,0:T(1,128)}, f32[1,2048]{1,0:T(1,128)S(1)}, u32[]{:S(2)}) copy-start(f32[1,2048]{1,0:T(1,128)S(1)} %get-tuple-element.114) | copy-start | bytes 24580
  17.4 7.2 %copy-start.49 = (f32[136]{0:T(256)}, f32[136]{0:T(256)S(1)}, u32[]{:S(2)}) copy-start(f32[136]{0:T(256)S(1)} %get-tuple-element.115) | copy-start | bytes 1636
  17.4 7.2 %copy-start.51 = (f32[136]{0:T(256)}, f32[136]{0:T(256)S(1)}, u32[]{:S(2)}) copy-start(f32[136]{0:T(256)S(1)} %get-tuple-element.116) | copy-start | bytes 1636
  17.4 7.1 %copy-start.53 = (f32[136]{0:T(256)}, f32[136]{0:T(256)S(1)}, u32[]{:S(2)}) copy-start(f32[136]{0:T(256)S(1)} %get-tuple-element.117) | copy-start | bytes 1636
  17.5 7.0 %copy-start.60 = (f32[128]{0:T(128)}, f32[128]{0:T(128)S(1)}, u32[]{:S(2)}) copy-start(f32[128]{0:T(128)S(1)} %slice.167) | copy-start | bytes 1540
  17.8 6.8 %copy-start.6 = (f32[136,2048]{1,0:T(8,128)}, f32[136,2048]{1,0:T(8,128)S(1)}, u32[]{:S(2)}) copy-start(f32[136,2048]{1,0:T(8,128)S(1)} %maximum_convert_fusion) | copy-start | bytes 3342340
  17.8 6.8 %copy-start.47 = (bf16[2048,96]{0,1:T(8,128)(2,1)S(1)}, bf16[2048,96]{0,1:T(8,128)(2,1)}, u32[]{:S(2)}) copy-start(bf16[2048,96]{0,1:T(8,128)(2,1)} %param.40) | copy-start | bytes 1179652
  28.8 7.7 %copy-start = (f32[128,16,128]{2,0,1:T(8,128)}, f32[128,16,128]{2,0,1:T(8,128)S(1)}, u32[]{:S(2)}) copy-start(f32[128,16,128]{2,0,1:T(8,128)S(1)} %copy.114) | copy-start | bytes 3145732
  31.0 5.4 %copy-start.1 = (f32[128,16,128]{2,0,1:T(8,128)}, f32[128,16,128]{2,0,1:T(8,128)S(1)}, u32[]{:S(2)}) copy-start(f32[128,16,128]{2,0,1:T(8,128)S(1)} %copy.116) | copy-start | bytes 3145732
  35.6 8.8 %copy-start.2 = (f32[128,16,128]{2,0,1:T(8,128)}, f32[128,16,128]{2,0,1:T(8,128)S(1)}, u32[]{:S(2)}) copy-start(f32[128,16,128]{2,0,1:T(8,128)S(1)} %copy.118) | copy-start | bytes 3145732
  45.4 116.6 %all-gather.10.cloned.1.call-start = ((), (), s32[]{:S(2)}) async-start(), calls=%async_computation.6 | async-start | bytes 2359296 | tf_op jit(solution)/shard_map/all_gather | solution.py:268
  46.1 154.8 %all-gather.6.cloned.1.call-start = ((), (), s32[]{:S(2)}) async-start(), calls=%async_computation.4 | async-start | bytes 2359296 | tf_op jit(solution)/shard_map/all_gather | solution.py:267
  121.7 4.9 %copy-start.29 = (bf16[64,2048]{1,0:T(8,128)(2,1)S(1)}, bf16[64,2048]{1,0:T(8,128)(2,1)}, u32[]{:S(2)}) copy-start(bf16[64,2048]{1,0:T(8,128)(2,1)} %param.41) | copy-start | bytes 786436
  122.2 4.8 %copy-start.11 = (f32[128,2048]{1,0:T(8,128)S(1)}, f32[128,2048]{1,0:T(8,128)}, u32[]{:S(2)}) copy-start(f32[128,2048]{1,0:T(8,128)} %copy.124) | copy-start | bytes 3145732
  122.2 4.8 %copy-start.17 = (f32[128,2048]{1,0:T(8,128)S(1)}, f32[128,2048]{1,0:T(8,128)}, u32[]{:S(2)}) copy-start(f32[128,2048]{1,0:T(8,128)} %get-tuple-element.91) | copy-start | bytes 3145732
  122.2 4.8 %copy-start.23 = (f32[128,2048]{1,0:T(8,128)S(1)}, f32[128,2048]{1,0:T(8,128)}, u32[]{:S(2)}) copy-start(f32[128,2048]{1,0:T(8,128)} %copy-done.22) | copy-start | bytes 3145732
  122.2 4.8 %copy-start.24 = (f32[128,2048]{1,0:T(8,128)S(1)}, f32[128,2048]{1,0:T(8,128)}, u32[]{:S(2)}) copy-start(f32[128,2048]{1,0:T(8,128)} %get-tuple-element.119) | copy-start | bytes 3145732
  122.3 8.7 %slice-start = ((s8[8388608]{0:T(1024)(128)(4,1)}), s8[4194304]{0:T(1024)(128)(4,1)S(1)}, s32[]{:S(2)}) async-start(s8[8388608]{0:T(1024)(128)(4,1)} %bitcast.125), calls=%async_computation.9 | async-start | bytes 8388608
  128.2 11.9 %collective-permute-start.1 = (f32[8,2048]{1,0:T(8,128)S(1)}, f32[8,2048]{1,0:T(8,128)S(1)}, u32[]{:S(2)}, u32[]{:S(2)}) collective-permute-start(f32[8,2048]{1,0:T(8,128)S(1)} %slice.216), channel_id=1, source_target_pairs={{1,0},{2,1},{3,2},{4,3},{5,4},{6,5},{7,6},{9,8},{10,9},{11,10},{12... | collective-permute-start | bytes 196616 | tf_op jit(solution)/shard_map/ppermute | solution.py:363
  133.3 6.7 %copy-start.50 = (f32[136]{0:T(256)S(1)}, f32[136]{0:T(256)}, u32[]{:S(2)}) copy-start(f32[136]{0:T(256)} %copy-done.49) | copy-start | bytes 1636
  133.3 6.8 %copy-start.52 = (f32[136]{0:T(256)S(1)}, f32[136]{0:T(256)}, u32[]{:S(2)}) copy-start(f32[136]{0:T(256)} %copy-done.51) | copy-start | bytes 1636
  133.3 6.8 %copy-start.54 = (f32[136]{0:T(256)S(1)}, f32[136]{0:T(256)}, u32[]{:S(2)}) copy-start(f32[136]{0:T(256)} %copy-done.53) | copy-start | bytes 1636
  135.2 21.5 %all-to-all-start.2 = ((bf16[128,8,256]{2,0,1:T(8,128)(2,1)}), bf16[128,8,256]{2,0,1:T(8,128)(2,1)S(1)}, u32[]{:S(2)}, u32[]{:S(2)}) async-start(bf16[128,8,256]{2,0,1:T(8,128)(2,1)} %bitcast.142), calls=%async_computation.2 | async-start | bytes 1048576 | tf_op jit(solution)/shard_map/all_to_all | solution.py:333
  140.0 65.2 %reduce-scatter.2.cloned.1.call-start = ((), (), s32[]{:S(2)}) async-start(), calls=%async_computation.7 | async-start | bytes 1695744 | tf_op jit(solution)/shard_map/reduce_scatter | solution.py:413
  156.7 43.5 %all-to-all-start = ((bf16[2,128,2048]{1,0,2:T(2,128)(2,1)}), bf16[2,128,2048]{1,0,2:T(2,128)(2,1)S(1)}, u32[]{:S(2)}, u32[]{:S(2)}) async-start(bf16[2,128,2048]{1,0,2:T(2,128)(2,1)} %copy.130), calls=%async_computation | async-start | bytes 2097152 | tf_op jit(solution)/shard_map/all_to_all | solution.py:378
  161.7 134.1 %all-reduce.4.cloned.1.call-start = ((), (), s32[]{:S(2)}) async-start(), calls=%async_computation.8 | async-start | bytes 6668288 | tf_op jit(solution)/shard_map/psum | solution.py:412
  300.4 53.7 %all-to-all-start.1 = ((f32[1024,2,256]{2,1,0:T(2,128)}), f32[1024,2,256]{2,1,0:T(2,128)S(1)}, u32[]{:S(2)}, u32[]{:S(2)}) async-start(f32[1024,2,256]{2,1,0:T(2,128)} %copy.133), calls=%async_computation.1 | async-start | bytes 4194304 | tf_op jit(solution)/shard_map/all_to_all | solution.py:395
  305.0 7.5 %copy-start.9 = (f32[256,1024]{1,0:T(8,128)S(1)}, f32[256,1024]{1,0:T(8,128)}, u32[]{:S(2)}) copy-start(f32[256,1024]{1,0:T(8,128)} %get-tuple-element.59) | copy-start | bytes 3145732
  308.8 54.5 %copy-start.19 = (bf16[1,128,1024]{2,1,0:T(8,128)(2,1)S(1)}, bf16[1,128,1024]{2,1,0:T(8,128)(2,1)}, u32[]{:S(2)}) copy-start(bf16[1,128,1024]{2,1,0:T(8,128)(2,1)} %param.34) | copy-start | bytes 786436
  308.8 54.5 %copy-start.42 = (f32[1024]{0:T(1024)S(1)}, f32[1024]{0:T(1024)}, u32[]{:S(2)}) copy-start(f32[1024]{0:T(1024)} %param.36) | copy-start | bytes 12292
  308.8 54.5 %copy-start.59 = (f32[128]{0:T(128)S(1)}, f32[128]{0:T(128)}, u32[]{:S(2)}) copy-start(f32[128]{0:T(128)} %copy-done.57) | copy-start | bytes 1540
  382.6 6.1 %copy-start.43 = (f32[16,256]{1,0:T(8,128)S(1)}, f32[16,256]{1,0:T(8,128)}, u32[]{:S(2)}) copy-start(f32[16,256]{1,0:T(8,128)} %param.63) | copy-start | bytes 49156
  382.6 6.0 %copy-start.44 = (f32[16,256]{1,0:T(8,128)S(1)}, f32[16,256]{1,0:T(8,128)}, u32[]{:S(2)}) copy-start(f32[16,256]{1,0:T(8,128)} %param.53) | copy-start | bytes 49156
  382.6 6.7 %copy-start.10 = (f32[256,1024]{1,0:T(8,128)S(1)}, f32[256,1024]{1,0:T(8,128)}, u32[]{:S(2)}) copy-start(f32[256,1024]{1,0:T(8,128)} %get-tuple-element.59) | copy-start | bytes 3145732
  382.6 6.7 %copy-start.20 = (f32[256,1024]{1,0:T(8,128)S(1)}, f32[256,1024]{1,0:T(8,128)}, u32[]{:S(2)}) copy-start(f32[256,1024]{1,0:T(8,128)} %param.65) | copy-start | bytes 3145732
  382.6 6.6 %copy-start.21 = (f32[256,1024]{1,0:T(8,128)S(1)}, f32[256,1024]{1,0:T(8,128)}, u32[]{:S(2)}) copy-start(f32[256,1024]{1,0:T(8,128)} %param.55) | copy-start | bytes 3145732
  393.2 6.0 %copy-start.64 = (f32[256]{0:T(256)S(1)}, f32[256]{0:T(256)}, u32[]{:S(2)}) copy-start(f32[256]{0:T(256)} %param.64) | copy-start | bytes 3076
  393.2 6.0 %copy-start.65 = (f32[256]{0:T(256)S(1)}, f32[256]{0:T(256)}, u32[]{:S(2)}) copy-start(f32[256]{0:T(256)} %param.54) | copy-start | bytes 3076
  393.2 6.0 %copy-start.66 = (f32[256]{0:T(256)S(1)}, f32[256]{0:T(256)}, u32[]{:S(2)}) copy-start(f32[256]{0:T(256)} %param.52) | copy-start | bytes 3076
  393.2 6.0 %copy-start.67 = (f32[256]{0:T(256)S(1)}, f32[256]{0:T(256)}, u32[]{:S(2)}) copy-start(f32[256]{0:T(256)} %param.62) | copy-start | bytes 3076
  (38 other events, 94.6 us)
Sparse Core Ops, SparseCore 0:
  45.5 38.5 all-gather.7
  85.7 28.0 all-gather.9
  115.5 29.2 all-gather.5
  153.6 42.7 reduce-scatter.1
  205.3 90.5 all-reduce.3
where the time goes:
time: 410 us; the launch traced here: 408 us
  waiting for transfers between devices  205 us (50%)
  local copies, waits for them, and re-layouts  44.3 us (11%)
  other arithmetic  37.3 us (9%)
  matrix products  36.3 us (9%)
  Pallas kernels  28.3 us (7%)
  between operations  23.3 us (6%)
  starting transfers between devices  18.9 us (5%)
  blocking collectives  15 us (4%)
    psum x1, waiting for transfers between devices, local(): small = lax.psum(small, 'rows')  90.7 us
    all_to_all x1, waiting for transfers between devices, local(): lax.all_to_all(summed[0], 'seq', split_axis=0, concat_axis=2, tiled=True)  40.7 us
    all_gather x1, waiting for transfers between devices, local(): everyone = lax.all_gather(ends, 'seq', axis=0)  37.3 us
    all_to_all x1, waiting for transfers between devices, local(): lax.all_to_all(back_xz, 'seq', split_axis=2, concat_axis=1, tiled=True)  34.8 us
    pallas_call x1, Pallas kernels, scan_of(): pl.pallas_call(scan_kernel, grid=(E // block,), in_specs=[pl.BlockSpec(me...  21.1 us
    add x9, other arithmetic, local(): AVERAGE * averages[ordinal] + (1.0 - AVERAGE) * renewed  16 us
    psum x1, blocking collectives, local(): squares_all = lax.psum(squares, 'seq')  15 us
  transfers between devices with their start and end apart: 10, of which 5 were waited for; matrix products, arithmetic and copies ran while one was open for 15% of the time, Pallas kernels for 5%

commit v1 on v0

--- a/solution.py
+++ b/solution.py
@@ -1,3 +1,4 @@
+import functools
 import math
 
 import jax
@@ -16,6 +17,7 @@
 
 LANES = 128
 RESET = 1e30
+MESH = pl.DeviceIdType.MESH
 
 
 EPS = 1e-05
@@ -41,7 +43,7 @@
     return (docid, first > 0)
 
 
-def ends_kernel(ddec_ref, drive_ref, grady_ref, inb_ref, outb_ref, rates_ref, ends_ref):
+def ends_kernel(ddec_ref, drive_ref, grady_ref, inb_ref, outb_ref, rates_ref, ends_ref, sums_ref):
     groups, steps = ddec_ref.shape[:2]
     columns = [pl.ds(group * LANES, LANES) for group in range(groups)]
 
@@ -62,10 +64,11 @@
     ones = [jnp.ones((N, LANES), jnp.float32) for _ in range(groups)]
     hidden, _, pulled = lax.fori_loop(0, steps, step, (zeros, ones, zeros), unroll=4)
     for group in range(groups):
-        ends_ref[:N, columns[group]] = hidden[group]
-        ends_ref[N : 2 * N, columns[group]] = pulled[group]
-        total = jnp.sum(ddec_ref[group], axis=0, keepdims=True)
-        ends_ref[2 * N :, columns[group]] = jnp.broadcast_to(total, (8, LANES))
+        ends_ref[0, :, columns[group]] = hidden[group].astype(ends_ref.dtype)
+        ends_ref[1, :, columns[group]] = pulled[group].astype(ends_ref.dtype)
+        sums_ref[pl.ds(pl.program_id(0) * groups + group, 1), :] = jnp.sum(
+            ddec_ref[group], axis=0, keepdims=True
+        )
 
 
 def scan_kernel(
@@ -77,6 +80,7 @@
     outb_ref,
     rates_ref,
     all_ref,
+    sums_ref,
     scanned_ref,
     along_ref,
     decayed_ref,
@@ -89,6 +93,7 @@
 ):
     groups, steps = ddec_ref.shape[:2]
     devices = all_ref.shape[0]
+    base = pl.program_id(0) * groups
     member = member_ref[0]
     columns = [pl.ds(group * LANES, LANES) for group in range(groups)]
     half = N // 2
@@ -98,14 +103,21 @@
         gin_ref[...] = jnp.zeros_like(gin_ref)
         gout_ref[...] = jnp.zeros_like(gout_ref)
 
-    def through(device, state, offset):
-        factor = jnp.exp2(all_ref[device, 2 * N : 2 * N + 1, :] * rates_ref[...])
-        return factor * state + all_ref[device, offset : offset + N, :]
-
-    nothing = jnp.zeros(rates_ref.shape, jnp.float32)
-    entering = lax.fori_loop(0, member, lambda d, s: through(d, s, 0), nothing)
+    def through(device, states):
+        new = []
+        for group in range(groups):
+            total = sums_ref[device, pl.ds(base + group, 1), :]
+            factor = jnp.exp2(total * rates_ref[:, columns[group]])
+            new.append(
+                factor * states[group]
+                + all_ref[device, :, columns[group]].astype(jnp.float32)
+            )
+        return new
+
+    zeros = [jnp.zeros((N, LANES), jnp.float32) for _ in range(groups)]
+    entering = lax.fori_loop(0, member, through, zeros)
     leaving = lax.fori_loop(
-        0, devices - 1 - member, lambda d, s: through(devices - 1 - d, s, N), nothing
+        0, devices - 1 - member, lambda d, s: through(devices - 1 - d, s), zeros
     )
 
     def fold(values):
@@ -123,9 +135,9 @@
             new.append(state)
         return new
 
-    kept[0] = entering
-    begin = [entering[:, group * LANES : (group + 1) * LANES] for group in range(groups)]
-    lax.fori_loop(0, steps, forward, begin, unroll=4)
+    for group in range(groups):
+        kept[0, :, columns[group]] = entering[group]
+    lax.fori_loop(0, steps, forward, entering, unroll=4)
 
     def collapse(source, target_ref):
         for group in range(groups):
@@ -161,9 +173,7 @@
         gout_ref[t] = gout
         return new
 
-    end = [leaving[:, group * LANES : (group + 1) * LANES] for group in range(groups)]
-    zeros = [jnp.zeros((N, LANES), jnp.float32) for _ in range(groups)]
-    _, grates = lax.fori_loop(0, steps, backward, (end, zeros), unroll=4)
+    _, grates = lax.fori_loop(0, steps, backward, (leaving, zeros), unroll=4)
     collapse(first, along_ref)
     collapse(second, decayed_ref)
     for group in range(groups):
@@ -178,14 +188,20 @@
         ends_kernel,
         grid=(E // block,),
         in_specs=[wide, wide, wide, whole, whole, pl.BlockSpec((N, block), lambda b: (0, b))],
-        out_specs=pl.BlockSpec((2 * N + 8, block), lambda b: (0, b)),
-        out_shape=jax.ShapeDtypeStruct((2 * N + 8, E), jnp.float32),
+        out_specs=[
+            pl.BlockSpec((2, N, block), lambda b: (0, 0, b)),
+            pl.BlockSpec((E // LANES, LANES), lambda b: (0, 0)),
+        ],
+        out_shape=[
+            jax.ShapeDtypeStruct((2, N, E), jnp.bfloat16),
+            jax.ShapeDtypeStruct((E // LANES, LANES), jnp.float32),
+        ],
         compiler_params=pltpu.CompilerParams(vmem_limit_bytes=48 * 2**20),
         name="ends",
     )(ddec, drive, grady, inb, outb, rates)
 
 
-def scan_of(member, ddec, drive, grady, inb, outb, rates, everyone, block):
+def scan_of(member, ddec, drive, grady, inb, outb, rates, everyone, sums, block):
     steps = ddec.shape[1]
     devices = everyone.shape[0]
     groups = block // LANES
@@ -205,7 +221,8 @@
             whole,
             whole,
             narrow,
-            pl.BlockSpec((devices, 2 * N + 8, block), lambda b: (0, 0, b)),
+            pl.BlockSpec((devices, N, block), lambda b: (0, 0, b)),
+            pl.BlockSpec(sums.shape, lambda b: (0, 0, 0)),
         ],
         out_specs=[wide, wide, wide, whole, whole, narrow],
         out_shape=[full, full, full, spread, spread, jax.ShapeDtypeStruct((N, E), jnp.float32)],
@@ -216,7 +233,308 @@
         ],
         compiler_params=pltpu.CompilerParams(vmem_limit_bytes=48 * 2**20),
         name="scan",
-    )(member, ddec, drive, grady, inb, outb, rates, everyone)
+    )(member, ddec, drive, grady, inb, outb, rates, everyone, sums)
+
+
+def partner(axis, offset):
+    size = lax.axis_size(axis)
+    return lax.rem(lax.axis_index(axis) + offset, size)
+
+
+def greet(counts):
+    barrier = pltpu.get_barrier_semaphore()
+    total = 0
+    for axis, count in counts:
+        for offset in range(1, count):
+            pl.semaphore_signal(
+                barrier, inc=1, device_id={axis: partner(axis, offset)}, device_id_type=MESH
+            )
+        total += count - 1
+    pl.semaphore_wait(barrier, total)
+
+
+def push(source, target, semaphores, at, axis, offset):
+    copy = pltpu.make_async_remote_copy(
+        src_ref=source,
+        dst_ref=target,
+        send_sem=semaphores.at[0, at],
+        recv_sem=semaphores.at[1, at],
+        device_id={axis: partner(axis, offset)},
+        device_id_type=MESH,
+    )
+    copy.start()
+    return copy
+
+
+def states_kernel(devices, ends_ref, sums_ref, ends_out, sums_out, wires, sum_wires):
+    member = lax.axis_index("seq")
+    greet((("seq", devices),))
+    copies = []
+    for offset in range(1, devices):
+        wrapped = (member + offset) // devices
+        copies.append(
+            push(ends_ref.at[wrapped], ends_out.at[member], wires, offset - 1, "seq", offset)
+        )
+        copies.append(push(sums_ref, sums_out.at[member], sum_wires, offset - 1, "seq", offset))
+    ends_out[member] = ends_ref[0]
+    sums_out[member] = sums_ref[...]
+    for copy in copies:
+        copy.wait()
+
+
+def states_of(ends, sums, devices):
+    return pl.pallas_call(
+        functools.partial(states_kernel, devices),
+        in_specs=[pl.BlockSpec(memory_space=pltpu.VMEM)] * 2,
+        out_specs=[pl.BlockSpec(memory_space=pltpu.VMEM)] * 2,
+        out_shape=[
+            jax.ShapeDtypeStruct((devices,) + ends.shape[1:], ends.dtype),
+            jax.ShapeDtypeStruct((devices,) + sums.shape, sums.dtype),
+        ],
+        scratch_shapes=[
+            pltpu.SemaphoreType.DMA((2, devices - 1)),
+            pltpu.SemaphoreType.DMA((2, devices - 1)),
+        ],
+        compiler_params=pltpu.CompilerParams(
+            collective_id=0, has_side_effects=True, vmem_limit_bytes=48 * 2**20
+        ),
+        name="states",
+    )(ends, sums)
+
+
+def trade_kernel(devices, gated_ref, back_ref, gated_out, back_out, wires, back_wires, local):
+    member = lax.axis_index("seq")
+    steps = gated_ref.shape[0]
+    channels = gated_ref.shape[1] // devices
+    rows = pl.ds(pl.multiple_of(member * steps, steps), steps)
+    greet((("seq", devices),))
+    copies = []
+    for offset in range(1, devices):
+        columns = pl.ds(pl.multiple_of(partner("seq", offset) * channels, channels), channels)
+        copies.append(
+            push(
+                back_ref.at[:, :, columns],
+                back_out.at[:, rows, :],
+                back_wires,
+                offset - 1,
+                "seq",
+                offset,
+            )
+        )
+        copies.append(
+            push(
+                gated_ref.at[:, columns], gated_out.at[rows, :], wires, offset - 1, "seq", offset
+            )
+        )
+    columns = pl.ds(pl.multiple_of(member * channels, channels), channels)
+    own = pltpu.make_async_copy(back_ref.at[:, :, columns], back_out.at[:, rows, :], local.at[0])
+    own_gated = pltpu.make_async_copy(
+        gated_ref.at[:, columns], gated_out.at[rows, :], local.at[1]
+    )
+    own.start()
+    own_gated.start()
+    own.wait()
+    own_gated.wait()
+    for copy in copies:
+        copy.wait()
+
+
+def trade(gated, back, devices):
+    steps = gated.shape[0]
+    channels = gated.shape[1] // devices
+    return pl.pallas_call(
+        functools.partial(trade_kernel, devices),
+        in_specs=[pl.BlockSpec(memory_space=pltpu.VMEM)] * 2,
+        out_specs=[pl.BlockSpec(memory_space=pltpu.VMEM)] * 2,
+        out_shape=[
+            jax.ShapeDtypeStruct((steps * devices, channels), gated.dtype),
+            jax.ShapeDtypeStruct((2, steps * devices, channels), back.dtype),
+        ],
+        scratch_shapes=[
+            pltpu.SemaphoreType.DMA((2, devices - 1)),
+            pltpu.SemaphoreType.DMA((2, devices - 1)),
+            pltpu.SemaphoreType.DMA((2,)),
+        ],
+        compiler_params=pltpu.CompilerParams(
+            collective_id=1, has_side_effects=True, vmem_limit_bytes=48 * 2**20
+        ),
+        name="trade",
+    )(gated, back)
+
+
+def grads_kernel(
+    nrows,
+    devices,
+    normed_ref,
+    back_ref,
+    gated_ref,
+    cot_ref,
+    small_ref,
+    gin_out,
+    gout_out,
+    small_out,
+    norm_out,
+    small_got,
+    small_part,
+    small_seq,
+    gout_sum,
+    gout_low,
+    gout_got,
+    gin_sum,
+    gin_low,
+    gin_got,
+    gin_part,
+    norm_seq,
+    norm_rows,
+    row_wires,
+    seq_wires,
+):
+    row = lax.axis_index("rows")
+    member = lax.axis_index("seq")
+    few = small_ref.shape[0] // nrows
+    outer = gout_out.shape[0] // nrows
+    inner = gin_part.shape[0] // devices
+    channels = small_out.shape[1]
+    greet((("rows", nrows), ("seq", devices)))
+
+    def share(index, size):
+        return pl.ds(pl.multiple_of(index * size, size), size)
+
+    def to_rows(kind, make):
+        return [
+            push(*make(partner("rows", offset), offset - 1), row_wires.at[kind], offset - 1, "rows", offset)
+            for offset in range(1, nrows)
+        ]
+
+    def to_seq(kind, make):
+        return [
+            push(*make(partner("seq", offset), offset - 1), seq_wires.at[kind], offset - 1, "seq", offset)
+            for offset in range(1, devices)
+        ]
+
+    def settle(copies):
+        for copy in copies:
+            copy.wait()
+
+    def squares(values):
+        return jnp.sum(values * values, axis=0, keepdims=True)
+
+    small_moves = to_rows(
+        0, lambda other, at: (small_ref.at[share(other, few)], small_got.at[at])
+    )
+    gout_sum[...] = lax.dot_general(
+        gated_ref[...], cot_ref[...], (((0,), (0,)), ((), ())), preferred_element_type=jnp.float32
+    )
+    gout_low[...] = gout_sum[...].astype(jnp.bfloat16)
+    gout_moves = to_rows(
+        1, lambda other, at: (gout_low.at[share(other, outer)], gout_got.at[at])
+    )
+    for half in range(2):
+        result = lax.dot_general(
+            normed_ref[...],
+            back_ref[half],
+            (((0,), (0,)), ((), ())),
+            preferred_element_type=jnp.float32,
+        )
+        wide = gin_sum.shape[2]
+        for place in range(nrows // 2):
+            piece = result[:, place * wide : (place + 1) * wide]
+            gin_sum[half * (nrows // 2) + place] = piece
+            gin_low[half * (nrows // 2) + place] = piece.astype(jnp.bfloat16)
+    gin_moves = to_rows(2, lambda other, at: (gin_low.at[other], gin_got.at[at]))
+
+    settle(small_moves)
+    total = small_ref[share(row, few), :].astype(jnp.float32)
+    for at in range(nrows - 1):
+        total = total + small_got[at].astype(jnp.float32)
+    small_part[...] = total.astype(jnp.bfloat16)
+    small_moves = to_seq(
+        0, lambda other, at: (small_part.at[:, share(other, channels)], small_seq.at[at])
+    )
+
+    settle(gout_moves)
+    total = gout_sum[share(row, outer), :]
+    for at in range(nrows - 1):
+        total = total + gout_got[at].astype(jnp.float32)
+    gout_out[share(row, outer), :] = total.astype(jnp.bfloat16)
+    gout_moves = to_rows(
+        3,
+        lambda other, at: (gout_out.at[share(row, outer)], gout_out.at[share(row, outer)]),
+    )
+    norm = jnp.sum(squares(total), axis=1, keepdims=True)
+
+    settle(gin_moves)
+    total = gin_sum[row]
+    for at in range(nrows - 1):
+        total = total + gin_got[at].astype(jnp.float32)
+    gin_part[...] = total.astype(jnp.bfloat16)
+    gin_moves = to_seq(
+        1, lambda other, at: (gin_part.at[share(other, inner)], gin_out.at[row, member])
+    )
+    gin_out[row, member] = gin_part[share(member, inner), :]
+    norm = norm + jnp.sum(squares(total), axis=1, keepdims=True)
+
+    settle(small_moves)
+    total = small_part[:, share(member, channels)].astype(jnp.float32)
+    for at in range(devices - 1):
+        total = total + small_seq[at].astype(jnp.float32)
+    small_out[share(row, few), :] = total.astype(jnp.bfloat16)
+    small_moves = to_rows(
+        4, lambda other, at: (small_out.at[share(row, few)], small_out.at[share(row, few)])
+    )
+    norm = norm + jnp.sum(squares(total), axis=1, keepdims=True)
+    norm_seq[member] = jnp.broadcast_to(norm, (8, LANES))
+    norm_moves = to_seq(2, lambda other, at: (norm_seq.at[member], norm_seq.at[member]))
+
+    settle(gin_moves)
+    gin_moves = to_rows(5, lambda other, at: (gin_out.at[row], gin_out.at[row]))
+    settle(norm_moves)
+    norm_rows[row] = jnp.sum(norm_seq[...], axis=0)
+    norm_moves = to_rows(6, lambda other, at: (norm_rows.at[row], norm_rows.at[row]))
+    settle(norm_moves)
+    norm_out[...] = jnp.sqrt(jnp.sum(norm_rows[...], axis=0))
+    settle(small_moves)
+    settle(gout_moves)
+    settle(gin_moves)
+
+
+def grads_of(normed_all, back_mine, gated_mine, cot_all, small, nrows, devices):
+    depth = normed_all.shape[1]
+    channels = gated_mine.shape[1]
+    wide = 2 * channels // nrows
+    few = small.shape[0] // nrows
+    low = jnp.bfloat16
+    return pl.pallas_call(
+        functools.partial(grads_kernel, nrows, devices),
+        in_specs=[pl.BlockSpec(memory_space=pltpu.VMEM)] * 5,
+        out_specs=[pl.BlockSpec(memory_space=pltpu.VMEM)] * 4,
+        out_shape=[
+            jax.ShapeDtypeStruct((nrows, devices, depth // devices, wide), low),
+            jax.ShapeDtypeStruct((channels, depth), low),
+            jax.ShapeDtypeStruct((small.shape[0], channels), low),
+            jax.ShapeDtypeStruct((8, LANES), jnp.float32),
+        ],
+        scratch_shapes=[
+            pltpu.VMEM((nrows - 1, few, E), low),
+            pltpu.VMEM((few, E), low),
+            pltpu.VMEM((devices - 1, few, channels), low),
+            pltpu.VMEM((channels, depth), jnp.float32),
+            pltpu.VMEM((channels, depth), low),
+            pltpu.VMEM((nrows - 1, channels // nrows, depth), low),
+            pltpu.VMEM((nrows, depth, wide), jnp.float32),
+            pltpu.VMEM((nrows, depth, wide), low),
+            pltpu.VMEM((nrows - 1, depth, wide), low),
+            pltpu.VMEM((depth, wide), low),
+            pltpu.VMEM((devices, 8, LANES), jnp.float32),
+            pltpu.VMEM((nrows, 8, LANES), jnp.float32),
+            pltpu.SemaphoreType.DMA((7, 2, nrows - 1)),
+            pltpu.SemaphoreType.DMA((3, 2, devices - 1)),
+        ],
+        compiler_params=pltpu.CompilerParams(
+            collective_id=2, has_side_effects=True, vmem_limit_bytes=56 * 2**20
+        ),
+        name="grads",
+    )(normed_all, back_mine, gated_mine, cot_all, small)
 
 
 def local(
@@ -318,11 +636,11 @@
         return jnp.transpose(values, (1, 0, 2)).reshape(steps, E)
 
     ddec, drive, grady_rows = grouped(ddec), grouped(drive), grouped(grad_y)
-    ends = ends_of(ddec, drive, grady_rows, inb, outb, scaled_rates, 512)
-    everyone = lax.all_gather(ends, "seq", axis=0)
+    ends, sums = ends_of(ddec, drive, grady_rows, inb, outb, scaled_rates, 512)
+    everyone, all_sums = states_of(ends, sums, devices)
     member_word = jnp.reshape(member_id, (1,)).astype(jnp.int32)
     scanned, along_in, pulled_sum, gin, gout, grad_rates = scan_of(
-        member_word, ddec, drive, grady_rows, inb, outb, scaled_rates, everyone, 512
+        member_word, ddec, drive, grady_rows, inb, outb, scaled_rates, everyone, all_sums, 512
     )
     scanned, along_in, pulled_sum = flat(scanned), flat(along_in), flat(pulled_sum)
     y_full = scanned + d_skip[None, :] * act
@@ -330,10 +648,6 @@
     block_output = (
         stream + jnp.dot(gated, out_proj, preferred_element_type=jnp.float32)
     )[None]
-    gated_mine = lax.all_to_all(gated, "seq", split_axis=1, concat_axis=0, tiled=True)
-    grad_out_proj = lax.dot_general(
-        gated_mine, cot_all, (((0,), (0,)), ((), ())), preferred_element_type=jnp.float32
-    )
     grad_gates = chan_back * y_full * silu_slope(gates)
     grad_dskip = jnp.sum(grad_y * act, axis=0)
     grad_in_mat = jnp.sum(gin, axis=2)
@@ -375,14 +689,10 @@
         grad_inner = grad_inner + conv_weight[offset][None, :] * masked[offset : offset + steps]
     grad_convw = jnp.stack(conv_rows)
     back_xz = jnp.stack([grad_inner, grad_gates]).astype(jnp.bfloat16)
-    back_mine = lax.all_to_all(back_xz, "seq", split_axis=2, concat_axis=1, tiled=True)
     grad_normed = lax.dot_general(
         back_xz[0], in_proj[:, :E], (((1,), (1,)), ((), ())), preferred_element_type=jnp.float32
     ) + lax.dot_general(
         back_xz[1], in_proj[:, E:], (((1,), (1,)), ((), ())), preferred_element_type=jnp.float32
-    )
-    grad_in_proj = jnp.einsum(
-        "td,ktc->dkc", normed_all, back_mine, preferred_element_type=jnp.float32
     )
     grad_gain = jnp.sum(grad_normed * stream * inverse, axis=0)
     scaled = grad_normed * norm_gain[None, :]
@@ -391,8 +701,6 @@
         + inverse * scaled
         - stream * inverse * inverse * inverse * jnp.mean(scaled * stream, axis=1, keepdims=True)
     )
-    summed = lax.psum((grad_in_proj, grad_out_proj), "rows")
-    in_share = lax.all_to_all(summed[0], "seq", split_axis=0, concat_axis=2, tiled=True)
     small = jnp.concatenate(
         [
             grad_xproj.T,
@@ -406,11 +714,41 @@
                 grad_gain.reshape(devices, D // devices),
                 ((0, 0), (0, channels - D // devices)),
             ).reshape(1, E),
+            jnp.zeros((8, E), jnp.float32),
         ],
         axis=0,
     )
-    small = lax.psum(small, "rows")
-    small = lax.psum_scatter(small, "seq", scatter_dimension=1, tiled=True)
+    nrows = lax.axis_size("rows")
+    if channels % LANES == 0 and 2 * channels == nrows * LANES:
+        gated_mine, back_mine = trade(gated, back_xz, devices)
+        gin_parts, gout_share, small, norm_tile = grads_of(
+            normed_all, back_mine, gated_mine, cot_all, small.astype(jnp.bfloat16), nrows, devices
+        )
+        gin_share = jnp.transpose(
+            gin_parts.reshape(2, nrows // 2, devices, D // devices, LANES), (3, 0, 2, 1, 4)
+        ).reshape(D // devices, 2 * E)
+        grad_norm = norm_tile[0, 0]
+    else:
+        gated_mine = lax.all_to_all(gated, "seq", split_axis=1, concat_axis=0, tiled=True)
+        back_mine = lax.all_to_all(back_xz, "seq", split_axis=2, concat_axis=1, tiled=True)
+        gout_share = lax.psum(
+            lax.dot_general(
+                gated_mine, cot_all, (((0,), (0,)), ((), ())), preferred_element_type=jnp.float32
+            ),
+            "rows",
+        )
+        gin_share = lax.psum(
+            jnp.einsum("td,ktc->dkc", normed_all, back_mine, preferred_element_type=jnp.float32),
+            "rows",
+        )
+        gin_share = lax.all_to_all(
+            gin_share, "seq", split_axis=0, concat_axis=2, tiled=True
+        ).reshape(D // devices, 2 * E)
+        small = lax.psum(small, "rows")
+        small = lax.psum_scatter(small, "seq", scatter_dimension=1, tiled=True)
+        squares = jnp.sum(gin_share * gin_share) + jnp.sum(gout_share * gout_share)
+        grad_norm = jnp.sqrt(lax.psum(squares + jnp.sum(small * small), "seq"))
+    small = small.astype(jnp.float32)
     parts = []
     at = 0
     for count in (R + 2 * N, R, N, K, 1, 1, 1, 1):
@@ -418,7 +756,7 @@
         at += count
     owner_grads = (
         parts[7][0, : D // devices],
-        in_share.reshape(D // devices, 2 * E),
+        gin_share.astype(jnp.float32),
         parts[3],
         parts[4][0],
         parts[0].T,
@@ -426,7 +764,7 @@
         parts[5][0],
         parts[2],
         parts[6][0],
-        summed[1],
+        gout_share.astype(jnp.float32),
     )
     conv_mine = lax.dynamic_slice_in_dim(conv_weight, begin, channels, 1)
     cbias_mine = lax.dynamic_slice_in_dim(conv_bias, begin, channels, 0)
@@ -435,11 +773,6 @@
     dtbias_mine = lax.dynamic_slice_in_dim(dt_bias, begin, channels, 0)
     alog_mine = lax.dynamic_slice_in_dim(a_log, begin, channels, 1)
     dskip_mine = lax.dynamic_slice_in_dim(d_skip, begin, channels, 0)
-    squares = jnp.float32(0.0)
-    for member in owner_grads:
-        squares = squares + jnp.sum(member * member)
-    squares_all = lax.psum(squares, "seq")
-    grad_norm = jnp.sqrt(squares_all)
     shrink_by = 1.0 / jnp.maximum(grad_norm, 1.0)
     gain_rows = D // devices
     outer_rows = E // devices

time: 410 us -> 243 us (0.59)
  waiting for transfers between devices: 205 us -> 0.04 us
  Pallas kernels: 28.3 us -> 147 us
  local copies, waits for them, and re-layouts: 44.3 us -> 18.7 us
  blocking collectives: 15 us -> 0 us
  starting transfers between devices: 18.9 us -> 3.91 us
  matrix products: 36.3 us -> 21.4 us
  between operations: 23.3 us -> 15.9 us
    pallas_call x0 -> x3, Pallas kernels: none -> 120 us  [the longest x1 64 us: grads_of(): pl.pallas_call(functools.partial(grads_kernel, nrows, devices), in_specs=...]
    psum x1 -> x0, waiting for transfers between devices: 90.7 us -> none  [local(): small = lax.psum(small, 'rows')]
    all_to_all x3 -> x0, waiting for transfers between devices: 75.5 us -> none  [the longest x1 40.7 us: local(): lax.all_to_all(summed[0], 'seq', split_axis=0, concat_axis=2, tiled=True)]
    all_gather x1 -> x0, waiting for transfers between devices: 37.3 us -> none  [local(): everyone = lax.all_gather(ends, 'seq', axis=0)]
    psum x1 -> x0, blocking collectives: 15 us -> none  [local(): squares_all = lax.psum(squares, 'seq')]
    all_to_all x3 -> x0, starting transfers between devices: 14.4 us -> none  [the longest x1 5.08 us: local(): lax.all_to_all(back_xz, 'seq', split_axis=2, concat_axis=1, tiled=True)]
    mul x4 -> x0, local copies, waits for them, and re-layouts: 9.93 us -> none  [the longest x2 5.06 us: local(): grad_delta = along_in * act + pulled_sum * math.log(2.0)]
    dot_general x2 -> x0, matrix products: 7.48 us -> none  [the longest x1 4.19 us: local(): jnp.einsum('td,ktc->dkc', normed_all, back_mine, preferred_element_type=j...]
  transfers between devices with their start and end apart: 10 -> 4, of which waited for: 5 -> 0; matrix products, arithmetic and copies ran while one was open for 15% -> 15% of each run, Pallas kernels for 5% -> 34%
where the time goes in v1:
time: 243 us; the launch traced here: 242 us
  Pallas kernels  147 us (60%)
  other arithmetic  34.5 us (14%)
  matrix products  21.4 us (9%)
  local copies, waits for them, and re-layouts  18.7 us (8%)
  between operations  15.9 us (7%)
  starting transfers between devices  3.91 us (2%)
    pallas_call x1, Pallas kernels, grads_of(): pl.pallas_call(functools.partial(grads_kernel, nrows, devices), in_specs=...  64 us
    pallas_call x1, Pallas kernels, trade(): pl.pallas_call(functools.partial(trade_kernel, devices), in_specs=[pl.Blo...  40.2 us
    pallas_call x1, Pallas kernels, scan_of(): pl.pallas_call(scan_kernel, grid=(E // block,), in_specs=[pl.BlockSpec(me...  21 us
    add x10, other arithmetic, local(): AVERAGE * averages[ordinal] + (1.0 - AVERAGE) * renewed  19.6 us
    pallas_call x1, Pallas kernels, states_of(): pl.pallas_call(functools.partial(states_kernel, devices), in_specs=[pl.Bl...  15.3 us
    unnamed x144, local copies, waits for them, and re-layouts  7.59 us
    pallas_call x1, Pallas kernels, ends_of(): pl.pallas_call(ends_kernel, grid=(E // block,), in_specs=[wide, wide, wid...  6.87 us
  transfers between devices with their start and end apart: 4, of which 0 were waited for; matrix products, arithmetic and copies ran while one was open for 15% of the time, Pallas kernels for 34%

profile of v1, /device:TPU:0, one launch (start us, length us, event | category | flops | bytes accessed | tf_op | source)
XLA Modules:
  0.0 241.9 jit_solution(9888815010583004232)
XLA Ops:
  7.3 1.1 fusion.41
  8.4 0.5 copy-done.58
  8.9 1.8 fusion.36
  10.8 4.8 %convolution_convert_fusion = bf16[128,4096]{1,0:T(8,128)(2,1)S(1)} fusion(bf16[128,1024]{1,0:T(8,128)(2,1)} %fusion.36, bf16[1024,4096]{1,0:T(8,128)(2,1)} %param.37), kind=kOutput, calls=%fused_computation | convolution fusion | flops 1074266112 | bytes 9699328 | tf_op jit(solution)/shard_map/dot_general | solution.py:587
  15.6 2.4 collective-permute-start
  18.4 3.8 %fusion.5 = f32[128,2048]{1,0:T(8,128)S(1)} fusion(bf16[2048,1024]{1,0:T(8,128)(2,1)} %param.45, bf16[1,128,1024]{2,1,0:T(8,128)(2,1)S(1)} %copy-done.24), kind=kOutput, calls=%fused_computation.10 | convolution fusion | flops 537395200 | bytes 5505024 | tf_op jit(solution)/shard_map/dot_general | solution.py:591
  23.0 2.8 %multiply_reduce_fusion = (bf16[2048]{0:T(1024)(128)(2,1)}, f32[128,2048]{1,0:T(8,128)S(1)}, f32[16,16,8,128]{3,2,1,0:T(8,128)}) fusion(f32[128,2048]{1,0:T(8,128)S(1)} %fusion.5, bf16[128,4096]{1,0:T(8,128)(2,1)S(1)} %convolution_convert_fusion, f32[128]{0:T(128)S(1)} %slice.186, f32[136,2048]{1,0:T(8,128)S(1)} %maximum_convert_fusion, ...), kind=kLoop, calls=%fused_computation.68 | loop fusion | flops 6289408 | bytes 7911424 | tf_op jit(solution)/shard_map/reduce_sum | solution.py:652
  26.6 0.9 copy-done.22
  27.9 0.8 multiply_bitcast_fusion.1
  29.7 6.9 %ends.1 = (bf16[2,16,2048]{2,1,0:T(8,128)(2,1)S(1)}, f32[16,128]{1,0:T(8,128)S(1)}) custom-call(f32[16,128,128]{2,1,0:T(8,128)S(1)} %get-tuple-element.132.ddec_ref, f32[16,128,128]{2,1,0:T(8,128)S(1)} %get-tuple-element.131.drive_ref, f32[16,128,128]{2,1,0:T(8,128)S(1)} %bitcast.129, f32[128,16,128]{2,1,0:T(8,128)S(1)} %broadcast_in_dim.36.inb_ref, ...), custom_call_target="tpu_custom_call" | custom-call | tf_op jit(solution)/shard_map/ends/pallas_call | solution.py:187
  36.6 15.3 %states.1 = (bf16[8,16,2048]{2,1,0:T(8,128)(2,1)S(1)}, f32[8,16,128]{2,1,0:T(8,128)S(1)}) custom-call(bf16[2,16,2048]{2,1,0:T(8,128)(2,1)S(1)} %get-tuple-element.49.ends_ref, f32[16,128]{1,0:T(8,128)S(1)} %get-tuple-element.50.sums_ref), custom_call_target="tpu_custom_call" | custom-call | tf_op jit(solution)/shard_map/states/pallas_call | solution.py:286
  52.0 21.0 %scan.1 = (f32[16,128,128]{2,1,0:T(8,128)S(1)}, f32[16,128,128]{2,1,0:T(8,128)S(1)}, f32[16,128,128]{2,1,0:T(8,128)S(1)}, f32[128,16,128]{2,1,0:T(8,128)S(1)}, f...) custom-call(s32[1]{0:T(128)} %bitcast.1.member_ref, f32[16,128,128]{2,1,0:T(8,128)} %copy-done.4, ...), custom_call_target="tpu_custom_call" | custom-call | tf_op jit(solution)/shard_map/scan/pallas_call | solution.py:213
  73.1 0.6 fusion.59
  74.0 0.8 copy-done.20
  76.1 4.0 %fusion.4 = f32[128,2048]{1,0:T(8,128)S(1)} fusion(bf16[2048,96]{0,1:T(8,128)(2,1)} %param.40, f32[128,2048]{1,0:T(8,128)} %copy-done.11, f32[2048]{0:T(1024)S(1)} %copy-done.43, f32[128,2048]{1,0:T(8,128)} %copy-done.14, bf16[128,16]{0,1:T(8,128)(2,1)S(1)} %copy.95, bf16[128,16]{0,1:T(8,128)(2,1)S(1)} %copy.94, ...), kind=kOutput, calls=%fused_computation.7 | convolution fusion | flops 56696832 | bytes 6193152 | tf_op jit(solution)/shard_map/dot_general | solution.py:672
  80.0 1.5 collective-permute-start.1
  81.6 0.8 fusion.18
  82.4 3.9 %fusion = f32[128,1024]{1,0:T(8,128)S(1)} fusion(bf16[128,2048]{1,0:T(8,128)(2,1)S(1)} %get-tuple-element.110, bf16[1024,4096]{1,0:T(8,128)(2,1)} %param.37), kind=kOutput, calls=%fused_computation.1 | convolution fusion | flops 536870912 | bytes 5242880 | tf_op jit(solution)/shard_map/dot_general | solution.py:694
  86.3 1.5 fusion.6
  87.8 0.5 convolution_convert_fusion.2
  88.4 0.5 copy-done.21
  89.5 0.9 copy-done.9
  90.4 0.7 fusion.22
  91.4 0.5 fusion.26
  92.0 1.2 slice-done.1
  93.2 1.7 fusion.44
  95.0 40.2 %trade.1 = (bf16[1024,256]{1,0:T(8,128)(2,1)S(1)}, bf16[2,1024,256]{2,1,0:T(8,128)(2,1)S(1)}) custom-call(bf16[128,2048]{1,0:T(8,128)(2,1)S(1)} %get-tuple-element.111.gated_ref, bf16[2,128,2048]{2,1,0:T(8,128)(2,1)S(1)} %pad_maximum_fusion.1.back_ref), custom_call_target="tpu_custom_call" | custom-call | tf_op jit(solution)/shard_map/trade/pallas_call | solution.py:345
  135.2 1.0 copy-done.5
  136.2 0.8 copy-done.7
  137.0 4.1 %concatenate.17.small_ref = bf16[192,2048]{1,0:T(8,128)(2,1)} concatenate(bf16[96,2048]{1,0:T(8,128)(2,1)S(1)} %convolution_convert_fusion.2, bf16[64,2048]{1,0:T(8,128)(2,1)S(1)} %convolution_convert_fusion.3, bf16[16,2048]{1,0:T(8,128)(2,1)S(1)} %multiply_convert_fusion.1, bf16[1,2048]{1,0:T(2,128)(2,1)S(1)} %stack.31, bf16[1,2048]{1,0:T(2,128)(2,1)S(1)} %stack.32, ...), dimensions={0} | concatenate | bytes 1572864 | tf_op jit(solution)/shard_map/concatenate | solution.py:704
  141.1 1.0 fusion.40
  142.1 64.0 %grads.1 = (bf16[4,8,128,128]{3,2,1,0:T(8,128)(2,1)}, bf16[256,1024]{1,0:T(8,128)(2,1)}, bf16[192,256]{1,0:T(8,128)(2,1)}, f32[8,128]{1,0:T(8,128)}) custom-call(bf16[1024,1024]{1,0:T(8,128)(2,1)} %all-gather.4.cloned.1.call-done.normed_ref, bf16[2,1024,256]{2,1,0:T(8,128)(2,1)} %copy-done.5, bf16[1024,256]{1,0:T(8,128)(2,1)} %copy-done.7, ...), custom_call_target="tpu_custom_call" | custom-call | tf_op jit(solution)/shard_map/grads/pallas_call | solution.py:507
  206.1 1.2 slice.201
  208.0 0.9 convert_element_type.106
  208.9 0.6 slice_multiply_fusion.10
  209.5 1.5 convert_multiply_fusion
  211.0 1.6 copy.96
  212.6 2.7 %mul.666 = f32[128,4096]{1,0:T(8,128)} reshape(f32[128,2,8,2,128]{4,3,2,1,0:T(2,128)S(1)} %copy.96) | data formatting | bytes 4194304 | tf_op jit(solution)/shard_map/mul | solution.py:819
  215.3 1.3 multiply_add_fusion.8
  216.7 1.6 multiply_add_fusion.6
  218.2 1.7 multiply_add_fusion.4
  219.9 1.3 multiply_add_fusion.10
  221.4 3.8 %multiply_add_fusion.2 = (f32[256,1024]{1,0:T(8,128)}, f32[256,1024]{1,0:T(8,128)}, f32[256,1024]{1,0:T(8,128)}) fusion(f32[256,1024]{1,0:T(8,128)S(1)} %copy-done.30, f32[]{:T(128)S(6)} %div.25, bf16[256,1024]{1,0:T(8,128)(2,1)} %get-tuple-element.64, bf16[2048,1024]{1,0:T(8,128)(2,1)} %param.45, s32[]{:T(128)S(6)} %select_n.25, f32[256,1024]{1,0:T(8,128)} %param.55), kind=kLoop, calls=%fused_computation.64 | loop fusion | flops 3145728 | bytes 6291464 | tf_op jit(solution)/shard_map/add | solution.py:824
  225.2 1.3 multiply_add_fusion.12
  226.5 1.3 multiply_add_fusion.14
  227.9 1.3 multiply_add_fusion.16
  229.2 1.3 multiply_add_fusion.18
  230.5 4.6 %multiply_add_fusion = (f32[128,4096]{1,0:T(8,128)}, f32[128,4096]{1,0:T(8,128)}, f32[128,4096]{1,0:T(8,128)}) fusion(f32[128,4096]{1,0:T(8,128)S(1)} %copy-done.26, f32[128,4096]{1,0:T(8,128)S(1)} %copy-done.17, bf16[1024,4096]{1,0:T(8,128)(2,1)} %param.37, s32[]{:T(128)S(6)} %select_n.24, f32[128,4096]{1,0:T(8,128)S(1)} %copy-done.27), kind=kLoop, calls=%fused_computation.13 | loop fusion | flops 5242880 | bytes 13631492 | tf_op jit(solution)/shard_map/add | solution.py:824
  (191 shorter events, 5.9 us)
Async XLA Ops:
  7.2 134.9 %all-gather.4.cloned.1.call-start = ((), (), s32[]{:S(2)}) async-start(), calls=%async_computation | async-start | bytes 2359296 | tf_op jit(solution)/shard_map/all_gather | solution.py:585
  10.7 7.3 %copy-start.68 = (s32[1,8]{1,0:T(1,128)S(1)}, s32[1,8]{1,0:T(1,128)}, u32[]{:S(2)}) copy-start(s32[1,8]{1,0:T(1,128)} %param.35) | copy-start | bytes 100
  10.7 7.7 %copy-start.39 = (f32[4,2048]{1,0:T(4,128)S(1)}, f32[4,2048]{1,0:T(4,128)}, u32[]{:S(2)}) copy-start(f32[4,2048]{1,0:T(4,128)} %param.38) | copy-start | bytes 98308
  10.7 7.7 %copy-start.24 = (bf16[1,128,1024]{2,1,0:T(8,128)(2,1)S(1)}, bf16[1,128,1024]{2,1,0:T(8,128)(2,1)}, u32[]{:S(2)}) copy-start(bf16[1,128,1024]{2,1,0:T(8,128)(2,1)} %param.34) | copy-start | bytes 786436
  10.7 131.4 %all-gather.6.cloned.1.call-start = ((), (), s32[]{:S(2)}) async-start(), calls=%async_computation.1 | async-start | bytes 2359296 | tf_op jit(solution)/shard_map/all_gather | solution.py:586
  15.6 7.2 %copy-start.18 = (bf16[128,4096]{1,0:T(8,128)(2,1)}, bf16[128,4096]{1,0:T(8,128)(2,1)S(1)}, u32[]{:S(2)}) copy-start(bf16[128,4096]{1,0:T(8,128)(2,1)S(1)} %convolution_convert_fusion) | copy-start | bytes 3145732
  15.6 7.0 %collective-permute-start = (bf16[8,2048]{1,0:T(8,128)(2,1)S(1)}, bf16[8,2048]{1,0:T(8,128)(2,1)S(1)}, u32[]{:S(2)}, u32[]{:S(2)}) collective-permute-start(bf16[8,2048]{1,0:T(8,128)(2,1)S(1)} %slice.210), channel_id=1, source_target_pairs={{0,1},{1,2},{2,3},{3,4},{4,5},{5,6},{6,7},{8,9},{9,10},{10,11},{11... | collective-permute-start | bytes 98312 | tf_op jit(solution)/shard_map/ppermute | solution.py:588
  18.4 4.4 %copy-start.34 = (f32[1,2048]{1,0:T(1,128)}, f32[1,2048]{1,0:T(1,128)S(1)}, u32[]{:S(2)}) copy-start(f32[1,2048]{1,0:T(1,128)S(1)} %get-tuple-element.125) | copy-start | bytes 24580
  18.4 4.4 %copy-start.36 = (f32[1,2048]{1,0:T(1,128)}, f32[1,2048]{1,0:T(1,128)S(1)}, u32[]{:S(2)}) copy-start(f32[1,2048]{1,0:T(1,128)S(1)} %get-tuple-element.126) | copy-start | bytes 24580
  18.4 3.8 %copy-start.31 = (f32[16,2048]{1,0:T(8,128)S(1)}, f32[16,2048]{1,0:T(8,128)}, u32[]{:S(2)}) copy-start(f32[16,2048]{1,0:T(8,128)} %param.43) | copy-start | bytes 393220
  22.3 3.5 %copy-start.15 = (f32[128,2048]{1,0:T(8,128)}, f32[128,2048]{1,0:T(8,128)S(1)}, u32[]{:S(2)}) copy-start(f32[128,2048]{1,0:T(8,128)S(1)} %fusion.5) | copy-start | bytes 3145732
  22.4 3.4 %copy-start.49 = (f32[136]{0:T(256)}, f32[136]{0:T(256)S(1)}, u32[]{:S(2)}) copy-start(f32[136]{0:T(256)S(1)} %get-tuple-element.127) | copy-start | bytes 1636
  22.4 3.4 %copy-start.51 = (f32[136]{0:T(256)}, f32[136]{0:T(256)S(1)}, u32[]{:S(2)}) copy-start(f32[136]{0:T(256)S(1)} %get-tuple-element.128) | copy-start | bytes 1636
  22.4 3.4 %copy-start.53 = (f32[136]{0:T(256)}, f32[136]{0:T(256)S(1)}, u32[]{:S(2)}) copy-start(f32[136]{0:T(256)S(1)} %get-tuple-element.129) | copy-start | bytes 1636
  22.5 3.2 %copy-start.47 = (f32[128]{0:T(128)}, f32[128]{0:T(128)S(1)}, u32[]{:S(2)}) copy-start(f32[128]{0:T(128)S(1)} %slice.170) | copy-start | bytes 1540
  22.7 3.0 %copy-start.8 = (f32[136,2048]{1,0:T(8,128)}, f32[136,2048]{1,0:T(8,128)S(1)}, u32[]{:S(2)}) copy-start(f32[136,2048]{1,0:T(8,128)S(1)} %maximum_convert_fusion) | copy-start | bytes 3342340
  23.0 2.8 %copy-start.46 = (bf16[2048,96]{0,1:T(8,128)(2,1)S(1)}, bf16[2048,96]{0,1:T(8,128)(2,1)}, u32[]{:S(2)}) copy-start(bf16[2048,96]{0,1:T(8,128)(2,1)} %param.40) | copy-start | bytes 1179652
  27.9 45.1 %copy-start.14 = (f32[128,2048]{1,0:T(8,128)}, f32[128,2048]{1,0:T(8,128)S(1)}, u32[]{:S(2)}) copy-start(f32[128,2048]{1,0:T(8,128)S(1)} %convolution_add_fusion.1) | copy-start | bytes 3145732
  29.0 7.6 %copy-start.3 = (f32[16,128,128]{2,1,0:T(8,128)}, f32[16,128,128]{2,1,0:T(8,128)S(1)}, u32[]{:S(2)}) copy-start(f32[16,128,128]{2,1,0:T(8,128)S(1)} %get-tuple-element.131.drive_ref) | copy-start | bytes 3145732
  29.0 7.6 %copy-start.4 = (f32[16,128,128]{2,1,0:T(8,128)}, f32[16,128,128]{2,1,0:T(8,128)S(1)}, u32[]{:S(2)}) copy-start(f32[16,128,128]{2,1,0:T(8,128)S(1)} %get-tuple-element.132.ddec_ref) | copy-start | bytes 3145732
  29.4 7.3 %copy-start.1 = (f32[128,16,128]{2,1,0:T(8,128)}, f32[128,16,128]{2,1,0:T(8,128)S(1)}, u32[]{:S(2)}) copy-start(f32[128,16,128]{2,1,0:T(8,128)S(1)} %broadcast_in_dim.36.inb_ref) | copy-start | bytes 3145732
  29.7 6.9 %copy-start.2 = (f32[128,16,128]{2,1,0:T(8,128)}, f32[128,16,128]{2,1,0:T(8,128)S(1)}, u32[]{:S(2)}) copy-start(f32[128,16,128]{2,1,0:T(8,128)S(1)} %broadcast_in_dim.37.outb_ref) | copy-start | bytes 3145732
  52.0 21.1 %copy-start.12 = (f32[128,2048]{1,0:T(8,128)S(1)}, f32[128,2048]{1,0:T(8,128)}, u32[]{:S(2)}) copy-start(f32[128,2048]{1,0:T(8,128)} %copy-done.11) | copy-start | bytes 3145732
  76.0 5.5 %copy-start.13 = (f32[128,2048]{1,0:T(8,128)S(1)}, f32[128,2048]{1,0:T(8,128)}, u32[]{:S(2)}) copy-start(f32[128,2048]{1,0:T(8,128)} %copy-done.11) | copy-start | bytes 3145732
  76.0 5.5 %copy-start.16 = (f32[128,2048]{1,0:T(8,128)S(1)}, f32[128,2048]{1,0:T(8,128)}, u32[]{:S(2)}) copy-start(f32[128,2048]{1,0:T(8,128)} %copy-done.15) | copy-start | bytes 3145732
  76.1 5.5 %copy-start.19 = (bf16[128,4096]{1,0:T(8,128)(2,1)S(1)}, bf16[128,4096]{1,0:T(8,128)(2,1)}, u32[]{:S(2)}) copy-start(bf16[128,4096]{1,0:T(8,128)(2,1)} %copy-done.18) | copy-start | bytes 3145732
  80.0 9.1 %collective-permute-start.1 = (f32[8,2048]{1,0:T(8,128)S(1)}, f32[8,2048]{1,0:T(8,128)S(1)}, u32[]{:S(2)}, u32[]{:S(2)}) collective-permute-start(f32[8,2048]{1,0:T(8,128)S(1)} %slice.220), channel_id=1, source_target_pairs={{1,0},{2,1},{3,2},{4,3},{5,4},{6,5},{7,6},{9,8},{10,9},{11,10},{12... | collective-permute-start | bytes 196616 | tf_op jit(solution)/shard_map/ppermute | solution.py:677
  82.4 3.9 %copy-start.10 = (bf16[2048,1024]{1,0:T(8,128)(2,1)S(1)}, bf16[2048,1024]{1,0:T(8,128)(2,1)}, u32[]{:S(2)}) copy-start(bf16[2048,1024]{1,0:T(8,128)(2,1)} %param.45) | copy-start | bytes 12582916
  82.4 3.9 %copy-start.23 = (bf16[1,128,1024]{2,1,0:T(8,128)(2,1)S(1)}, bf16[1,128,1024]{2,1,0:T(8,128)(2,1)}, u32[]{:S(2)}) copy-start(bf16[1,128,1024]{2,1,0:T(8,128)(2,1)} %param.33) | copy-start | bytes 786436
  89.2 2.8 %slice-start = ((s8[8388608]{0:T(1024)(128)(4,1)}), s8[4194304]{0:T(1024)(128)(4,1)S(1)}, s32[]{:S(2)}) async-start(s8[8388608]{0:T(1024)(128)(4,1)} %bitcast.131), calls=%async_computation.2 | async-start | bytes 8388608
  90.4 2.8 %slice-start.1 = ((s8[8388608]{0:T(1024)(128)(4,1)}), s8[4194304]{0:T(1024)(128)(4,1)S(1)}, s32[]{:S(2)}) async-start(s8[8388608]{0:T(1024)(128)(4,1)} %bitcast.131), calls=%async_computation.3 | async-start | bytes 8388608
  95.0 46.1 %copy-start.25 = (bf16[1,128,1024]{2,1,0:T(8,128)(2,1)S(1)}, bf16[1,128,1024]{2,1,0:T(8,128)(2,1)}, u32[]{:S(2)}) copy-start(bf16[1,128,1024]{2,1,0:T(8,128)(2,1)} %param.34) | copy-start | bytes 786436
  212.6 4.0 %copy-start.38 = (f32[64,256]{1,0:T(8,128)S(1)}, f32[64,256]{1,0:T(8,128)}, u32[]{:S(2)}) copy-start(f32[64,256]{1,0:T(8,128)} %param.61) | copy-start | bytes 196612
  212.6 8.6 %copy-start.30 = (f32[256,1024]{1,0:T(8,128)S(1)}, f32[256,1024]{1,0:T(8,128)}, u32[]{:S(2)}) copy-start(f32[256,1024]{1,0:T(8,128)} %param.65) | copy-start | bytes 3145732
  218.2 7.0 %copy-start.61 = (f32[256]{0:T(256)S(1)}, f32[256]{0:T(256)}, u32[]{:S(2)}) copy-start(f32[256]{0:T(256)} %param.54) | copy-start | bytes 3076
  221.3 3.9 %copy-start.57 = (f32[1,256]{1,0:T(1,128)S(1)}, f32[1,256]{1,0:T(1,128)}, u32[]{:S(2)}) copy-start(f32[1,256]{1,0:T(1,128)} %get-tuple-element.118) | copy-start | bytes 3076
  221.3 3.9 %copy-start.60 = (f32[256]{0:T(256)S(1)}, f32[256]{0:T(256)}, u32[]{:S(2)}) copy-start(f32[256]{0:T(256)} %param.64) | copy-start | bytes 3076
  221.3 5.3 %copy-start.56 = (f32[1,256]{1,0:T(1,128)S(1)}, f32[1,256]{1,0:T(1,128)}, u32[]{:S(2)}) copy-start(f32[1,256]{1,0:T(1,128)} %get-tuple-element.119) | copy-start | bytes 3076
  221.3 5.3 %copy-start.62 = (f32[256]{0:T(256)S(1)}, f32[256]{0:T(256)}, u32[]{:S(2)}) copy-start(f32[256]{0:T(256)} %param.62) | copy-start | bytes 3076
  221.3 5.2 %copy-start.63 = (f32[256]{0:T(256)S(1)}, f32[256]{0:T(256)}, u32[]{:S(2)}) copy-start(f32[256]{0:T(256)} %param.52) | copy-start | bytes 3076
  221.3 6.6 %copy-start.55 = (f32[1,256]{1,0:T(1,128)S(1)}, f32[1,256]{1,0:T(1,128)}, u32[]{:S(2)}) copy-start(f32[1,256]{1,0:T(1,128)} %get-tuple-element.120) | copy-start | bytes 3076
  221.3 6.6 %copy-start.64 = (f32[256]{0:T(256)S(1)}, f32[256]{0:T(256)}, u32[]{:S(2)}) copy-start(f32[256]{0:T(256)} %param.59) | copy-start | bytes 3076
  221.3 6.6 %copy-start.65 = (f32[256]{0:T(256)S(1)}, f32[256]{0:T(256)}, u32[]{:S(2)}) copy-start(f32[256]{0:T(256)} %param.49) | copy-start | bytes 3076
  221.3 7.9 %copy-start.66 = (f32[128]{0:T(128)S(1)}, f32[128]{0:T(128)}, u32[]{:S(2)}) copy-start(f32[128]{0:T(128)} %param.56) | copy-start | bytes 1540
  221.3 7.9 %copy-start.67 = (f32[128]{0:T(128)S(1)}, f32[128]{0:T(128)}, u32[]{:S(2)}) copy-start(f32[128]{0:T(128)} %param.46) | copy-start | bytes 1540
  221.4 9.1 %copy-start.17 = (f32[128,4096]{1,0:T(8,128)S(1)}, f32[128,4096]{1,0:T(8,128)}, u32[]{:S(2)}) copy-start(f32[128,4096]{1,0:T(8,128)} %mul.666) | copy-start | bytes 6291460
  221.4 9.1 %copy-start.26 = (f32[128,4096]{1,0:T(8,128)S(1)}, f32[128,4096]{1,0:T(8,128)}, u32[]{:S(2)}) copy-start(f32[128,4096]{1,0:T(8,128)} %param.57) | copy-start | bytes 6291460
  221.4 9.1 %copy-start.27 = (f32[128,4096]{1,0:T(8,128)S(1)}, f32[128,4096]{1,0:T(8,128)}, u32[]{:S(2)}) copy-start(f32[128,4096]{1,0:T(8,128)} %param.47) | copy-start | bytes 6291460
  (27 other events, 37.5 us)
Sparse Core Ops, SparseCore 0:
  10.8 31.7 all-gather.3
  44.2 29.2 all-gather.5

commit v2 on v1

--- a/solution.py
+++ b/solution.py
@@ -41,34 +41,6 @@
     docid = jnp.sum((positions[None, :] >= starts[:, None]).astype(jnp.int32), axis=0)
     first = jnp.sum((positions[None, :] == starts[:, None]).astype(jnp.int32), axis=0)
     return (docid, first > 0)
-
-
-def ends_kernel(ddec_ref, drive_ref, grady_ref, inb_ref, outb_ref, rates_ref, ends_ref, sums_ref):
-    groups, steps = ddec_ref.shape[:2]
-    columns = [pl.ds(group * LANES, LANES) for group in range(groups)]
-
-    def step(t, carry):
-        hidden, decayed, pulled = carry
-        in_row, out_row = inb_ref[t], outb_ref[t]
-        new = ([], [], [])
-        for group in range(groups):
-            here = (group, pl.ds(t, 1))
-            decay = jnp.exp2(ddec_ref[here] * rates_ref[:, columns[group]])
-            new[0].append(decay * hidden[group] + drive_ref[here] * in_row)
-            product = decay * decayed[group]
-            new[1].append(product)
-            new[2].append(pulled[group] + product * (grady_ref[here] * out_row))
-        return new
-
-    zeros = [jnp.zeros((N, LANES), jnp.float32) for _ in range(groups)]
-    ones = [jnp.ones((N, LANES), jnp.float32) for _ in range(groups)]
-    hidden, _, pulled = lax.fori_loop(0, steps, step, (zeros, ones, zeros), unroll=4)
-    for group in range(groups):
-        ends_ref[0, :, columns[group]] = hidden[group].astype(ends_ref.dtype)
-        ends_ref[1, :, columns[group]] = pulled[group].astype(ends_ref.dtype)
-        sums_ref[pl.ds(pl.program_id(0) * groups + group, 1), :] = jnp.sum(
-            ddec_ref[group], axis=0, keepdims=True
-        )
 
 
 def scan_kernel(
@@ -110,15 +82,15 @@
             factor = jnp.exp2(total * rates_ref[:, columns[group]])
             new.append(
                 factor * states[group]
-                + all_ref[device, :, columns[group]].astype(jnp.float32)
+                + all_ref[device, 0, :, columns[group]].astype(jnp.float32)
             )
         return new
 
     zeros = [jnp.zeros((N, LANES), jnp.float32) for _ in range(groups)]
-    entering = lax.fori_loop(0, member, through, zeros)
-    leaving = lax.fori_loop(
-        0, devices - 1 - member, lambda d, s: through(devices - 1 - d, s), zeros
-    )
+    reach = devices // 2
+    entering = lax.fori_loop(jnp.maximum(member - reach, 0), member, through, zeros)
+    last = jnp.minimum(member + reach, devices - 1)
+    leaving = lax.fori_loop(0, last - member, lambda d, s: through(last - d, s), zeros)
 
     def fold(values):
         return values[:half] + values[half:]
@@ -180,27 +152,6 @@
         grates_ref[:, columns[group]] = grates[group]
 
 
-def ends_of(ddec, drive, grady, inb, outb, rates, block):
-    steps = ddec.shape[1]
-    wide = pl.BlockSpec((block // LANES, steps, LANES), lambda b: (b, 0, 0))
-    whole = pl.BlockSpec((steps, N, LANES), lambda b: (0, 0, 0))
-    return pl.pallas_call(
-        ends_kernel,
-        grid=(E // block,),
-        in_specs=[wide, wide, wide, whole, whole, pl.BlockSpec((N, block), lambda b: (0, b))],
-        out_specs=[
-            pl.BlockSpec((2, N, block), lambda b: (0, 0, b)),
-            pl.BlockSpec((E // LANES, LANES), lambda b: (0, 0)),
-        ],
-        out_shape=[
-            jax.ShapeDtypeStruct((2, N, E), jnp.bfloat16),
-            jax.ShapeDtypeStruct((E // LANES, LANES), jnp.float32),
-        ],
-        compiler_params=pltpu.CompilerParams(vmem_limit_bytes=48 * 2**20),
-        name="ends",
-    )(ddec, drive, grady, inb, outb, rates)
-
-
 def scan_of(member, ddec, drive, grady, inb, outb, rates, everyone, sums, block):
     steps = ddec.shape[1]
     devices = everyone.shape[0]
@@ -221,7 +172,7 @@
             whole,
             whole,
             narrow,
-            pl.BlockSpec((devices, N, block), lambda b: (0, 0, b)),
+            pl.BlockSpec((devices, 1, N, block), lambda b: (0, b, 0, 0)),
             pl.BlockSpec(sums.shape, lambda b: (0, 0, 0)),
         ],
         out_specs=[wide, wide, wide, whole, whole, narrow],
@@ -266,40 +217,331 @@
     return copy
 
 
-def states_kernel(devices, ends_ref, sums_ref, ends_out, sums_out, wires, sum_wires):
+def span(index, size):
+    return pl.ds(index * size, size)
+
+
+def softplus(values):
+    return jnp.maximum(values, 0.0) + jnp.log1p(jnp.exp(-jnp.abs(values)))
+
+
+def front_kernel(
+    devices,
+    starts_ref,
+    tokens_ref,
+    cot_ref,
+    gain_ref,
+    in_proj_ref,
+    out_proj_ref,
+    conv_ref,
+    cbias_ref,
+    x_proj_ref,
+    dt_proj_ref,
+    dtbias_ref,
+    rates_ref,
+    normed_ref,
+    inner_ref,
+    gates_ref,
+    back_ref,
+    pre_act_ref,
+    delta_pre_ref,
+    ddec_ref,
+    drive_ref,
+    grady_ref,
+    rank_ref,
+    inb_ref,
+    outb_ref,
+    ends_out,
+    sums_out,
+    in_proj_buf,
+    out_proj_buf,
+    padded,
+    docid,
+    masks,
+    proj,
+    ends,
+    loads,
+    halo_wires,
+    wires,
+    sum_wires,
+):
     member = lax.axis_index("seq")
-    greet((("seq", devices),))
-    copies = []
+    steps = tokens_ref.shape[0]
+    groups = E // LANES
+    chunk = 4 * LANES
+    chunks = E // chunk
+    reach = devices // 2
+    halo = inner_ref.shape[0] - steps
+    in_loads = [
+        pltpu.make_async_copy(
+            in_proj_ref.at[:, span(at, chunk)], in_proj_buf.at[at], loads.at[at]
+        )
+        for at in range(2 * chunks)
+    ]
+    out_loads = [
+        pltpu.make_async_copy(
+            out_proj_ref.at[span(at, chunk), :], out_proj_buf.at[at], loads.at[2 * chunks + at]
+        )
+        for at in range(chunks)
+    ]
+    for load in in_loads + out_loads:
+        load.start()
+    barrier = pltpu.get_barrier_semaphore()
     for offset in range(1, devices):
-        wrapped = (member + offset) // devices
-        copies.append(
-            push(ends_ref.at[wrapped], ends_out.at[member], wires, offset - 1, "seq", offset)
-        )
-        copies.append(push(sums_ref, sums_out.at[member], sum_wires, offset - 1, "seq", offset))
-    ends_out[member] = ends_ref[0]
-    sums_out[member] = sums_ref[...]
-    for copy in copies:
-        copy.wait()
-
-
-def states_of(ends, sums, devices):
+        pl.semaphore_signal(
+            barrier, inc=1, device_id={"seq": partner("seq", offset)}, device_id_type=MESH
+        )
+
+    stream = tokens_ref[...].astype(jnp.float32)
+    inverse = lax.rsqrt(jnp.mean(stream * stream, axis=1, keepdims=True) + EPS)
+    normed_ref[...] = (stream * inverse * gain_ref[...]).astype(jnp.bfloat16)
+
+    places = member * steps - 8 + lax.broadcasted_iota(jnp.int32, docid.shape, 0)
+    count = jnp.zeros(docid.shape, jnp.int32)
+    first = jnp.zeros(docid.shape, jnp.float32)
+    for index in range(starts_ref.shape[0]):
+        count = count + jnp.where(places >= starts_ref[index], 1, 0)
+        first = jnp.where(places == starts_ref[index], 1.0, first)
+    docid[...] = count
+    masks[0] = first[8 : 8 + steps]
+    for offset in range(1, K):
+        masks[offset] = jnp.where(
+            docid[8 - offset : 8 - offset + steps, :] == docid[8 : 8 + steps, :], 1.0, 0.0
+        )
+
+    def project(at):
+        in_loads[at].wait()
+        return jnp.dot(
+            normed_ref[...], in_proj_buf[at], preferred_element_type=jnp.float32
+        ).astype(jnp.bfloat16)
+
+    for at in range(chunks):
+        inner_ref[halo:, span(at, chunk)] = project(at)
+    pl.semaphore_wait(barrier, devices - 1)
+    halo_copy = pltpu.make_async_remote_copy(
+        src_ref=inner_ref.at[steps : steps + halo, :],
+        dst_ref=inner_ref.at[0:halo, :],
+        send_sem=halo_wires.at[0],
+        recv_sem=halo_wires.at[1],
+        device_id={"seq": partner("seq", 1)},
+        device_id_type=MESH,
+    )
+
+    @pl.when(member < devices - 1)
+    def _():
+        halo_copy.start()
+
+    @pl.when(member == 0)
+    def _():
+        inner_ref[0:halo, :] = jnp.zeros((halo, E), jnp.bfloat16)
+
+    for at in range(chunks):
+        gates_ref[:, span(at, chunk)] = project(chunks + at)
+    for at in range(chunks):
+        out_loads[at].wait()
+        back_ref[:, span(at, chunk)] = lax.dot_general(
+            cot_ref[...],
+            out_proj_buf[at],
+            (((1,), (1,)), ((), ())),
+            preferred_element_type=jnp.float32,
+        ).astype(jnp.bfloat16)
+
+    @pl.when(member < devices - 1)
+    def _():
+        halo_copy.wait_send()
+
+    @pl.when(member > 0)
+    def _():
+        halo_copy.wait_recv()
+
+    proj[...] = jnp.zeros_like(proj)
+    for at in range(chunks):
+        lows = []
+        for group in range(4 * at, 4 * at + 4):
+            columns = span(group, LANES)
+            padded[...] = inner_ref[halo - 8 :, columns].astype(jnp.float32)
+            value = cbias_ref[:, columns] + conv_ref[0:1, columns] * padded[8:, :]
+            for offset in range(1, K):
+                value = (
+                    value
+                    + conv_ref[offset : offset + 1, columns]
+                    * padded[8 - offset : 8 - offset + steps, :]
+                    * masks[offset]
+                )
+            pre_act_ref[group] = value
+            act = silu(value)
+            drive_ref[group] = act
+            lows.append(act.astype(jnp.bfloat16))
+        proj[...] += jnp.dot(
+            jnp.concatenate(lows, axis=1),
+            x_proj_ref[span(at, chunk), :],
+            preferred_element_type=jnp.float32,
+        )
+    rank_ref[...] = proj[:, :R].astype(jnp.bfloat16)
+    inb_ref[...] = jnp.broadcast_to(proj[:, R : R + N][:, :, None], inb_ref.shape)
+    outb_ref[...] = jnp.broadcast_to(proj[:, R + N :][:, :, None], outb_ref.shape)
+
+    def later(distance, at):
+        return pltpu.make_async_remote_copy(
+            src_ref=ends.at[0, at],
+            dst_ref=ends_out.at[member, at],
+            send_sem=wires.at[0, 0, at, distance - 1],
+            recv_sem=wires.at[0, 1, at, distance - 1],
+            device_id={"seq": partner("seq", distance)},
+            device_id_type=MESH,
+        )
+
+    def earlier(distance, at):
+        return pltpu.make_async_remote_copy(
+            src_ref=ends.at[1, at],
+            dst_ref=ends_out.at[member, at],
+            send_sem=wires.at[1, 0, at, distance - 1],
+            recv_sem=wires.at[1, 1, at, distance - 1],
+            device_id={"seq": partner("seq", devices - distance)},
+            device_id_type=MESH,
+        )
+
+    def sums_to(distance, side):
+        offset = distance if side == 0 else devices - distance
+        return pltpu.make_async_remote_copy(
+            src_ref=sums_out.at[member],
+            dst_ref=sums_out.at[member],
+            send_sem=sum_wires.at[side, 0, distance - 1],
+            recv_sem=sum_wires.at[side, 1, distance - 1],
+            device_id={"seq": partner("seq", offset)},
+            device_id_type=MESH,
+        )
+
+    for at in range(chunks):
+        delta_pre = (
+            jnp.dot(
+                rank_ref[...], dt_proj_ref[:, span(at, chunk)], preferred_element_type=jnp.float32
+            )
+            + dtbias_ref[:, span(at, chunk)]
+        )
+        for place in range(4):
+            group = 4 * at + place
+            columns = span(group, LANES)
+            here = delta_pre[:, place * LANES : (place + 1) * LANES]
+            delta = softplus(here)
+            delta_pre_ref[group] = here
+            drive_ref[group] = drive_ref[group] * delta
+            ddec = jnp.where(masks[0] > 0.0, RESET, delta)
+            ddec_ref[group] = ddec
+            sums_out[member, group : group + 1, :] = jnp.sum(ddec, axis=0, keepdims=True)
+            grady_ref[group] = back_ref[:, columns].astype(jnp.float32) * silu(
+                gates_ref[:, columns].astype(jnp.float32)
+            )
+
+        def step(t, carry):
+            hidden, decayed, pulled = carry
+            in_row, out_row = inb_ref[t], outb_ref[t]
+            new = ([], [], [])
+            for place in range(4):
+                here = (4 * at + place, pl.ds(t, 1))
+                decay = jnp.exp2(ddec_ref[here] * rates_ref[:, span(4 * at + place, LANES)])
+                new[0].append(decay * hidden[place] + drive_ref[here] * in_row)
+                product = decay * decayed[place]
+                new[1].append(product)
+                new[2].append(pulled[place] + product * (grady_ref[here] * out_row))
+            return new
+
+        zeros = [jnp.zeros((N, LANES), jnp.float32) for _ in range(4)]
+        ones = [jnp.ones((N, LANES), jnp.float32) for _ in range(4)]
+        hidden, _, pulled = lax.fori_loop(0, steps, step, (zeros, ones, zeros), unroll=4)
+        ends[0, at] = jnp.concatenate(hidden, axis=1).astype(jnp.bfloat16)
+        ends[1, at] = jnp.concatenate(pulled, axis=1).astype(jnp.bfloat16)
+        for distance in range(1, reach + 1):
+
+            @pl.when(member + distance < devices)
+            def _():
+                later(distance, at).start()
+
+            @pl.when(member >= distance)
+            def _():
+                earlier(distance, at).start()
+
+    for distance in range(1, reach + 1):
+
+        @pl.when(member + distance < devices)
+        def _():
+            sums_to(distance, 0).start()
+
+        @pl.when(member >= distance)
+        def _():
+            sums_to(distance, 1).start()
+
+    for distance in range(1, reach + 1):
+
+        @pl.when(member + distance < devices)
+        def _():
+            for at in range(chunks):
+                later(distance, at).wait_send()
+                earlier(distance, at).wait_recv()
+            sums_to(distance, 0).wait_send()
+            sums_to(distance, 1).wait_recv()
+
+        @pl.when(member >= distance)
+        def _():
+            for at in range(chunks):
+                earlier(distance, at).wait_send()
+                later(distance, at).wait_recv()
+            sums_to(distance, 1).wait_send()
+            sums_to(distance, 0).wait_recv()
+
+
+def front_of(starts, tokens, cot, gain, in_proj, out_proj, conv, cbias, x_proj, dt_proj, dtbias, rates, devices):
+    steps = tokens.shape[0]
+    groups = E // LANES
+    chunk = 4 * LANES
+    chunks = E // chunk
+    reach = devices // 2
+    halo = 16
+    low = jnp.bfloat16
+    vmem = pl.BlockSpec(memory_space=pltpu.VMEM)
+    grouped = jax.ShapeDtypeStruct((groups, steps, LANES), jnp.float32)
+    spread = jax.ShapeDtypeStruct((steps, N, LANES), jnp.float32)
     return pl.pallas_call(
-        functools.partial(states_kernel, devices),
-        in_specs=[pl.BlockSpec(memory_space=pltpu.VMEM)] * 2,
-        out_specs=[pl.BlockSpec(memory_space=pltpu.VMEM)] * 2,
+        functools.partial(front_kernel, devices),
+        in_specs=[pl.BlockSpec(memory_space=pltpu.SMEM)]
+        + [vmem] * 3
+        + [pl.BlockSpec(memory_space=pl.ANY)] * 2
+        + [vmem] * 6,
+        out_specs=[vmem] * 14,
         out_shape=[
-            jax.ShapeDtypeStruct((devices,) + ends.shape[1:], ends.dtype),
-            jax.ShapeDtypeStruct((devices,) + sums.shape, sums.dtype),
+            jax.ShapeDtypeStruct((steps, D), low),
+            jax.ShapeDtypeStruct((steps + halo, E), low),
+            jax.ShapeDtypeStruct((steps, E), low),
+            jax.ShapeDtypeStruct((steps, E), low),
+            grouped,
+            grouped,
+            grouped,
+            grouped,
+            grouped,
+            jax.ShapeDtypeStruct((steps, R), low),
+            spread,
+            spread,
+            jax.ShapeDtypeStruct((devices, chunks, N, chunk), low),
+            jax.ShapeDtypeStruct((devices, groups, LANES), jnp.float32),
         ],
         scratch_shapes=[
-            pltpu.SemaphoreType.DMA((2, devices - 1)),
-            pltpu.SemaphoreType.DMA((2, devices - 1)),
+            pltpu.VMEM((2 * chunks, D, chunk), low),
+            pltpu.VMEM((chunks, chunk, D), low),
+            pltpu.VMEM((steps + 8, LANES), jnp.float32),
+            pltpu.VMEM((steps + 16, LANES), jnp.int32),
+            pltpu.VMEM((K, steps, LANES), jnp.float32),
+            pltpu.VMEM((steps, R + 2 * N), jnp.float32),
+            pltpu.VMEM((2, chunks, N, chunk), low),
+            pltpu.SemaphoreType.DMA((3 * chunks,)),
+            pltpu.SemaphoreType.DMA((2,)),
+            pltpu.SemaphoreType.DMA((2, 2, chunks, reach)),
+            pltpu.SemaphoreType.DMA((2, 2, reach)),
         ],
         compiler_params=pltpu.CompilerParams(
-            collective_id=0, has_side_effects=True, vmem_limit_bytes=48 * 2**20
+            collective_id=0, has_side_effects=True, vmem_limit_bytes=60 * 2**20
         ),
-        name="states",
-    )(ends, sums)
+        name="front",
+    )(starts, tokens, cot, gain, in_proj, out_proj, conv, cbias, x_proj, dt_proj, dtbias, rates)
 
 
 def trade_kernel(devices, gated_ref, back_ref, gated_out, back_out, wires, back_wires, local):
@@ -535,6 +777,123 @@
         ),
         name="grads",
     )(normed_all, back_mine, gated_mine, cot_all, small)
+
+
+PACKED = (R + 2 * N, R, N, K, 1, 1, 1, 1)
+PACKED_ROWS = 192
+
+
+def packed_rows():
+    spans = []
+    at = 0
+    for count in PACKED:
+        spans.append((at, at + count))
+        at += count
+    return spans
+
+
+def update_kernel(member_ref, norm_ref, gin_ref, gout_ref, small_ref, *refs):
+    weights, moments, averages, outs = refs[:10], refs[10:20], refs[20:30], refs[30:]
+    shrink_by = 1.0 / jnp.maximum(norm_ref[0:1, 0:1], 1.0)
+
+    def renew(ordinal, grad, at=Ellipsis):
+        clipped = grad * shrink_by
+        momentum_new = MOMENTUM * moments[ordinal][at] + clipped
+        renewed = weights[ordinal][at].astype(jnp.float32) - RATES[ordinal] * math.sqrt(PARAMS) * (
+            clipped + MOMENTUM * momentum_new
+        )
+        outs[3 * ordinal][at] = momentum_new
+        outs[3 * ordinal + 1][at] = renewed
+        outs[3 * ordinal + 2][at] = AVERAGE * averages[ordinal][at] + (1.0 - AVERAGE) * renewed
+
+    places, members = gin_ref.shape[:2]
+    for column in range(members):
+        for place in range(places):
+            columns = pl.ds((column * places + place) * LANES, LANES)
+            renew(1, gin_ref[place, column].astype(jnp.float32), (slice(None), columns))
+    renew(9, gout_ref[...].astype(jnp.float32))
+
+    @pl.when(pl.program_id(0) == 0)
+    def _():
+        spans = packed_rows()
+
+        def part(index):
+            return small_ref[spans[index][0] : spans[index][1], :].astype(jnp.float32)
+
+        small = small_ref[...].astype(jnp.float32)
+        renew(4, jnp.transpose(part(0)))
+        renew(5, part(1))
+        renew(7, part(2))
+        renew(2, part(3))
+        for ordinal, index in ((3, 4), (6, 5), (8, 6)):
+            renew(ordinal, small[spans[index][0] : spans[index][1]])
+        gain = small[spans[7][0] : spans[7][1], : weights[0].shape[1]]
+        renew(0, gain)
+
+
+def update_of(member, norm_tile, gin_parts, gout, small, weights, moments, averages):
+    nrows, devices, inner, wide = gin_parts.shape
+    channels = gout.shape[0]
+    blocks = 8
+    outer = channels // blocks
+    half = blocks // 2
+    pair = devices // half
+    block = nrows // 2 * pair * wide
+    flat = (0, 3, 6, 8)
+
+    def rows_of(array, ordinal):
+        return array.reshape(1, -1) if ordinal in flat else array
+
+    def shard(shape, ordinal):
+        if ordinal == 1:
+            return pl.BlockSpec((inner, block), lambda j, m: (0, j))
+        if ordinal == 9:
+            return pl.BlockSpec((outer, shape[1]), lambda j, m: (j, 0))
+        return pl.BlockSpec(shape, lambda j, m: (0, 0))
+
+    def weight(shape, ordinal):
+        if ordinal == 1:
+            return pl.BlockSpec((inner, block), lambda j, m: (m[0], j))
+        if ordinal == 9:
+            return pl.BlockSpec((outer, shape[1]), lambda j, m: (m[0] * blocks + j, 0))
+        if ordinal == 4:
+            return pl.BlockSpec(shape, lambda j, m: (m[0], 0))
+        return pl.BlockSpec(shape, lambda j, m: (0, m[0]))
+
+    weights = [rows_of(array, ordinal) for ordinal, array in enumerate(weights)]
+    moments = [rows_of(array, ordinal) for ordinal, array in enumerate(moments)]
+    averages = [rows_of(array, ordinal) for ordinal, array in enumerate(averages)]
+    shapes = [array.shape for array in moments]
+    shards = [shard(shape, ordinal) for ordinal, shape in enumerate(shapes)]
+    outs = pl.pallas_call(
+        update_kernel,
+        grid_spec=pltpu.PrefetchScalarGridSpec(
+            num_scalar_prefetch=1,
+            grid=(blocks,),
+            in_specs=[
+                pl.BlockSpec(norm_tile.shape, lambda j, m: (0, 0)),
+                pl.BlockSpec(
+                    (nrows // 2, pair, inner, wide), lambda j, m: (j // half, j % half, 0, 0)
+                ),
+                pl.BlockSpec((outer, gout.shape[1]), lambda j, m: (j, 0)),
+                pl.BlockSpec(small.shape, lambda j, m: (0, 0)),
+            ]
+            + [weight(shape, ordinal) for ordinal, shape in enumerate(shapes)]
+            + shards
+            + shards,
+            out_specs=[shards[ordinal] for ordinal in range(10) for _ in range(3)],
+        ),
+        out_shape=[
+            jax.ShapeDtypeStruct(shapes[ordinal], jnp.float32)
+            for ordinal in range(10)
+            for _ in range(3)
+        ],
+        compiler_params=pltpu.CompilerParams(vmem_limit_bytes=48 * 2**20),
+        name="update",
+    )(member, norm_tile, gin_parts, gout, small, *weights, *moments, *averages)
+    return [
+        out.reshape(-1) if index // 3 in flat else out for index, out in enumerate(outs)
+    ]
 
 
 def local(
@@ -581,63 +940,63 @@
     length = steps * devices
     cot_low = cotangent[0]
     inverse = lax.rsqrt(jnp.mean(stream * stream, axis=1, keepdims=True) + EPS)
-    normed = (stream * inverse * norm_gain[None, :]).astype(jnp.bfloat16)
+    rates = -jnp.exp(a_log)
+    scaled_rates = rates * (1.0 / math.log(2.0))
+    lengths = doc_lengths[0]
+    starts = (jnp.cumsum(lengths) - lengths).astype(jnp.int32)
+    (
+        normed,
+        inner_low,
+        gates_low,
+        back_gated,
+        pre_act,
+        delta_pre,
+        ddec,
+        drive,
+        grady_rows,
+        rank_low,
+        inb,
+        outb,
+        everyone,
+        all_sums,
+    ) = front_of(
+        starts,
+        tokens[0],
+        cot_low,
+        norm_gain[None],
+        in_proj,
+        out_proj,
+        conv_weight,
+        conv_bias[None],
+        x_proj,
+        dt_proj,
+        dt_bias[None],
+        scaled_rates,
+        devices,
+    )
     normed_all = lax.all_gather(normed, "seq", axis=0, tiled=True)
     cot_all = lax.all_gather(cot_low, "seq", axis=0, tiled=True)
-    xz = jnp.dot(normed, in_proj, preferred_element_type=jnp.float32).astype(jnp.bfloat16)
-    halo = lax.ppermute(
-        xz[steps - 8 :, :E], "seq", [(i, i + 1) for i in range(devices - 1)]
-    )
-    back_gated = lax.dot_general(
-        cot_low, out_proj, (((1,), (1,)), ((), ())), preferred_element_type=jnp.float32
-    ).astype(jnp.bfloat16)
     positions = member_id * steps + jnp.arange(-8, steps + 8, dtype=jnp.int32)
     docid, starting = doc_tables(doc_lengths[0], positions)
-    reset = starting[8 : 8 + steps, None]
     masks = []
     for offset in range(K):
         linked = (docid[8:] == docid[8 - offset : steps + 16 - offset]) & (
             positions[8 - offset : steps + 16 - offset] >= 0
         )
         masks.append((linked & (positions[8:] < length)).astype(jnp.float32)[:, None])
-    padded = jnp.concatenate([halo, xz[:, :E]], axis=0).astype(jnp.float32)
-    gates = xz[:, E:].astype(jnp.float32)
-    pre_act = jnp.broadcast_to(conv_bias[None, :], (steps, E))
-    for offset in range(K):
-        pre_act = (
-            pre_act
-            + conv_weight[offset][None, :]
-            * padded[8 - offset : 8 - offset + steps]
-            * masks[offset][:steps]
-        )
+
+    def flat(values):
+        return jnp.transpose(values, (1, 0, 2)).reshape(steps, E)
+
+    pre_act, delta_pre = flat(pre_act), flat(delta_pre)
+    padded = inner_low[8:].astype(jnp.float32)
+    gates = gates_low.astype(jnp.float32)
     act = silu(pre_act)
     act_low = act.astype(jnp.bfloat16)
-    proj = jnp.dot(act_low, x_proj, preferred_element_type=jnp.float32)
-    rank_low = proj[:, :R].astype(jnp.bfloat16)
-    in_mat = proj[:, R : R + N]
-    out_mat = proj[:, R + N :]
-    delta_pre = (
-        jnp.dot(rank_low, dt_proj, preferred_element_type=jnp.float32) + dt_bias[None, :]
-    )
     delta = jax.nn.softplus(delta_pre)
-    rates = -jnp.exp(a_log)
-    scaled_rates = rates * (1.0 / math.log(2.0))
-    ddec = jnp.where(reset, RESET, delta)
-    drive = delta * act
     silu_gate = silu(gates)
     chan_back = back_gated.astype(jnp.float32)
     grad_y = chan_back * silu_gate
-    inb = jnp.broadcast_to(in_mat[:, :, None], (steps, N, LANES))
-    outb = jnp.broadcast_to(out_mat[:, :, None], (steps, N, LANES))
-    def grouped(values):
-        return jnp.transpose(values.reshape(steps, E // LANES, LANES), (1, 0, 2))
-
-    def flat(values):
-        return jnp.transpose(values, (1, 0, 2)).reshape(steps, E)
-
-    ddec, drive, grady_rows = grouped(ddec), grouped(drive), grouped(grad_y)
-    ends, sums = ends_of(ddec, drive, grady_rows, inb, outb, scaled_rates, 512)
-    everyone, all_sums = states_of(ends, sums, devices)
     member_word = jnp.reshape(member_id, (1,)).astype(jnp.int32)
     scanned, along_in, pulled_sum, gin, gout, grad_rates = scan_of(
         member_word, ddec, drive, grady_rows, inb, outb, scaled_rates, everyone, all_sums, 512
@@ -714,19 +1073,17 @@
                 grad_gain.reshape(devices, D // devices),
                 ((0, 0), (0, channels - D // devices)),
             ).reshape(1, E),
-            jnp.zeros((8, E), jnp.float32),
+            jnp.zeros((PACKED_ROWS - sum(PACKED), E), jnp.float32),
         ],
         axis=0,
     )
     nrows = lax.axis_size("rows")
-    if channels % LANES == 0 and 2 * channels == nrows * LANES:
+    direct = channels % LANES == 0 and 2 * channels == nrows * LANES
+    if direct:
         gated_mine, back_mine = trade(gated, back_xz, devices)
         gin_parts, gout_share, small, norm_tile = grads_of(
             normed_all, back_mine, gated_mine, cot_all, small.astype(jnp.bfloat16), nrows, devices
         )
-        gin_share = jnp.transpose(
-            gin_parts.reshape(2, nrows // 2, devices, D // devices, LANES), (3, 0, 2, 1, 4)
-        ).reshape(D // devices, 2 * E)
         grad_norm = norm_tile[0, 0]
     else:
         gated_mine = lax.all_to_all(gated, "seq", split_axis=1, concat_axis=0, tiled=True)
@@ -748,12 +1105,49 @@
         small = lax.psum_scatter(small, "seq", scatter_dimension=1, tiled=True)
         squares = jnp.sum(gin_share * gin_share) + jnp.sum(gout_share * gout_share)
         grad_norm = jnp.sqrt(lax.psum(squares + jnp.sum(small * small), "seq"))
-    small = small.astype(jnp.float32)
-    parts = []
-    at = 0
-    for count in (R + 2 * N, R, N, K, 1, 1, 1, 1):
-        parts.append(small[at : at + count])
-        at += count
+    moments = (
+        moment_norm_gain,
+        moment_in_proj,
+        moment_conv_weight,
+        moment_conv_bias,
+        moment_x_proj,
+        moment_dt_proj,
+        moment_dt_bias,
+        moment_a_log,
+        moment_d_skip,
+        moment_out_proj,
+    )
+    averages = (
+        average_norm_gain,
+        average_in_proj,
+        average_conv_weight,
+        average_conv_bias,
+        average_x_proj,
+        average_dt_proj,
+        average_dt_bias,
+        average_a_log,
+        average_d_skip,
+        average_out_proj,
+    )
+    results = [block_output, input_grad[None], grad_norm]
+    if direct:
+        weights = (
+            norm_gain,
+            in_proj,
+            conv_weight,
+            conv_bias,
+            x_proj,
+            dt_proj,
+            dt_bias,
+            a_log,
+            d_skip,
+            out_proj,
+        )
+        results += update_of(
+            member_word, norm_tile, gin_parts, gout_share, small, weights, moments, averages
+        )
+        return tuple(results)
+    parts = [small[low:high] for low, high in packed_rows()]
     owner_grads = (
         parts[7][0, : D // devices],
         gin_share.astype(jnp.float32),
@@ -790,31 +1184,6 @@
             jnp.float32
         ),
     )
-    moments = (
-        moment_norm_gain,
-        moment_in_proj,
-        moment_conv_weight,
-        moment_conv_bias,
-        moment_x_proj,
-        moment_dt_proj,
-        moment_dt_bias,
-        moment_a_log,
-        moment_d_skip,
-        moment_out_proj,
-    )
-    averages = (
-        average_norm_gain,
-        average_in_proj,
-        average_conv_weight,
-        average_conv_bias,
-        average_x_proj,
-        average_dt_proj,
-        average_dt_bias,
-        average_a_log,
-        average_d_skip,
-        average_out_proj,
-    )
-    results = [block_output, input_grad[None], grad_norm]
     for ordinal in range(10):
         clipped = owner_grads[ordinal] * shrink_by
         momentum_new = MOMENTUM * moments[ordinal] + clipped

time: 243 us -> 231 us (0.951)
  other arithmetic: 34.5 us -> 18.7 us
  local copies, waits for them, and re-layouts: 18.7 us -> 28.6 us
  matrix products: 21.4 us -> 13.8 us
  Pallas kernels: 147 us -> 153 us
    add x10 -> x0, other arithmetic: 19.6 us -> none  [local(): AVERAGE * averages[ordinal] + (1.0 - AVERAGE) * renewed]
    pallas_call x2, Pallas kernels: 22.2 us -> 38.7 us  [the longest x1 29.1 us: front_of(): pl.pallas_call(functools.partial(front_kernel, devices), in_specs=[pl.Blo...]
    pallas_call x1, Pallas kernels: 40.2 us -> 28.4 us  [trade(): pl.pallas_call(functools.partial(trade_kernel, devices), in_specs=[pl.Blo...]
    unnamed x144 -> x139, local copies, waits for them, and re-layouts: 7.59 us -> 17.6 us
    dot_general x4 -> x0, matrix products: 9.39 us -> none  [the longest x1 4.78 us: local(): jnp.dot(normed, in_proj, preferred_element_type=jnp.float32)]
    mul x2 -> x0, local copies, waits for them, and re-layouts: 4.3 us -> none  [local(): clipped = owner_grads[ordinal] * shrink_by]
    squeeze x1, other arithmetic: 0.84 us -> 4.5 us  [local(): back_xz[1]]
    reduce_sum x1 -> x0, other arithmetic: 2.77 us -> none  [local(): grad_dskip = jnp.sum(grad_y * act, axis=0)]
  transfers between devices with their start and end apart: 4 -> 3, of which waited for: 0 -> 0; matrix products, arithmetic and copies ran while one was open for 15% -> 18% of each run, Pallas kernels for 34% -> 21%
where the time goes in v2:
time: 231 us; the launch traced here: 230 us
  Pallas kernels  153 us (66%)
  local copies, waits for them, and re-layouts  28.6 us (12%)
  other arithmetic  18.7 us (8%)
  between operations  14.8 us (6%)
  matrix products  13.8 us (6%)
    pallas_call x1, Pallas kernels, grads_of(): pl.pallas_call(functools.partial(grads_kernel, nrows, devices), in_specs=...  64.7 us
    pallas_call x1, Pallas kernels, front_of(): pl.pallas_call(functools.partial(front_kernel, devices), in_specs=[pl.Blo...  29.1 us
    pallas_call x1, Pallas kernels, trade(): pl.pallas_call(functools.partial(trade_kernel, devices), in_specs=[pl.Blo...  28.4 us
    pallas_call x1, Pallas kernels, scan_of(): pl.pallas_call(scan_kernel, grid=(E // block,), in_specs=[pl.BlockSpec(me...  21.1 us
    unnamed x139, local copies, waits for them, and re-layouts  17.6 us
    pallas_call x1, Pallas kernels, update_of(): pl.pallas_call(update_kernel, grid_spec=pltpu.PrefetchScalarGridSpec(num_...  9.61 us
    dot_general x1, matrix products, local(): lax.dot_general(back_xz[1], in_proj[:, E:], (((1,), (1,)), ((), ())), pre...  4.9 us
    concatenate x1, local copies, waits for them, and re-layouts, local(): jnp.concatenate([grad_xproj.T, grad_dtproj, grad_alog, grad_convw, grad_c...  4.89 us
  transfers between devices with their start and end apart: 3, of which 0 were waited for; matrix products, arithmetic and copies ran while one was open for 18% of the time, Pallas kernels for 21%

profile of v2, /device:TPU:0, one launch (start us, length us, event | category | flops | bytes accessed | tf_op | source)
XLA Modules:
  0.0 230.3 jit_solution(7978567190063809906)
XLA Ops:
  7.3 2.0 copy.92.x_proj_ref.refs_4_
  9.3 1.6 fusion.64.rates_ref
  11.6 29.1 %front.1 = (bf16[128,1024]{1,0:T(8,128)(2,1)}, bf16[144,2048]{1,0:T(8,128)(2,1)}, bf16[128,2048]{1,0:T(8,128)(2,1)}, bf16[128,2048]{1,0:T(8,128)(2,1)}, f32[16,1...) custom-call(s32[8]{0:T(128)} %bitcast_subtract_fusion.starts_ref, ...), custom_call_target="tpu_custom_call" | custom-call | tf_op jit(solution)/shard_map/front/pallas_call | solution.py:504
  40.7 1.0 copy-done.12
  41.8 0.8 copy-done.18
  42.6 21.1 %scan.1 = (f32[16,128,128]{2,1,0:T(8,128)S(1)}, f32[16,128,128]{2,1,0:T(8,128)S(1)}, f32[16,128,128]{2,1,0:T(8,128)S(1)}, f32[128,16,128]{2,1,0:T(8,128)S(1)}, f...) custom-call(s32[1]{0:T(128)} %bitcast.1.member_ref, f32[16,128,128]{2,1,0:T(8,128)} %get-tuple-element.89.ddec_ref, ...), custom_call_target="tpu_custom_call" | custom-call | tf_op jit(solution)/shard_map/scan/pallas_call | solution.py:164
  63.7 1.0 copy-done.5
  64.7 1.0 copy-done.6
  65.6 1.0 copy-done.7
  66.6 1.6 reduce_sum.118
  68.2 1.6 reduce_sum.119
  70.0 4.5 %fusion.12 = (bf16[128,2048]{1,0:T(8,128)(2,1)}, bf16[128,2048]{1,0:T(8,128)(2,1)S(1)}, bf16[2048]{0:T(1024)(128)(2,1)S(1)}, bf16[128,2048]{1,0:T(8,128)(2,1)S(1)}) fusion(bf16[128,2048]{1,0:T(8,128)(2,1)} %get-tuple-element.99, bf16[128,2048]{1,0:T(8,128)(2,1)} %get-tuple-element.98, f32[2048]{0:T(1024)S(1)} %copy-done.22, ...), kind=kLoop, calls=%fused_computation.24 | loop fusion | flops 8386560 | bytes 7876608 | tf_op jit(solution)/shard_map/squeeze | solution.py:1054
  74.9 1.4 fusion.4
  76.3 1.0 copy-done.37
  77.2 0.6 slice.123
  77.9 1.5 collective-permute-start
  79.4 2.9 %fusion.63 = bf16[16,128]{1,0:T(8,128)(2,1)} fusion(f32[16,128,128]{2,1,0:T(8,128)} %get-tuple-element.101, f32[16,128,128]{2,1,0:T(8,128)S(1)} %get-tuple-element.102, f32[16,128,128]{2,1,0:T(8,128)} %get-tuple-element.97, f32[16,128,128]{2,1,0:T(8,128)S(1)} %get-tuple-element.100), kind=kLoop, calls=%fused_computation.105 | loop fusion | flops 3405824 | bytes 4198400 | tf_op jit(solution)/shard_map/reduce_sum | solution.py:1017
  82.4 2.5 %convolution_convert_fusion = bf16[96,2048]{1,0:T(8,128)(2,1)} fusion(bf16[128,16]{0,1:T(8,128)(2,1)S(1)} %copy.99, bf16[128,16]{0,1:T(8,128)(2,1)S(1)} %copy.98, bf16[128,64]{0,1:T(8,128)(2,1)S(1)} %convolution_convert_fusion.2, f32[16,128,128]{2,1,0:T(8,128)} %get-tuple-element.97), kind=kOutput, calls=%fused_computation.7 | convolution fusion | flops 51912704 | bytes 1466368 | tf_op jit(solution)/shard_map/dot_general | solution.py:1025
  85.0 1.0 convolution_convert_fusion.1
  86.0 4.9 %fusion = f32[128,1024]{1,0:T(8,128)} fusion(bf16[128,2048]{1,0:T(8,128)(2,1)S(1)} %copy-done.47, bf16[1024,4096]{1,0:T(8,128)(2,1)} %refs_1_.1), kind=kOutput, calls=%fused_computation | convolution fusion | flops 536870912 | bytes 5242880 | tf_op jit(solution)/shard_map/dot_general | solution.py:1053
  91.0 1.5 fusion.5
  92.5 0.6 and_convert_fusion.2
  93.9 0.6 copy.137
  95.1 0.6 broadcast_in_dim.50
  95.8 1.0 copy.102.refs_24_
  96.8 1.1 fusion.51
  98.0 0.7 fusion.34
  98.7 0.6 broadcast_in_dim.48
  99.3 0.6 stack.31
  99.9 0.6 stack.32
  101.1 0.6 stack.34
  102.9 2.2 fusion.61
  105.1 0.6 copy.112
  105.8 28.4 %trade.1 = (bf16[1024,256]{1,0:T(8,128)(2,1)S(1)}, bf16[2,1024,256]{2,1,0:T(8,128)(2,1)S(1)}) custom-call(bf16[128,2048]{1,0:T(8,128)(2,1)S(1)} %get-tuple-element.254.gated_ref, bf16[2,128,2048]{2,1,0:T(8,128)(2,1)S(1)} %pad_maximum_fusion.1.back_ref), custom_call_target="tpu_custom_call" | custom-call | tf_op jit(solution)/shard_map/trade/pallas_call | solution.py:587
  134.2 0.8 copy-done.11
  135.0 4.9 %concatenate.13.small_ref = bf16[192,2048]{1,0:T(8,128)(2,1)} concatenate(bf16[96,2048]{1,0:T(8,128)(2,1)S(1)} %copy-done.54, bf16[64,2048]{1,0:T(8,128)(2,1)S(1)} %copy-done.49, bf16[16,2048]{1,0:T(8,128)(2,1)S(1)} %multiply_convert_fusion.1, bf16[1,2048]{1,0:T(2,128)(2,1)} %stack.31, bf16[1,2048]{1,0:T(2,128)(2,1)} %stack.32, bf16[1,2048]{1,0:T(2,128)(2,1)} %stack.33, ...), dimensions={0} | concatenate | bytes 1572864 | tf_op jit(solution)/shard_map/concatenate | solution.py:1063
  139.9 0.7 broadcast_multiply_fusion
  140.6 1.0 fusion.58
  141.8 64.7 %grads.1 = (bf16[4,8,128,128]{3,2,1,0:T(8,128)(2,1)}, bf16[256,1024]{1,0:T(8,128)(2,1)}, bf16[192,256]{1,0:T(8,128)(2,1)}, f32[8,128]{1,0:T(8,128)}) custom-call(bf16[1024,1024]{1,0:T(8,128)(2,1)} %all-gather.4.cloned.1.call-done.normed_ref, bf16[2,1024,256]{2,1,0:T(8,128)(2,1)} %copy-done.4, bf16[1024,256]{1,0:T(8,128)(2,1)} %copy-done.11, ...), custom_call_target="tpu_custom_call" | custom-call | tf_op jit(solution)/shard_map/grads/pallas_call | solution.py:749
  206.5 1.2 slice.122
  207.9 1.2 copy-done.10
  209.1 1.0 copy-done.13
  210.1 0.9 copy-done.15
  211.0 0.7 copy-done.27
  211.7 9.6 %update.1 = (f32[1,128]{1,0:T(1,128)}, f32[1,128]{1,0:T(1,128)}, f32[1,128]{1,0:T(1,128)}, f32[128,4096]{1,0:T(8,128)}, f32[128,4096]{1,0:T(8,128)}, /*index=5*/...) custom-call(s32[1]{0:T(128)} %bitcast.1.member_ref, ...), custom_call_target="tpu_custom_call" | custom-call | tf_op jit(solution)/shard_map/update/pallas_call | solution.py:868
  221.3 0.7 copy.103
  222.0 0.7 copy.104
  222.8 0.7 copy.105
  (147 shorter events, 4.9 us)
Async XLA Ops:
  7.2 3.6 %copy-start.61 = (s32[1,8]{1,0:T(1,128)S(1)}, s32[1,8]{1,0:T(1,128)}, u32[]{:S(2)}) copy-start(s32[1,8]{1,0:T(1,128)} %param.35) | copy-start | bytes 100
  7.2 134.4 %all-gather.4.cloned.1.call-start = ((), (), s32[]{:S(2)}) async-start(), calls=%async_computation | async-start | bytes 2359296 | tf_op jit(solution)/shard_map/all_gather | solution.py:977
  11.6 29.2 %copy-start.3 = (f32[16,2048]{1,0:T(8,128)S(1)}, f32[16,2048]{1,0:T(8,128)}, u32[]{:S(2)}) copy-start(f32[16,2048]{1,0:T(8,128)} %fusion.64.rates_ref) | copy-start | bytes 393220
  40.7 100.9 %all-gather.6.cloned.1.call-start = ((), (), s32[]{:S(2)}) async-start(), calls=%async_computation.1 | async-start | bytes 2359296 | tf_op jit(solution)/shard_map/all_gather | solution.py:978
  66.6 3.3 %copy-start.22 = (f32[2048]{0:T(1024)S(1)}, f32[2048]{0:T(1024)}, u32[]{:S(2)}) copy-start(f32[2048]{0:T(1024)} %param.44) | copy-start | bytes 24580
  69.9 4.6 %copy-start.1 = (bf16[64,2048]{1,0:T(8,128)(2,1)S(1)}, bf16[64,2048]{1,0:T(8,128)(2,1)}, u32[]{:S(2)}) copy-start(bf16[64,2048]{1,0:T(8,128)(2,1)} %refs_5_.1) | copy-start | bytes 786436
  69.9 4.9 %copy-start.41 = (f32[16,128,128]{2,1,0:T(8,128)S(1)}, f32[16,128,128]{2,1,0:T(8,128)}, u32[]{:S(2)}) copy-start(f32[16,128,128]{2,1,0:T(8,128)} %get-tuple-element.97) | copy-start | bytes 3145732
  69.9 4.9 %copy-start.42 = (f32[16,128,128]{2,1,0:T(8,128)S(1)}, f32[16,128,128]{2,1,0:T(8,128)}, u32[]{:S(2)}) copy-start(f32[16,128,128]{2,1,0:T(8,128)} %get-tuple-element.101) | copy-start | bytes 3145732
  70.0 4.9 %copy-start.51 = (bf16[128,2048]{1,0:T(8,128)(2,1)S(1)}, bf16[128,2048]{1,0:T(8,128)(2,1)}, u32[]{:S(2)}) copy-start(bf16[128,2048]{1,0:T(8,128)(2,1)} %get-tuple-element.98) | copy-start | bytes 1572868
  70.0 4.9 %copy-start.52 = (bf16[128,2048]{1,0:T(8,128)(2,1)S(1)}, bf16[128,2048]{1,0:T(8,128)(2,1)}, u32[]{:S(2)}) copy-start(bf16[128,2048]{1,0:T(8,128)(2,1)} %get-tuple-element.99) | copy-start | bytes 1572868
  70.0 4.9 %copy-start.53 = (bf16[2048,96]{0,1:T(8,128)(2,1)S(1)}, bf16[2048,96]{0,1:T(8,128)(2,1)}, u32[]{:S(2)}) copy-start(bf16[2048,96]{0,1:T(8,128)(2,1)} %param.40) | copy-start | bytes 1179652
  77.9 18.9 %collective-permute-start = (f32[8,2048]{1,0:T(8,128)}, f32[8,2048]{1,0:T(8,128)S(1)}, u32[]{:S(2)}, u32[]{:S(2)}) collective-permute-start(f32[8,2048]{1,0:T(8,128)} %slice.123), channel_id=1, source_target_pairs={{1,0},{2,1},{3,2},{4,3},{5,4},{6,5},{7,6},{9,8},{10,9},{11,10},{12... | collective-permute-start | bytes 196616 | tf_op jit(solution)/shard_map/ppermute | solution.py:1036
  79.4 2.9 %copy-start.59 = (s32[8]{0:T(128)S(1)}, s32[8]{0:T(128)}, u32[]{:S(2)}) copy-start(s32[8]{0:T(128)} %bitcast_subtract_fusion.starts_ref) | copy-start | bytes 100
  82.4 2.6 %copy-start.40 = (bf16[128,2048]{1,0:T(8,128)(2,1)S(1)}, bf16[128,2048]{1,0:T(8,128)(2,1)}, u32[]{:S(2)}) copy-start(bf16[128,2048]{1,0:T(8,128)(2,1)} %copy-done.39) | copy-start | bytes 1572868
  82.4 2.6 %copy-start.56 = (bf16[128,64]{1,0:T(8,128)(2,1)S(1)}, bf16[128,64]{1,0:T(8,128)(2,1)}, u32[]{:S(2)}) copy-start(bf16[128,64]{1,0:T(8,128)(2,1)} %get-tuple-element.108) | copy-start | bytes 49156
  82.4 3.6 %copy-start.47 = (bf16[128,2048]{1,0:T(8,128)(2,1)S(1)}, bf16[128,2048]{1,0:T(8,128)(2,1)}, u32[]{:S(2)}) copy-start(bf16[128,2048]{1,0:T(8,128)(2,1)} %get-tuple-element.253) | copy-start | bytes 1572868
  86.0 4.9 %copy-start.2 = (f32[16,2048]{1,0:T(8,128)S(1)}, f32[16,2048]{1,0:T(8,128)}, u32[]{:S(2)}) copy-start(f32[16,2048]{1,0:T(8,128)} %refs_7_.1) | copy-start | bytes 393220
  86.0 4.9 %copy-start.36 = (bf16[2048,1024]{1,0:T(8,128)(2,1)S(1)}, bf16[2048,1024]{1,0:T(8,128)(2,1)}, u32[]{:S(2)}) copy-start(bf16[2048,1024]{1,0:T(8,128)(2,1)} %refs_9_.1) | copy-start | bytes 12582916
  86.0 5.0 %copy-start.43 = (bf16[1,128,1024]{2,1,0:T(8,128)(2,1)S(1)}, bf16[1,128,1024]{2,1,0:T(8,128)(2,1)}, u32[]{:S(2)}) copy-start(bf16[1,128,1024]{2,1,0:T(8,128)(2,1)} %param.33) | copy-start | bytes 786436
  92.5 3.2 %copy-start.55 = (f32[256,96]{0,1:T(8,128)S(1)}, f32[256,96]{0,1:T(8,128)}, u32[]{:S(2)}) copy-start(f32[256,96]{0,1:T(8,128)} %param.50) | copy-start | bytes 294916
  93.3 3.5 %copy-start.38 = (f32[128,2048]{1,0:T(8,128)S(1)}, f32[128,2048]{1,0:T(8,128)}, u32[]{:S(2)}) copy-start(f32[128,2048]{1,0:T(8,128)} %copy-done.37) | copy-start | bytes 3145732
  96.8 5.5 %slice-start = ((s8[8388608]{0:T(1024)(128)(4,1)}), s8[4194304]{0:T(1024)(128)(4,1)S(1)}, s32[]{:S(2)}) async-start(s8[8388608]{0:T(1024)(128)(4,1)} %bitcast.225), calls=%async_computation.2 | async-start | bytes 8388608
  98.0 4.4 %slice-start.1 = ((s8[8388608]{0:T(1024)(128)(4,1)}), s8[4194304]{0:T(1024)(128)(4,1)S(1)}, s32[]{:S(2)}) async-start(s8[8388608]{0:T(1024)(128)(4,1)} %bitcast.225), calls=%async_computation.3 | async-start | bytes 8388608
  102.9 2.8 %copy-start.48 = (bf16[128,2048]{1,0:T(8,128)(2,1)S(1)}, bf16[128,2048]{1,0:T(8,128)(2,1)}, u32[]{:S(2)}) copy-start(bf16[128,2048]{1,0:T(8,128)(2,1)} %get-tuple-element.253) | copy-start | bytes 1572868
  105.8 29.2 %copy-start.49 = (bf16[64,2048]{1,0:T(8,128)(2,1)S(1)}, bf16[64,2048]{1,0:T(8,128)(2,1)}, u32[]{:S(2)}) copy-start(bf16[64,2048]{1,0:T(8,128)(2,1)} %convolution_convert_fusion.1) | copy-start | bytes 786436
  105.8 29.2 %copy-start.54 = (bf16[96,2048]{1,0:T(8,128)(2,1)S(1)}, bf16[96,2048]{1,0:T(8,128)(2,1)}, u32[]{:S(2)}) copy-start(bf16[96,2048]{1,0:T(8,128)(2,1)} %convolution_convert_fusion) | copy-start | bytes 1179652
  135.0 6.6 %copy-start.4 = (bf16[2,1024,256]{2,1,0:T(8,128)(2,1)}, bf16[2,1024,256]{2,1,0:T(8,128)(2,1)S(1)}, u32[]{:S(2)}) copy-start(bf16[2,1024,256]{2,1,0:T(8,128)(2,1)S(1)} %get-tuple-element.106.back_ref) | copy-start | bytes 3145732
  135.0 5.6 %copy-start.45 = (bf16[1,128,1024]{2,1,0:T(8,128)(2,1)S(1)}, bf16[1,128,1024]{2,1,0:T(8,128)(2,1)}, u32[]{:S(2)}) copy-start(bf16[1,128,1024]{2,1,0:T(8,128)(2,1)} %param.33) | copy-start | bytes 786436
  135.0 5.6 %copy-start.46 = (bf16[1,128,1024]{2,1,0:T(8,128)(2,1)S(1)}, bf16[1,128,1024]{2,1,0:T(8,128)(2,1)}, u32[]{:S(2)}) copy-start(bf16[1,128,1024]{2,1,0:T(8,128)(2,1)} %param.34) | copy-start | bytes 786436
  141.6 66.1 %copy-start = (bf16[2048,96]{1,0:T(8,128)(2,1)S(1)}, bf16[2048,96]{1,0:T(8,128)(2,1)}, u32[]{:S(2)}) copy-start(bf16[2048,96]{1,0:T(8,128)(2,1)} %copy.92.x_proj_ref.refs_4_) | copy-start | bytes 1179652
  141.6 66.1 %copy-start.8 = (f32[256,1024]{1,0:T(8,128)S(1)}, f32[256,1024]{1,0:T(8,128)}, u32[]{:S(2)}) copy-start(f32[256,1024]{1,0:T(8,128)} %refs_19_.1) | copy-start | bytes 3145732
  141.6 66.1 %copy-start.9 = (f32[256,1024]{1,0:T(8,128)S(1)}, f32[256,1024]{1,0:T(8,128)}, u32[]{:S(2)}) copy-start(f32[256,1024]{1,0:T(8,128)} %refs_29_.1) | copy-start | bytes 3145732
  141.6 66.1 %copy-start.16 = (f32[64,256]{1,0:T(8,128)S(1)}, f32[64,256]{1,0:T(8,128)}, u32[]{:S(2)}) copy-start(f32[64,256]{1,0:T(8,128)} %refs_15_.1) | copy-start | bytes 196612
  141.6 66.1 %copy-start.17 = (f32[64,256]{1,0:T(8,128)S(1)}, f32[64,256]{1,0:T(8,128)}, u32[]{:S(2)}) copy-start(f32[64,256]{1,0:T(8,128)} %refs_25_.1) | copy-start | bytes 196612
  141.7 66.1 %copy-start.20 = (f32[2048]{0:T(1024)S(1)}, f32[2048]{0:T(1024)}, u32[]{:S(2)}) copy-start(f32[2048]{0:T(1024)} %param.39) | copy-start | bytes 24580
  141.7 66.1 %copy-start.21 = (f32[2048]{0:T(1024)S(1)}, f32[2048]{0:T(1024)}, u32[]{:S(2)}) copy-start(f32[2048]{0:T(1024)} %param.42) | copy-start | bytes 24580
  141.7 66.1 %copy-start.23 = (f32[16,256]{1,0:T(8,128)S(1)}, f32[16,256]{1,0:T(8,128)}, u32[]{:S(2)}) copy-start(f32[16,256]{1,0:T(8,128)} %refs_17_.1) | copy-start | bytes 49156
  141.7 66.1 %copy-start.24 = (f32[16,256]{1,0:T(8,128)S(1)}, f32[16,256]{1,0:T(8,128)}, u32[]{:S(2)}) copy-start(f32[16,256]{1,0:T(8,128)} %refs_27_.1) | copy-start | bytes 49156
  141.7 66.1 %copy-start.25 = (f32[4,256]{1,0:T(4,128)S(1)}, f32[4,256]{1,0:T(4,128)}, u32[]{:S(2)}) copy-start(f32[4,256]{1,0:T(4,128)} %refs_12_.1) | copy-start | bytes 12292
  141.7 66.1 %copy-start.26 = (f32[4,256]{1,0:T(4,128)S(1)}, f32[4,256]{1,0:T(4,128)}, u32[]{:S(2)}) copy-start(f32[4,256]{1,0:T(4,128)} %refs_22_.1) | copy-start | bytes 12292
  141.7 66.1 %copy-start.28 = (f32[256]{0:T(256)S(1)}, f32[256]{0:T(256)}, u32[]{:S(2)}) copy-start(f32[256]{0:T(256)} %param.49) | copy-start | bytes 3076
  141.7 66.0 %copy-start.29 = (f32[256]{0:T(256)S(1)}, f32[256]{0:T(256)}, u32[]{:S(2)}) copy-start(f32[256]{0:T(256)} %param.52) | copy-start | bytes 3076
  141.7 66.0 %copy-start.30 = (f32[256]{0:T(256)S(1)}, f32[256]{0:T(256)}, u32[]{:S(2)}) copy-start(f32[256]{0:T(256)} %param.54) | copy-start | bytes 3076
  141.8 66.0 %copy-start.31 = (f32[256]{0:T(256)S(1)}, f32[256]{0:T(256)}, u32[]{:S(2)}) copy-start(f32[256]{0:T(256)} %param.59) | copy-start | bytes 3076
  141.8 66.0 %copy-start.32 = (f32[256]{0:T(256)S(1)}, f32[256]{0:T(256)}, u32[]{:S(2)}) copy-start(f32[256]{0:T(256)} %param.62) | copy-start | bytes 3076
  141.8 66.0 %copy-start.33 = (f32[256]{0:T(256)S(1)}, f32[256]{0:T(256)}, u32[]{:S(2)}) copy-start(f32[256]{0:T(256)} %param.64) | copy-start | bytes 3076
  141.8 66.0 %copy-start.34 = (f32[128]{0:T(128)S(1)}, f32[128]{0:T(128)}, u32[]{:S(2)}) copy-start(f32[128]{0:T(128)} %param.46) | copy-start | bytes 1540
  141.8 66.0 %copy-start.35 = (f32[128]{0:T(128)S(1)}, f32[128]{0:T(128)}, u32[]{:S(2)}) copy-start(f32[128]{0:T(128)} %param.56) | copy-start | bytes 1540
  (20 other events, 23.4 us)
Sparse Core Ops, SparseCore 0:
  40.8 28.0 all-gather.3
  79.5 28.9 all-gather.5

commit v3 on v2

--- a/solution.py
+++ b/solution.py
@@ -227,6 +227,7 @@
 
 def front_kernel(
     devices,
+    nrows,
     starts_ref,
     tokens_ref,
     cot_ref,
@@ -264,8 +265,10 @@
     halo_wires,
     wires,
     sum_wires,
+    row_wires,
 ):
     member = lax.axis_index("seq")
+    own = lax.axis_index("rows") if nrows > 1 else 0
     steps = tokens_ref.shape[0]
     groups = E // LANES
     chunk = 4 * LANES
@@ -287,14 +290,15 @@
     for load in in_loads + out_loads:
         load.start()
     barrier = pltpu.get_barrier_semaphore()
-    for offset in range(1, devices):
-        pl.semaphore_signal(
-            barrier, inc=1, device_id={"seq": partner("seq", offset)}, device_id_type=MESH
-        )
+    for axis, count in (("seq", devices), ("rows", nrows)):
+        for offset in range(1, count):
+            pl.semaphore_signal(
+                barrier, inc=1, device_id={axis: partner(axis, offset)}, device_id_type=MESH
+            )
 
     stream = tokens_ref[...].astype(jnp.float32)
     inverse = lax.rsqrt(jnp.mean(stream * stream, axis=1, keepdims=True) + EPS)
-    normed_ref[...] = (stream * inverse * gain_ref[...]).astype(jnp.bfloat16)
+    normed_ref[own] = (stream * inverse * gain_ref[...]).astype(jnp.bfloat16)
 
     places = member * steps - 8 + lax.broadcasted_iota(jnp.int32, docid.shape, 0)
     count = jnp.zeros(docid.shape, jnp.int32)
@@ -312,12 +316,12 @@
     def project(at):
         in_loads[at].wait()
         return jnp.dot(
-            normed_ref[...], in_proj_buf[at], preferred_element_type=jnp.float32
+            normed_ref[own], in_proj_buf[at], preferred_element_type=jnp.float32
         ).astype(jnp.bfloat16)
 
     for at in range(chunks):
         inner_ref[halo:, span(at, chunk)] = project(at)
-    pl.semaphore_wait(barrier, devices - 1)
+    pl.semaphore_wait(barrier, devices + nrows - 2)
     halo_copy = pltpu.make_async_remote_copy(
         src_ref=inner_ref.at[steps : steps + halo, :],
         dst_ref=inner_ref.at[0:halo, :],
@@ -330,6 +334,11 @@
     @pl.when(member < devices - 1)
     def _():
         halo_copy.start()
+
+    row_copies = [
+        push(normed_ref.at[own], normed_ref.at[own], row_wires, offset - 1, "rows", offset)
+        for offset in range(1, nrows)
+    ]
 
     @pl.when(member == 0)
     def _():
@@ -372,9 +381,10 @@
             act = silu(value)
             drive_ref[group] = act
             lows.append(act.astype(jnp.bfloat16))
-        proj[...] += jnp.dot(
+        proj[...] += lax.dot_general(
             jnp.concatenate(lows, axis=1),
-            x_proj_ref[span(at, chunk), :],
+            x_proj_ref[:, span(at, chunk)],
+            (((1,), (1,)), ((), ())),
             preferred_element_type=jnp.float32,
         )
     rank_ref[...] = proj[:, :R].astype(jnp.bfloat16)
@@ -488,9 +498,11 @@
                 later(distance, at).wait_recv()
             sums_to(distance, 1).wait_send()
             sums_to(distance, 0).wait_recv()
-
-
-def front_of(starts, tokens, cot, gain, in_proj, out_proj, conv, cbias, x_proj, dt_proj, dtbias, rates, devices):
+    for copy in row_copies:
+        copy.wait()
+
+
+def front_of(starts, tokens, cot, gain, in_proj, out_proj, conv, cbias, x_proj, dt_proj, dtbias, rates, devices, nrows):
     steps = tokens.shape[0]
     groups = E // LANES
     chunk = 4 * LANES
@@ -502,14 +514,14 @@
     grouped = jax.ShapeDtypeStruct((groups, steps, LANES), jnp.float32)
     spread = jax.ShapeDtypeStruct((steps, N, LANES), jnp.float32)
     return pl.pallas_call(
-        functools.partial(front_kernel, devices),
+        functools.partial(front_kernel, devices, nrows),
         in_specs=[pl.BlockSpec(memory_space=pltpu.SMEM)]
         + [vmem] * 3
         + [pl.BlockSpec(memory_space=pl.ANY)] * 2
         + [vmem] * 6,
         out_specs=[vmem] * 14,
         out_shape=[
-            jax.ShapeDtypeStruct((steps, D), low),
+            jax.ShapeDtypeStruct((nrows, steps, D), low),
             jax.ShapeDtypeStruct((steps + halo, E), low),
             jax.ShapeDtypeStruct((steps, E), low),
             jax.ShapeDtypeStruct((steps, E), low),
@@ -536,247 +548,13 @@
             pltpu.SemaphoreType.DMA((2,)),
             pltpu.SemaphoreType.DMA((2, 2, chunks, reach)),
             pltpu.SemaphoreType.DMA((2, 2, reach)),
+            pltpu.SemaphoreType.DMA((2, max(nrows - 1, 1))),
         ],
         compiler_params=pltpu.CompilerParams(
             collective_id=0, has_side_effects=True, vmem_limit_bytes=60 * 2**20
         ),
         name="front",
     )(starts, tokens, cot, gain, in_proj, out_proj, conv, cbias, x_proj, dt_proj, dtbias, rates)
-
-
-def trade_kernel(devices, gated_ref, back_ref, gated_out, back_out, wires, back_wires, local):
-    member = lax.axis_index("seq")
-    steps = gated_ref.shape[0]
-    channels = gated_ref.shape[1] // devices
-    rows = pl.ds(pl.multiple_of(member * steps, steps), steps)
-    greet((("seq", devices),))
-    copies = []
-    for offset in range(1, devices):
-        columns = pl.ds(pl.multiple_of(partner("seq", offset) * channels, channels), channels)
-        copies.append(
-            push(
-                back_ref.at[:, :, columns],
-                back_out.at[:, rows, :],
-                back_wires,
-                offset - 1,
-                "seq",
-                offset,
-            )
-        )
-        copies.append(
-            push(
-                gated_ref.at[:, columns], gated_out.at[rows, :], wires, offset - 1, "seq", offset
-            )
-        )
-    columns = pl.ds(pl.multiple_of(member * channels, channels), channels)
-    own = pltpu.make_async_copy(back_ref.at[:, :, columns], back_out.at[:, rows, :], local.at[0])
-    own_gated = pltpu.make_async_copy(
-        gated_ref.at[:, columns], gated_out.at[rows, :], local.at[1]
-    )
-    own.start()
-    own_gated.start()
-    own.wait()
-    own_gated.wait()
-    for copy in copies:
-        copy.wait()
-
-
-def trade(gated, back, devices):
-    steps = gated.shape[0]
-    channels = gated.shape[1] // devices
-    return pl.pallas_call(
-        functools.partial(trade_kernel, devices),
-        in_specs=[pl.BlockSpec(memory_space=pltpu.VMEM)] * 2,
-        out_specs=[pl.BlockSpec(memory_space=pltpu.VMEM)] * 2,
-        out_shape=[
-            jax.ShapeDtypeStruct((steps * devices, channels), gated.dtype),
-            jax.ShapeDtypeStruct((2, steps * devices, channels), back.dtype),
-        ],
-        scratch_shapes=[
-            pltpu.SemaphoreType.DMA((2, devices - 1)),
-            pltpu.SemaphoreType.DMA((2, devices - 1)),
-            pltpu.SemaphoreType.DMA((2,)),
-        ],
-        compiler_params=pltpu.CompilerParams(
-            collective_id=1, has_side_effects=True, vmem_limit_bytes=48 * 2**20
-        ),
-        name="trade",
-    )(gated, back)
-
-
-def grads_kernel(
-    nrows,
-    devices,
-    normed_ref,
-    back_ref,
-    gated_ref,
-    cot_ref,
-    small_ref,
-    gin_out,
-    gout_out,
-    small_out,
-    norm_out,
-    small_got,
-    small_part,
-    small_seq,
-    gout_sum,
-    gout_low,
-    gout_got,
-    gin_sum,
-    gin_low,
-    gin_got,
-    gin_part,
-    norm_seq,
-    norm_rows,
-    row_wires,
-    seq_wires,
-):
-    row = lax.axis_index("rows")
-    member = lax.axis_index("seq")
-    few = small_ref.shape[0] // nrows
-    outer = gout_out.shape[0] // nrows
-    inner = gin_part.shape[0] // devices
-    channels = small_out.shape[1]
-    greet((("rows", nrows), ("seq", devices)))
-
-    def share(index, size):
-        return pl.ds(pl.multiple_of(index * size, size), size)
-
-    def to_rows(kind, make):
-        return [
-            push(*make(partner("rows", offset), offset - 1), row_wires.at[kind], offset - 1, "rows", offset)
-            for offset in range(1, nrows)
-        ]
-
-    def to_seq(kind, make):
-        return [
-            push(*make(partner("seq", offset), offset - 1), seq_wires.at[kind], offset - 1, "seq", offset)
-            for offset in range(1, devices)
-        ]
-
-    def settle(copies):
-        for copy in copies:
-            copy.wait()
-
-    def squares(values):
-        return jnp.sum(values * values, axis=0, keepdims=True)
-
-    small_moves = to_rows(
-        0, lambda other, at: (small_ref.at[share(other, few)], small_got.at[at])
-    )
-    gout_sum[...] = lax.dot_general(
-        gated_ref[...], cot_ref[...], (((0,), (0,)), ((), ())), preferred_element_type=jnp.float32
-    )
-    gout_low[...] = gout_sum[...].astype(jnp.bfloat16)
-    gout_moves = to_rows(
-        1, lambda other, at: (gout_low.at[share(other, outer)], gout_got.at[at])
-    )
-    for half in range(2):
-        result = lax.dot_general(
-            normed_ref[...],
-            back_ref[half],
-            (((0,), (0,)), ((), ())),
-            preferred_element_type=jnp.float32,
-        )
-        wide = gin_sum.shape[2]
-        for place in range(nrows // 2):
-            piece = result[:, place * wide : (place + 1) * wide]
-            gin_sum[half * (nrows // 2) + place] = piece
-            gin_low[half * (nrows // 2) + place] = piece.astype(jnp.bfloat16)
-    gin_moves = to_rows(2, lambda other, at: (gin_low.at[other], gin_got.at[at]))
-
-    settle(small_moves)
-    total = small_ref[share(row, few), :].astype(jnp.float32)
-    for at in range(nrows - 1):
-        total = total + small_got[at].astype(jnp.float32)
-    small_part[...] = total.astype(jnp.bfloat16)
-    small_moves = to_seq(
-        0, lambda other, at: (small_part.at[:, share(other, channels)], small_seq.at[at])
-    )
-
-    settle(gout_moves)
-    total = gout_sum[share(row, outer), :]
-    for at in range(nrows - 1):
-        total = total + gout_got[at].astype(jnp.float32)
-    gout_out[share(row, outer), :] = total.astype(jnp.bfloat16)
-    gout_moves = to_rows(
-        3,
-        lambda other, at: (gout_out.at[share(row, outer)], gout_out.at[share(row, outer)]),
-    )
-    norm = jnp.sum(squares(total), axis=1, keepdims=True)
-
-    settle(gin_moves)
-    total = gin_sum[row]
-    for at in range(nrows - 1):
-        total = total + gin_got[at].astype(jnp.float32)
-    gin_part[...] = total.astype(jnp.bfloat16)
-    gin_moves = to_seq(
-        1, lambda other, at: (gin_part.at[share(other, inner)], gin_out.at[row, member])
-    )
-    gin_out[row, member] = gin_part[share(member, inner), :]
-    norm = norm + jnp.sum(squares(total), axis=1, keepdims=True)
-
-    settle(small_moves)
-    total = small_part[:, share(member, channels)].astype(jnp.float32)
-    for at in range(devices - 1):
-        total = total + small_seq[at].astype(jnp.float32)
-    small_out[share(row, few), :] = total.astype(jnp.bfloat16)
-    small_moves = to_rows(
-        4, lambda other, at: (small_out.at[share(row, few)], small_out.at[share(row, few)])
-    )
-    norm = norm + jnp.sum(squares(total), axis=1, keepdims=True)
-    norm_seq[member] = jnp.broadcast_to(norm, (8, LANES))
-    norm_moves = to_seq(2, lambda other, at: (norm_seq.at[member], norm_seq.at[member]))
-
-    settle(gin_moves)
-    gin_moves = to_rows(5, lambda other, at: (gin_out.at[row], gin_out.at[row]))
-    settle(norm_moves)
-    norm_rows[row] = jnp.sum(norm_seq[...], axis=0)
-    norm_moves = to_rows(6, lambda other, at: (norm_rows.at[row], norm_rows.at[row]))
-    settle(norm_moves)
-    norm_out[...] = jnp.sqrt(jnp.sum(norm_rows[...], axis=0))
-    settle(small_moves)
-    settle(gout_moves)
-    settle(gin_moves)
-
-
-def grads_of(normed_all, back_mine, gated_mine, cot_all, small, nrows, devices):
-    depth = normed_all.shape[1]
-    channels = gated_mine.shape[1]
-    wide = 2 * channels // nrows
-    few = small.shape[0] // nrows
-    low = jnp.bfloat16
-    return pl.pallas_call(
-        functools.partial(grads_kernel, nrows, devices),
-        in_specs=[pl.BlockSpec(memory_space=pltpu.VMEM)] * 5,
-        out_specs=[pl.BlockSpec(memory_space=pltpu.VMEM)] * 4,
-        out_shape=[
-            jax.ShapeDtypeStruct((nrows, devices, depth // devices, wide), low),
-            jax.ShapeDtypeStruct((channels, depth), low),
-            jax.ShapeDtypeStruct((small.shape[0], channels), low),
-            jax.ShapeDtypeStruct((8, LANES), jnp.float32),
-        ],
-        scratch_shapes=[
-            pltpu.VMEM((nrows - 1, few, E), low),
-            pltpu.VMEM((few, E), low),
-            pltpu.VMEM((devices - 1, few, channels), low),
-            pltpu.VMEM((channels, depth), jnp.float32),
-            pltpu.VMEM((channels, depth), low),
-            pltpu.VMEM((nrows - 1, channels // nrows, depth), low),
-            pltpu.VMEM((nrows, depth, wide), jnp.float32),
-            pltpu.VMEM((nrows, depth, wide), low),
-            pltpu.VMEM((nrows - 1, depth, wide), low),
-            pltpu.VMEM((depth, wide), low),
-            pltpu.VMEM((devices, 8, LANES), jnp.float32),
-            pltpu.VMEM((nrows, 8, LANES), jnp.float32),
-            pltpu.SemaphoreType.DMA((7, 2, nrows - 1)),
-            pltpu.SemaphoreType.DMA((3, 2, devices - 1)),
-        ],
-        compiler_params=pltpu.CompilerParams(
-            collective_id=2, has_side_effects=True, vmem_limit_bytes=56 * 2**20
-        ),
-        name="grads",
-    )(normed_all, back_mine, gated_mine, cot_all, small)
 
 
 PACKED = (R + 2 * N, R, N, K, 1, 1, 1, 1)
@@ -792,6 +570,668 @@
     return spans
 
 
+def silu_pair(values):
+    sigmoid_of = jax.nn.sigmoid(values)
+    return values * sigmoid_of, sigmoid_of * (1.0 + values * (1.0 - sigmoid_of))
+
+
+def core_kernel(
+    nrows,
+    devices,
+    starts_ref,
+    tokens_ref,
+    cot_ref,
+    gain_ref,
+    in_proj_ref,
+    out_proj_ref,
+    conv_ref,
+    x_proj_ref,
+    dt_proj_ref,
+    dskip_ref,
+    rates_ref,
+    normed_ref,
+    inner_ref,
+    gates_ref,
+    back_ref,
+    pre_act_ref,
+    delta_pre_ref,
+    ddec_ref,
+    drive_ref,
+    grady_ref,
+    rank_ref,
+    inb_ref,
+    outb_ref,
+    all_ref,
+    sums_ref,
+    cot_all_ref,
+    output_ref,
+    grad_ref,
+    gin_out,
+    gout_out,
+    small_out,
+    norm_out,
+    in_proj_buf,
+    out_proj_buf,
+    docid,
+    masks,
+    kept,
+    first,
+    second,
+    gin,
+    gout,
+    gated,
+    back_gates,
+    back_inner,
+    grad_act,
+    grad_conv,
+    padded,
+    rank_back,
+    proj_back,
+    normed_sib,
+    gated_got,
+    back_got,
+    gout_sum,
+    gout_low,
+    gout_got,
+    gin_sum,
+    gin_low,
+    gin_got,
+    gin_pub,
+    small,
+    small_low,
+    small_got,
+    small_part,
+    small_seq,
+    norm_seq,
+    norm_rows,
+    loads,
+    sib_wires,
+    halo_wires,
+    gated_wires,
+    back_wires,
+    line_wires,
+    plane_wires,
+    row_wires,
+    seq_wires,
+    local,
+):
+    row = lax.axis_index("rows")
+    member = lax.axis_index("seq")
+    level, side = member // 2, lax.rem(member, 2)
+    levels = devices // 2
+    steps = tokens_ref.shape[0]
+    groups = E // LANES
+    chunk = 4 * LANES
+    chunks = E // chunk
+    shard = E // devices
+    halo = inner_ref.shape[0] - steps
+    reach = devices // 2
+    half = N // 2
+    low = jnp.bfloat16
+    wide = jnp.float32
+    spans = packed_rows()
+
+    in_loads = [
+        pltpu.make_async_copy(
+            in_proj_ref.at[:, span(at, chunk)], in_proj_buf.at[at], loads.at[at]
+        )
+        for at in range(2 * chunks)
+    ]
+    out_load = pltpu.make_async_copy(out_proj_ref, out_proj_buf, loads.at[2 * chunks])
+    for load in in_loads + [out_load]:
+        load.start()
+
+    def share(index, size):
+        return pl.ds(pl.multiple_of(index * size, size), size)
+
+    def plane(turn, other):
+        return {
+            "rows": lax.rem(row + turn, nrows),
+            "seq": 2 * level + lax.rem(side + other, 2),
+        }
+
+    def line(turn):
+        return {"seq": 2 * lax.rem(level + turn, levels) + side}
+
+    def remote(source, target, send, recv, device):
+        return pltpu.make_async_remote_copy(
+            src_ref=source,
+            dst_ref=target,
+            send_sem=send,
+            recv_sem=recv,
+            device_id=device,
+            device_id_type=MESH,
+        )
+
+    def begin(copies):
+        for copy in copies:
+            copy.start()
+        return copies
+
+    def settle(copies):
+        for copy in copies:
+            copy.wait()
+
+    barrier = pltpu.get_barrier_semaphore()
+    greeted = [{"seq": partner("seq", offset)} for offset in range(1, devices)]
+    greeted += [plane(turn, other) for turn in range(1, nrows) for other in range(2)]
+    for device in greeted:
+        pl.semaphore_signal(barrier, inc=1, device_id=device, device_id_type=MESH)
+
+    places = member * steps - 8 + lax.broadcasted_iota(jnp.int32, docid.shape, 0)
+    count = jnp.zeros(docid.shape, jnp.int32)
+    for index in range(starts_ref.shape[0]):
+        count = count + jnp.where(places >= starts_ref[index], 1, 0)
+    docid[...] = count
+    for offset in range(1, K):
+        masks[offset] = jnp.where(
+            docid[8 - offset : 16 - offset + steps, :] == docid[8:, :], 1.0, 0.0
+        )
+    gin[...] = jnp.zeros_like(gin)
+    gout[...] = jnp.zeros_like(gout)
+    rank_back[...] = jnp.zeros_like(rank_back)
+    small[...] = jnp.zeros_like(small)
+    pl.semaphore_wait(barrier, len(greeted))
+
+    normed_copy = remote(
+        normed_ref, normed_sib, sib_wires.at[0], sib_wires.at[1], {"seq": 2 * level + 1 - side}
+    )
+    normed_copy.start()
+
+    def fold(values):
+        return values[:half] + values[half:]
+
+    def collapse(source, place):
+        total = source[place, pl.ds(0, steps, stride=half), :]
+        for index in range(1, half):
+            total = total + source[place, pl.ds(index, steps, stride=half), :]
+        return total
+
+    def lanes(at, place):
+        return share(4 * at + place, LANES)
+
+    def column_sum(values):
+        return jnp.sum(values, axis=0, keepdims=True)
+
+    def trade(kind, source, at, turn):
+        copies = []
+        for other in range(2):
+            columns = share(2 * at + lax.rem(side + other, 2), shard)
+            target = back_got.at[kind, other, row]
+            if turn == 0 and other == 0:
+                copies.append(
+                    pltpu.make_async_copy(source.at[:, columns], target, local.at[kind])
+                )
+            else:
+                copies.append(
+                    remote(
+                        source.at[:, columns],
+                        target,
+                        back_wires.at[kind, 0, 2 * turn + other],
+                        back_wires.at[kind, 1, 2 * turn + other],
+                        plane(turn, other),
+                    )
+                )
+        return begin(copies)
+
+    def gated_copy(target_member):
+        return remote(
+            gated.at[:, share(target_member, shard)],
+            gated_got.at[share(member, steps), :],
+            gated_wires.at[0, target_member],
+            gated_wires.at[1, member],
+            {"seq": target_member},
+        )
+
+    gate_moves = []
+    order = [(turn, lax.rem(row + turn, nrows)) for turn in [*range(1, nrows), 0]]
+    for turn, at in order:
+
+        def through(device, states):
+            new = []
+            for place in range(4):
+                total = sums_ref[device, pl.ds(4 * at + place, 1), :]
+                factor = jnp.exp2(total * rates_ref[:, lanes(at, place)])
+                new.append(
+                    factor * states[place]
+                    + all_ref[device, at, :, place * LANES : (place + 1) * LANES].astype(wide)
+                )
+            return new
+
+        def forward(t, hidden):
+            in_row, out_row = inb_ref[t], outb_ref[t]
+            new = []
+            for place in range(4):
+                here = (4 * at + place, pl.ds(t, 1))
+                decay = jnp.exp2(ddec_ref[here] * rates_ref[:, lanes(at, place)])
+                state = decay * hidden[place] + drive_ref[here] * in_row
+                kept[t + 1, place] = state
+                first[place, share(t, half), :] = fold(state * out_row)
+                new.append(state)
+            return new
+
+        def backward(back, carry):
+            later, grates = carry
+            t = steps - 1 - back
+            in_row, out_row = inb_ref[t], outb_ref[t]
+            gin_row, gout_row = gin[t], gout[t]
+            new = ([], [])
+            for place in range(4):
+                here = (4 * at + place, pl.ds(t, 1))
+                grady = grady_ref[here]
+                delta = ddec_ref[here]
+                rates = rates_ref[:, lanes(at, place)]
+                adjoint = grady * out_row + later[place]
+                gout_row = gout_row + grady * kept[t + 1, place]
+                gin_row = gin_row + adjoint * drive_ref[here]
+                first[place, share(t, half), :] = fold(adjoint * in_row)
+                passed = jnp.exp2(delta * rates) * adjoint
+                pulled = passed * kept[t, place]
+                second[place, share(t, half), :] = fold(pulled * rates)
+                new[0].append(passed)
+                new[1].append(grates[place] + pulled * delta)
+            gin[t] = gin_row
+            gout[t] = gout_row
+            return new
+
+        zeros = [jnp.zeros((N, LANES), wide) for _ in range(4)]
+        entering = lax.fori_loop(jnp.maximum(member - reach, 0), member, through, zeros)
+        last = jnp.minimum(member + reach, devices - 1)
+        leaving = lax.fori_loop(0, last - member, lambda d, s: through(last - d, s), zeros)
+        for place in range(4):
+            kept[0, place] = entering[place]
+        lax.fori_loop(0, steps, forward, entering, unroll=4)
+        for place in range(4):
+            group, columns = 4 * at + place, lanes(at, place)
+            act = silu(pre_act_ref[group])
+            y_full = collapse(first, place) + dskip_ref[:, columns] * act
+            gate, slope = silu_pair(gates_ref[:, columns].astype(wide))
+            gated[:, columns] = (y_full * gate).astype(low)
+            back_gates[:, columns] = (
+                back_ref[:, columns].astype(wide) * y_full * slope
+            ).astype(low)
+            small[spans[6][0] : spans[6][1], columns] = column_sum(grady_ref[group] * act)
+        gate_moves += trade(1, back_gates, at, turn)
+        for core in range(2):
+
+            @pl.when(2 * at + core != member)
+            def _():
+                gated_copy(2 * at + core).start()
+
+        _, grates = lax.fori_loop(0, steps, backward, (leaving, zeros), unroll=4)
+        lows = []
+        for place in range(4):
+            group, columns = 4 * at + place, lanes(at, place)
+            along = collapse(first, place)
+            delta_pre = delta_pre_ref[group]
+            act = silu(pre_act_ref[group])
+            grad_delta = along * act + collapse(second, place) * math.log(2.0)
+            pre_low = (grad_delta * jax.nn.sigmoid(delta_pre)).astype(low)
+            lows.append(pre_low)
+            grad_act[group] = grady_ref[group] * dskip_ref[:, columns] + along * softplus(delta_pre)
+            small[spans[5][0] : spans[5][1], columns] = column_sum(pre_low.astype(wide))
+            small[spans[2][0] : spans[2][1], columns] = (
+                grates[place] * rates_ref[:, columns] * math.log(2.0)
+            )
+        lows = jnp.concatenate(lows, axis=1)
+        rank_back[...] += lax.dot_general(
+            lows,
+            dt_proj_ref[:, share(at, chunk)],
+            (((1,), (1,)), ((), ())),
+            preferred_element_type=wide,
+        )
+        small[spans[1][0] : spans[1][1], share(at, chunk)] = lax.dot_general(
+            rank_ref[...], lows, (((0,), (0,)), ((), ())), preferred_element_type=wide
+        )
+
+    gated_got[share(member, steps), :] = gated[:, share(member, shard)]
+    for offset in range(1, devices):
+        gated_copy(partner("seq", offset)).wait_send()
+        source = partner("seq", offset)
+        remote(
+            gated.at[:, share(member, shard)],
+            gated_got.at[share(source, steps), :],
+            gated_wires.at[0, member],
+            gated_wires.at[1, source],
+            {"seq": source},
+        ).wait_recv()
+
+    def to_rows(kind, make):
+        return begin(
+            [
+                remote(
+                    *make(partner("rows", offset), offset - 1),
+                    row_wires.at[kind, 0, offset - 1],
+                    row_wires.at[kind, 1, offset - 1],
+                    {"rows": partner("rows", offset)},
+                )
+                for offset in range(1, nrows)
+            ]
+        )
+
+    def to_seq(kind, make):
+        return begin(
+            [
+                remote(
+                    *make(partner("seq", offset), offset - 1),
+                    seq_wires.at[kind, 0, offset - 1],
+                    seq_wires.at[kind, 1, offset - 1],
+                    {"seq": partner("seq", offset)},
+                )
+                for offset in range(1, devices)
+            ]
+        )
+
+    def squares(values):
+        return jnp.sum(jnp.sum(values * values, axis=0, keepdims=True), axis=1, keepdims=True)
+
+    def in_grads(kind):
+        total = jnp.zeros((D, shard), wide)
+        for other, normed in ((0, normed_ref), (1, normed_sib)):
+            for source in range(nrows):
+                total = total + lax.dot_general(
+                    normed[source],
+                    back_got[kind, other, source],
+                    (((0,), (0,)), ((), ())),
+                    preferred_element_type=wide,
+                )
+        gin_sum[kind] = total
+        gin_low[kind] = total.astype(low)
+        return begin(
+            [
+                remote(
+                    gin_low.at[kind, share(lax.rem(level + turn, levels), D // levels), :],
+                    gin_got.at[kind, turn - 1],
+                    line_wires.at[kind, 0, turn - 1],
+                    line_wires.at[kind, 1, turn - 1],
+                    line(turn),
+                )
+                for turn in range(1, levels)
+            ]
+        )
+
+    def in_share(kind):
+        total = gin_sum[kind, share(level, D // levels), :]
+        for turn in range(levels - 1):
+            total = total + gin_got[kind, turn].astype(wide)
+        gin_pub[kind] = total.astype(low)
+        owned = D // devices
+        columns = share(kind * devices + 2 * row + side, shard)
+        gin_out[:, columns] = gin_pub[kind, share(side, owned), :]
+        copies = [
+            remote(
+                gin_pub.at[kind, share(lax.rem(side + other, 2), owned), :],
+                gin_out.at[:, columns],
+                plane_wires.at[kind, 0, 2 * turn + other],
+                plane_wires.at[kind, 1, 2 * turn + other],
+                plane(turn, other),
+            )
+            for turn in range(nrows)
+            for other in range(2)
+            if turn + other > 0
+        ]
+        return begin(copies), squares(total)
+
+    outer = gout_out.shape[0] // nrows
+    gout_sum[...] = lax.dot_general(
+        gated_got[...], cot_all_ref[...], (((0,), (0,)), ((), ())), preferred_element_type=wide
+    )
+    gout_low[...] = gout_sum[...].astype(low)
+    gout_moves = to_rows(
+        0, lambda other, at: (gout_low.at[share(other, outer), :], gout_got.at[at])
+    )
+    normed_copy.wait()
+    settle(gate_moves)
+    gate_moves = in_grads(1)
+
+    proj_back[:, :R] = rank_back[...].astype(low)
+    proj_back[:, R : R + N] = jnp.sum(gin[...], axis=2).astype(low)
+    proj_back[:, R + N :] = jnp.sum(gout[...], axis=2).astype(low)
+    for at in range(chunks):
+        pulled = jnp.dot(
+            proj_back[...], x_proj_ref[:, span(at, chunk)], preferred_element_type=wide
+        )
+        lows = []
+        for place in range(4):
+            group = 4 * at + place
+            act, slope = silu_pair(pre_act_ref[group])
+            lows.append(act.astype(low))
+            grad_conv[group, :steps, :] = (
+                grad_act[group] + pulled[:, place * LANES : (place + 1) * LANES]
+            ) * slope
+        small[spans[0][0] : spans[0][1], span(at, chunk)] = lax.dot_general(
+            proj_back[...],
+            jnp.concatenate(lows, axis=1),
+            (((0,), (0,)), ((), ())),
+            preferred_element_type=wide,
+        )
+    halo_copy = remote(
+        grad_conv.at[:, 0:8, :],
+        grad_conv.at[:, steps : steps + 8, :],
+        halo_wires.at[0],
+        halo_wires.at[1],
+        {"seq": partner("seq", devices - 1)},
+    )
+
+    @pl.when(member > 0)
+    def _():
+        halo_copy.start()
+
+    @pl.when(member == devices - 1)
+    def _():
+        grad_conv[:, steps : steps + 8, :] = jnp.zeros((groups, 8, LANES), wide)
+
+    out_load.wait()
+    stream = tokens_ref[...].astype(wide)
+    output_ref[...] = stream + jnp.dot(
+        gated[...], out_proj_buf[...], preferred_element_type=wide
+    )
+    for load in in_loads:
+        load.wait()
+    grad_normed = jnp.zeros((steps, D), wide)
+    for at in range(chunks):
+        grad_normed = grad_normed + lax.dot_general(
+            back_gates[:, span(at, chunk)],
+            in_proj_buf[chunks + at],
+            (((1,), (1,)), ((), ())),
+            preferred_element_type=wide,
+        )
+
+    @pl.when(member > 0)
+    def _():
+        halo_copy.wait_send()
+
+    @pl.when(member < devices - 1)
+    def _():
+        halo_copy.wait_recv()
+
+    inner_moves = []
+    for turn, at in order:
+        for place in range(4):
+            group, columns = 4 * at + place, lanes(at, place)
+            padded[...] = inner_ref[halo - 8 :, columns].astype(wide)
+            here = grad_conv[group, :steps, :]
+            pulled = conv_ref[0:1, columns] * here
+            small[spans[4][0] : spans[4][1], columns] = column_sum(here)
+            at_row = spans[3][0]
+            small[at_row : at_row + 1, columns] = column_sum(here * padded[8:, :])
+            for offset in range(1, K):
+                small[at_row + offset : at_row + offset + 1, columns] = column_sum(
+                    here * masks[offset, :steps, :] * padded[8 - offset : 8 - offset + steps, :]
+                )
+                pulled = pulled + conv_ref[offset : offset + 1, columns] * (
+                    grad_conv[group, offset : offset + steps, :]
+                    * masks[offset, offset : offset + steps, :]
+                )
+            back_inner[:, columns] = pulled.astype(low)
+        inner_moves += trade(0, back_inner, at, turn)
+
+    for at in range(chunks):
+        grad_normed = grad_normed + lax.dot_general(
+            back_inner[:, span(at, chunk)],
+            in_proj_buf[at],
+            (((1,), (1,)), ((), ())),
+            preferred_element_type=wide,
+        )
+    inverse = lax.rsqrt(jnp.mean(stream * stream, axis=1, keepdims=True) + EPS)
+    grad_gain = column_sum(grad_normed * stream * inverse)
+    owned = D // devices
+    for index in range(devices):
+        small[spans[7][0] : spans[7][1], index * shard : index * shard + owned] = grad_gain[
+            :, index * owned : (index + 1) * owned
+        ]
+    scaled = grad_normed * gain_ref[...]
+    grad_ref[...] = (
+        cot_ref[...].astype(wide)
+        + inverse * scaled
+        - stream
+        * inverse
+        * inverse
+        * inverse
+        * jnp.mean(scaled * stream, axis=1, keepdims=True)
+    )
+    few = small_low.shape[0] // nrows
+    small_low[...] = small[...].astype(low)
+    small_moves = to_rows(
+        1, lambda other, at: (small_low.at[share(other, few), :], small_got.at[at])
+    )
+
+    settle(gout_moves)
+    total = gout_sum[share(row, outer), :]
+    for at in range(nrows - 1):
+        total = total + gout_got[at].astype(wide)
+    gout_out[share(row, outer), :] = total.astype(low)
+    gout_moves = to_rows(
+        2,
+        lambda other, at: (
+            gout_out.at[share(row, outer), :],
+            gout_out.at[share(row, outer), :],
+        ),
+    )
+    norm = squares(total)
+
+    settle(inner_moves)
+    inner_moves = in_grads(0)
+
+    settle(small_moves)
+    total = small[share(row, few), :]
+    for at in range(nrows - 1):
+        total = total + small_got[at].astype(wide)
+    small_part[...] = total.astype(low)
+    small_moves = to_seq(
+        0, lambda other, at: (small_part.at[:, share(other, shard)], small_seq.at[at])
+    )
+
+    settle(gate_moves)
+    gate_moves, part = in_share(1)
+    norm = norm + part
+
+    settle(small_moves)
+    total = small_part[:, share(member, shard)].astype(wide)
+    for at in range(devices - 1):
+        total = total + small_seq[at].astype(wide)
+    small_out[share(row, few), :] = total.astype(low)
+    small_moves = to_rows(
+        3,
+        lambda other, at: (
+            small_out.at[share(row, few), :],
+            small_out.at[share(row, few), :],
+        ),
+    )
+    norm = norm + squares(total)
+
+    settle(inner_moves)
+    inner_moves, part = in_share(0)
+    norm_seq[member] = jnp.broadcast_to(norm + part, (8, LANES))
+    settle(to_seq(1, lambda other, at: (norm_seq.at[member], norm_seq.at[member])))
+    norm_rows[row] = jnp.sum(norm_seq[...], axis=0)
+    settle(to_rows(4, lambda other, at: (norm_rows.at[row], norm_rows.at[row])))
+    norm_out[...] = jnp.sqrt(jnp.sum(norm_rows[...], axis=0))
+    settle(gout_moves)
+    settle(gate_moves)
+    settle(small_moves)
+    settle(inner_moves)
+
+
+def core_of(operands, nrows, devices):
+    steps = operands[1].shape[0]
+    groups = E // LANES
+    chunk = 4 * LANES
+    chunks = E // chunk
+    levels = devices // 2
+    shard = E // devices
+    low, wide = jnp.bfloat16, jnp.float32
+    few = PACKED_ROWS // nrows
+    vmem = pl.BlockSpec(memory_space=pltpu.VMEM)
+    specs = [vmem] * len(operands)
+    specs[0] = pl.BlockSpec(memory_space=pltpu.SMEM)
+    specs[4] = specs[5] = pl.BlockSpec(memory_space=pl.ANY)
+    dma = pltpu.SemaphoreType.DMA
+    return pl.pallas_call(
+        functools.partial(core_kernel, nrows, devices),
+        in_specs=specs,
+        out_specs=[vmem] * 6,
+        out_shape=[
+            jax.ShapeDtypeStruct((steps, D), wide),
+            jax.ShapeDtypeStruct((steps, D), wide),
+            jax.ShapeDtypeStruct((D // devices, 2 * E), low),
+            jax.ShapeDtypeStruct((shard, D), low),
+            jax.ShapeDtypeStruct((PACKED_ROWS, shard), low),
+            jax.ShapeDtypeStruct((8, LANES), wide),
+        ],
+        scratch_shapes=[
+            pltpu.VMEM((2 * chunks, D, chunk), low),
+            pltpu.VMEM((E, D), low),
+            pltpu.VMEM((steps + 16, LANES), jnp.int32),
+            pltpu.VMEM((K, steps + 8, LANES), wide),
+            pltpu.VMEM((steps + 1, 4, N, LANES), wide),
+            pltpu.VMEM((4, steps * N // 2, LANES), wide),
+            pltpu.VMEM((4, steps * N // 2, LANES), wide),
+            pltpu.VMEM((steps, N, LANES), wide),
+            pltpu.VMEM((steps, N, LANES), wide),
+            pltpu.VMEM((steps, E), low),
+            pltpu.VMEM((steps, E), low),
+            pltpu.VMEM((steps, E), low),
+            pltpu.VMEM((groups, steps, LANES), wide),
+            pltpu.VMEM((groups, steps + 8, LANES), wide),
+            pltpu.VMEM((steps + 8, LANES), wide),
+            pltpu.VMEM((steps, R), wide),
+            pltpu.VMEM((steps, R + 2 * N), low),
+            pltpu.VMEM((nrows, steps, D), low),
+            pltpu.VMEM((steps * devices, shard), low),
+            pltpu.VMEM((2, 2, nrows, steps, shard), low),
+            pltpu.VMEM((shard, D), wide),
+            pltpu.VMEM((shard, D), low),
+            pltpu.VMEM((nrows - 1, shard // nrows, D), low),
+            pltpu.VMEM((2, D, shard), wide),
+            pltpu.VMEM((2, D, shard), low),
+            pltpu.VMEM((2, levels - 1, D // levels, shard), low),
+            pltpu.VMEM((2, D // levels, shard), low),
+            pltpu.VMEM((PACKED_ROWS, E), wide),
+            pltpu.VMEM((PACKED_ROWS, E), low),
+            pltpu.VMEM((nrows - 1, few, E), low),
+            pltpu.VMEM((few, E), low),
+            pltpu.VMEM((devices - 1, few, shard), low),
+            pltpu.VMEM((devices, 8, LANES), wide),
+            pltpu.VMEM((nrows, 8, LANES), wide),
+            dma((2 * chunks + 1,)),
+            dma((2,)),
+            dma((2,)),
+            dma((2, devices)),
+            dma((2, 2, 2 * nrows)),
+            dma((2, 2, levels - 1)),
+            dma((2, 2, 2 * nrows)),
+            dma((5, 2, nrows - 1)),
+            dma((2, 2, devices - 1)),
+            dma((2,)),
+        ],
+        compiler_params=pltpu.CompilerParams(
+            collective_id=1, has_side_effects=True, vmem_limit_bytes=62 * 2**20
+        ),
+        name="core",
+    )(*operands)
+
+
 def update_kernel(member_ref, norm_ref, gin_ref, gout_ref, small_ref, *refs):
     weights, moments, averages, outs = refs[:10], refs[10:20], refs[20:30], refs[30:]
     shrink_by = 1.0 / jnp.maximum(norm_ref[0:1, 0:1], 1.0)
@@ -806,11 +1246,7 @@
         outs[3 * ordinal + 1][at] = renewed
         outs[3 * ordinal + 2][at] = AVERAGE * averages[ordinal][at] + (1.0 - AVERAGE) * renewed
 
-    places, members = gin_ref.shape[:2]
-    for column in range(members):
-        for place in range(places):
-            columns = pl.ds((column * places + place) * LANES, LANES)
-            renew(1, gin_ref[place, column].astype(jnp.float32), (slice(None), columns))
+    renew(1, gin_ref[...].astype(jnp.float32))
     renew(9, gout_ref[...].astype(jnp.float32))
 
     @pl.when(pl.program_id(0) == 0)
@@ -821,7 +1257,7 @@
             return small_ref[spans[index][0] : spans[index][1], :].astype(jnp.float32)
 
         small = small_ref[...].astype(jnp.float32)
-        renew(4, jnp.transpose(part(0)))
+        renew(4, part(0))
         renew(5, part(1))
         renew(7, part(2))
         renew(2, part(3))
@@ -831,18 +1267,16 @@
         renew(0, gain)
 
 
-def update_of(member, norm_tile, gin_parts, gout, small, weights, moments, averages):
-    nrows, devices, inner, wide = gin_parts.shape
+def update_of(member, norm_tile, gin, gout, small, weights, moments, averages):
+    inner = gin.shape[0]
     channels = gout.shape[0]
     blocks = 8
     outer = channels // blocks
-    half = blocks // 2
-    pair = devices // half
-    block = nrows // 2 * pair * wide
+    block = gin.shape[1] // blocks
     flat = (0, 3, 6, 8)
 
     def rows_of(array, ordinal):
-        return array.reshape(1, -1) if ordinal in flat else array
+        return array.reshape(1, -1) if ordinal in flat else array.T if ordinal == 4 else array
 
     def shard(shape, ordinal):
         if ordinal == 1:
@@ -856,8 +1290,6 @@
             return pl.BlockSpec((inner, block), lambda j, m: (m[0], j))
         if ordinal == 9:
             return pl.BlockSpec((outer, shape[1]), lambda j, m: (m[0] * blocks + j, 0))
-        if ordinal == 4:
-            return pl.BlockSpec(shape, lambda j, m: (m[0], 0))
         return pl.BlockSpec(shape, lambda j, m: (0, m[0]))
 
     weights = [rows_of(array, ordinal) for ordinal, array in enumerate(weights)]
@@ -872,9 +1304,7 @@
             grid=(blocks,),
             in_specs=[
                 pl.BlockSpec(norm_tile.shape, lambda j, m: (0, 0)),
-                pl.BlockSpec(
-                    (nrows // 2, pair, inner, wide), lambda j, m: (j // half, j % half, 0, 0)
-                ),
+                pl.BlockSpec((inner, block), lambda j, m: (0, j)),
                 pl.BlockSpec((outer, gout.shape[1]), lambda j, m: (j, 0)),
                 pl.BlockSpec(small.shape, lambda j, m: (0, 0)),
             ]
@@ -888,11 +1318,12 @@
             for ordinal in range(10)
             for _ in range(3)
         ],
-        compiler_params=pltpu.CompilerParams(vmem_limit_bytes=48 * 2**20),
+        compiler_params=pltpu.CompilerParams(vmem_limit_bytes=63 * 2**20),
         name="update",
-    )(member, norm_tile, gin_parts, gout, small, *weights, *moments, *averages)
+    )(member, norm_tile, gin, gout, small, *weights, *moments, *averages)
     return [
-        out.reshape(-1) if index // 3 in flat else out for index, out in enumerate(outs)
+        out.reshape(-1) if index // 3 in flat else out.T if index // 3 == 4 else out
+        for index, out in enumerate(outs)
     ]
 
 
@@ -944,6 +1375,8 @@
     scaled_rates = rates * (1.0 / math.log(2.0))
     lengths = doc_lengths[0]
     starts = (jnp.cumsum(lengths) - lengths).astype(jnp.int32)
+    nrows = lax.axis_size("rows")
+    direct = devices == 2 * nrows and E % (2 * nrows * LANES) == 0 and E == nrows * 4 * LANES
     (
         normed,
         inner_low,
@@ -968,14 +1401,89 @@
         out_proj,
         conv_weight,
         conv_bias[None],
-        x_proj,
+        x_proj.T,
         dt_proj,
         dt_bias[None],
         scaled_rates,
         devices,
-    )
-    normed_all = lax.all_gather(normed, "seq", axis=0, tiled=True)
+        nrows if direct else 1,
+    )
     cot_all = lax.all_gather(cot_low, "seq", axis=0, tiled=True)
+    member_word = jnp.reshape(member_id, (1,)).astype(jnp.int32)
+    moments = (
+        moment_norm_gain,
+        moment_in_proj,
+        moment_conv_weight,
+        moment_conv_bias,
+        moment_x_proj,
+        moment_dt_proj,
+        moment_dt_bias,
+        moment_a_log,
+        moment_d_skip,
+        moment_out_proj,
+    )
+    averages = (
+        average_norm_gain,
+        average_in_proj,
+        average_conv_weight,
+        average_conv_bias,
+        average_x_proj,
+        average_dt_proj,
+        average_dt_bias,
+        average_a_log,
+        average_d_skip,
+        average_out_proj,
+    )
+    if direct:
+        weights = (
+            norm_gain,
+            in_proj,
+            conv_weight,
+            conv_bias,
+            x_proj,
+            dt_proj,
+            dt_bias,
+            a_log,
+            d_skip,
+            out_proj,
+        )
+        block_output, input_grad, gin_share, gout_share, small, norm_tile = core_of(
+            (
+                starts,
+                tokens[0],
+                cot_low,
+                norm_gain[None],
+                in_proj,
+                out_proj,
+                conv_weight,
+                x_proj.T,
+                dt_proj,
+                d_skip[None],
+                scaled_rates,
+                normed,
+                inner_low,
+                gates_low,
+                back_gated,
+                pre_act,
+                delta_pre,
+                ddec,
+                drive,
+                grady_rows,
+                rank_low,
+                inb,
+                outb,
+                everyone,
+                all_sums,
+                cot_all,
+            ),
+            nrows,
+            devices,
+        )
+        updated = update_of(
+            member_word, norm_tile, gin_share, gout_share, small, weights, moments, averages
+        )
+        return (block_output[None], input_grad[None], norm_tile[0, 0], *updated)
+    normed_all = lax.all_gather(normed[0], "seq", axis=0, tiled=True)
     positions = member_id * steps + jnp.arange(-8, steps + 8, dtype=jnp.int32)
     docid, starting = doc_tables(doc_lengths[0], positions)
     masks = []
@@ -997,7 +1505,6 @@
     silu_gate = silu(gates)
     chan_back = back_gated.astype(jnp.float32)
     grad_y = chan_back * silu_gate
-    member_word = jnp.reshape(member_id, (1,)).astype(jnp.int32)
     scanned, along_in, pulled_sum, gin, gout, grad_rates = scan_of(
         member_word, ddec, drive, grady_rows, inb, outb, scaled_rates, everyone, all_sums, 512
     )
@@ -1077,76 +1584,26 @@
         ],
         axis=0,
     )
-    nrows = lax.axis_size("rows")
-    direct = channels % LANES == 0 and 2 * channels == nrows * LANES
-    if direct:
-        gated_mine, back_mine = trade(gated, back_xz, devices)
-        gin_parts, gout_share, small, norm_tile = grads_of(
-            normed_all, back_mine, gated_mine, cot_all, small.astype(jnp.bfloat16), nrows, devices
-        )
-        grad_norm = norm_tile[0, 0]
-    else:
-        gated_mine = lax.all_to_all(gated, "seq", split_axis=1, concat_axis=0, tiled=True)
-        back_mine = lax.all_to_all(back_xz, "seq", split_axis=2, concat_axis=1, tiled=True)
-        gout_share = lax.psum(
-            lax.dot_general(
-                gated_mine, cot_all, (((0,), (0,)), ((), ())), preferred_element_type=jnp.float32
-            ),
-            "rows",
-        )
-        gin_share = lax.psum(
-            jnp.einsum("td,ktc->dkc", normed_all, back_mine, preferred_element_type=jnp.float32),
-            "rows",
-        )
-        gin_share = lax.all_to_all(
-            gin_share, "seq", split_axis=0, concat_axis=2, tiled=True
-        ).reshape(D // devices, 2 * E)
-        small = lax.psum(small, "rows")
-        small = lax.psum_scatter(small, "seq", scatter_dimension=1, tiled=True)
-        squares = jnp.sum(gin_share * gin_share) + jnp.sum(gout_share * gout_share)
-        grad_norm = jnp.sqrt(lax.psum(squares + jnp.sum(small * small), "seq"))
-    moments = (
-        moment_norm_gain,
-        moment_in_proj,
-        moment_conv_weight,
-        moment_conv_bias,
-        moment_x_proj,
-        moment_dt_proj,
-        moment_dt_bias,
-        moment_a_log,
-        moment_d_skip,
-        moment_out_proj,
-    )
-    averages = (
-        average_norm_gain,
-        average_in_proj,
-        average_conv_weight,
-        average_conv_bias,
-        average_x_proj,
-        average_dt_proj,
-        average_dt_bias,
-        average_a_log,
-        average_d_skip,
-        average_out_proj,
-    )
+    gated_mine = lax.all_to_all(gated, "seq", split_axis=1, concat_axis=0, tiled=True)
+    back_mine = lax.all_to_all(back_xz, "seq", split_axis=2, concat_axis=1, tiled=True)
+    gout_share = lax.psum(
+        lax.dot_general(
+            gated_mine, cot_all, (((0,), (0,)), ((), ())), preferred_element_type=jnp.float32
+        ),
+        "rows",
+    )
+    gin_share = lax.psum(
+        jnp.einsum("td,ktc->dkc", normed_all, back_mine, preferred_element_type=jnp.float32),
+        "rows",
+    )
+    gin_share = lax.all_to_all(
+        gin_share, "seq", split_axis=0, concat_axis=2, tiled=True
+    ).reshape(D // devices, 2 * E)
+    small = lax.psum(small, "rows")
+    small = lax.psum_scatter(small, "seq", scatter_dimension=1, tiled=True)
+    squares = jnp.sum(gin_share * gin_share) + jnp.sum(gout_share * gout_share)
+    grad_norm = jnp.sqrt(lax.psum(squares + jnp.sum(small * small), "seq"))
     results = [block_output, input_grad[None], grad_norm]
-    if direct:
-        weights = (
-            norm_gain,
-            in_proj,
-            conv_weight,
-            conv_bias,
-            x_proj,
-            dt_proj,
-            dt_bias,
-            a_log,
-            d_skip,
-            out_proj,
-        )
-        results += update_of(
-            member_word, norm_tile, gin_parts, gout_share, small, weights, moments, averages
-        )
-        return tuple(results)
     parts = [small[low:high] for low, high in packed_rows()]
     owner_grads = (
         parts[7][0, : D // devices],

time: 231 us -> 162 us (0.70)
  local copies, waits for them, and re-layouts: 28.6 us -> 3.87 us
  other arithmetic: 18.7 us -> 3.58 us
  matrix products: 13.8 us -> 0 us
  Pallas kernels: 153 us -> 140 us
    unnamed x139 -> x4, local copies, waits for them, and re-layouts: 17.6 us -> 2.68 us
    pallas_call x4 -> x2, Pallas kernels: 143 us -> 128 us  [the longest x1 86.9 us: core_of(): pl.pallas_call(functools.partial(core_kernel, nrows, devices), in_specs=s...]
    dot_general x7 -> x0, matrix products: 13.8 us -> none  [the longest x1 4.9 us: local(): lax.dot_general(back_xz[1], in_proj[:, E:], (((1,), (1,)), ((), ())), pre...]
    reduce_sum x6 -> x0, other arithmetic: 6.99 us -> none  [the longest x1 2.86 us: local(): grad_dtbias = jnp.sum(grad_pre.astype(jnp.float32), axis=0)]
    squeeze x2 -> x0, other arithmetic: 5.08 us -> none  [the longest x1 4.5 us: local(): back_xz[1]]
    concatenate x1 -> x0, local copies, waits for them, and re-layouts: 4.89 us -> none  [local(): jnp.concatenate([grad_xproj.T, grad_dtproj, grad_alog, grad_convw, grad_c...]
    another operation x4 -> x0, local copies, waits for them, and re-layouts: 2.41 us -> none  [local(): grad_convw = jnp.stack(conv_rows)]
  transfers between devices with their start and end apart: 3 -> 1, of which waited for: 0 -> 0; matrix products, arithmetic and copies ran while one was open for 18% -> 2% of each run, Pallas kernels for 21% -> 26%
where the time goes in v3:
time: 162 us
  Pallas kernels  140 us (86%)
  between operations  14.1 us (9%)
  local copies, waits for them, and re-layouts  3.87 us (2%)
  other arithmetic  3.58 us (2%)
    pallas_call x1, Pallas kernels, core_of(): pl.pallas_call(functools.partial(core_kernel, nrows, devices), in_specs=s...  86.9 us
    pallas_call x1, Pallas kernels, front_of(): pl.pallas_call(functools.partial(front_kernel, devices, nrows), in_specs=...  41.5 us
    pallas_call x1, Pallas kernels, update_of(): pl.pallas_call(update_kernel, grid_spec=pltpu.PrefetchScalarGridSpec(num_...  11.2 us
  transfers between devices with their start and end apart: 1, of which 0 were waited for; matrix products, arithmetic and copies ran while one was open for 2% of the time, Pallas kernels for 26%

profile of v3, /device:TPU:0, one launch (start us, length us, event | category | flops | bytes accessed | tf_op | source)
XLA Modules:
  0.0 161.9 jit_solution(16919206667775519128)
XLA Ops:
  7.2 0.0 all-gather.3.cloned.1.call-start
  7.3 0.7 all-gather.3.cloned.1.call-update
  8.0 0.8 reduce-window.9
  8.8 1.2 bitcast_subtract_fusion.starts_ref
  10.0 1.6 negate_multiply_fusion.rates_ref
  11.5 41.5 %front.1 = (bf16[4,128,1024]{2,1,0:T(8,128)(2,1)}, bf16[144,2048]{1,0:T(8,128)(2,1)}, bf16[128,2048]{1,0:T(8,128)(2,1)}, bf16[128,2048]{1,0:T(8,128)(2,1)}, f32[...) custom-call(s32[8]{0:T(128)} %bitcast_subtract_fusion.starts_ref, ...), custom_call_target="tpu_custom_call" | custom-call | tf_op jit(solution)/shard_map/front/pallas_call | solution.py:516
  53.1 0.0 all-gather.3.cloned.1.call-done
  53.1 86.9 %core.1 = (f32[128,1024]{1,0:T(8,128)}, f32[128,1024]{1,0:T(8,128)}, bf16[128,4096]{1,0:T(8,128)(2,1)}, bf16[256,1024]{1,0:T(8,128)(2,1)}, bf16[192,256]{1,0:T(8,128)(2,1)}, /*index=5*/f32[8,128]{1,0:T(8,128)}) custom-call(s32[8]{0:T(128)} %bitcast_subtract_fusion.starts_ref, bf16[128,1024]{1,0:T(8,128)(2,1)} %bitcast.49, bf16[128,1024]{1,0:T(8,128)(2,1)} %bitcast.46, ...), custom_call_target="tpu_custom_call" | custom-call | tf_op jit(solution)/shard_map/core/pallas_call | solution.py:1170
  140.0 1.2 slice.3
  141.2 0.0 copy-start
  141.2 11.2 %update.1 = (f32[1,128]{1,0:T(1,128)}, f32[1,128]{1,0:T(1,128)}, f32[1,128]{1,0:T(1,128)}, f32[128,4096]{1,0:T(8,128)}, f32[128,4096]{1,0:T(8,128)}, /*index=5*/...) custom-call(s32[1]{0:T(128)} %bitcast.14.member_ref, ...), custom_call_target="tpu_custom_call" | custom-call | tf_op jit(solution)/shard_map/update/pallas_call | solution.py:1300
  152.4 1.9 %copy.68 = f32[1,128,1024]{2,1,0:T(8,128)} copy(f32[1,128,1024]{2,1,0:T(8,128)} %bitcast.51) | data formatting | bytes 1048576
  154.3 0.0 copy-done
  154.3 0.8 copy.69
Async XLA Ops:
  7.2 45.9 %all-gather.3.cloned.1.call-start = ((), (), s32[]{:S(2)}) async-start(), calls=%async_computation | async-start | bytes 2359296 | tf_op jit(solution)/shard_map/all_gather | solution.py:1411
  141.2 13.1 %copy-start = (f32[128,1024]{1,0:T(8,128)S(1)}, f32[128,1024]{1,0:T(8,128)}, u32[]{:S(2)}) copy-start(f32[128,1024]{1,0:T(8,128)} %get-tuple-element.98) | copy-start | bytes 1572868
Sparse Core Ops, SparseCore 0:
  9.6 40.2 all-gather.2

commit v4 on v3

--- a/solution.py
+++ b/solution.py
@@ -575,35 +575,22 @@
     return values * sigmoid_of, sigmoid_of * (1.0 + values * (1.0 - sigmoid_of))
 
 
-def core_kernel(
+def block_kernel(
     nrows,
     devices,
-    starts_ref,
+    lengths_ref,
     tokens_ref,
     cot_ref,
     gain_ref,
     in_proj_ref,
     out_proj_ref,
     conv_ref,
+    cbias_ref,
     x_proj_ref,
     dt_proj_ref,
+    dtbias_ref,
+    alog_ref,
     dskip_ref,
-    rates_ref,
-    normed_ref,
-    inner_ref,
-    gates_ref,
-    back_ref,
-    pre_act_ref,
-    delta_pre_ref,
-    ddec_ref,
-    drive_ref,
-    grady_ref,
-    rank_ref,
-    inb_ref,
-    outb_ref,
-    all_ref,
-    sums_ref,
-    cot_all_ref,
     output_ref,
     grad_ref,
     gin_out,
@@ -612,8 +599,29 @@
     norm_out,
     in_proj_buf,
     out_proj_buf,
+    rates_ref,
+    normed_rows,
+    normed_sib,
+    cot_rows,
+    cot_sib,
+    inner,
+    gates,
+    back,
+    pre_act,
+    delta_pre,
+    ddec,
+    drive,
+    grady,
+    proj,
+    rank_low,
+    inb,
+    outb,
+    ends,
+    ends_all,
+    sums_all,
     docid,
     masks,
+    padded,
     kept,
     first,
     second,
@@ -622,12 +630,9 @@
     gated,
     back_gates,
     back_inner,
-    grad_act,
     grad_conv,
-    padded,
     rank_back,
     proj_back,
-    normed_sib,
     gated_got,
     back_got,
     gout_sum,
@@ -642,17 +647,22 @@
     small_got,
     small_part,
     small_seq,
-    norm_seq,
-    norm_rows,
+    norm_part,
+    norm_all,
     loads,
+    halo_wires,
+    state_wires,
+    sum_wires,
+    gather_wires,
     sib_wires,
-    halo_wires,
     gated_wires,
     back_wires,
+    gout_wires,
     line_wires,
     plane_wires,
     row_wires,
     seq_wires,
+    norm_wires,
     local,
 ):
     row = lax.axis_index("rows")
@@ -664,12 +674,13 @@
     chunk = 4 * LANES
     chunks = E // chunk
     shard = E // devices
-    halo = inner_ref.shape[0] - steps
+    halo = inner.shape[0] - steps
     reach = devices // 2
     half = N // 2
     low = jnp.bfloat16
     wide = jnp.float32
     spans = packed_rows()
+    everyone = nrows * devices
 
     in_loads = [
         pltpu.make_async_copy(
@@ -712,31 +723,218 @@
         for copy in copies:
             copy.wait()
 
+    def other_device(offset):
+        return {
+            "rows": lax.rem(row + offset // devices, nrows),
+            "seq": lax.rem(member + offset % devices, devices),
+        }
+
     barrier = pltpu.get_barrier_semaphore()
-    greeted = [{"seq": partner("seq", offset)} for offset in range(1, devices)]
-    greeted += [plane(turn, other) for turn in range(1, nrows) for other in range(2)]
-    for device in greeted:
-        pl.semaphore_signal(barrier, inc=1, device_id=device, device_id_type=MESH)
+    for offset in range(1, everyone):
+        pl.semaphore_signal(
+            barrier, inc=1, device_id=other_device(offset), device_id_type=MESH
+        )
+
+    def column_sum(values):
+        return jnp.sum(values, axis=0, keepdims=True)
+
+    stream = tokens_ref[...].astype(wide)
+    inverse = lax.rsqrt(jnp.mean(stream * stream, axis=1, keepdims=True) + EPS)
+    normed_rows[row] = (stream * inverse * gain_ref[...]).astype(low)
+    cot_rows[row] = cot_ref[...]
+    rates_ref[...] = jnp.exp(alog_ref[...]) * (-1.0 / math.log(2.0))
 
     places = member * steps - 8 + lax.broadcasted_iota(jnp.int32, docid.shape, 0)
     count = jnp.zeros(docid.shape, jnp.int32)
-    for index in range(starts_ref.shape[0]):
-        count = count + jnp.where(places >= starts_ref[index], 1, 0)
+    starting = jnp.zeros(docid.shape, wide)
+    start = 0
+    for index in range(lengths_ref.shape[1]):
+        count = count + jnp.where(places >= start, 1, 0)
+        starting = jnp.where(places == start, 1.0, starting)
+        start = start + lengths_ref[0, index]
     docid[...] = count
+    masks[0] = starting[8:]
     for offset in range(1, K):
         masks[offset] = jnp.where(
             docid[8 - offset : 16 - offset + steps, :] == docid[8:, :], 1.0, 0.0
         )
+
+    def project(at):
+        in_loads[at].wait()
+        return jnp.dot(
+            normed_rows[row], in_proj_buf[at], preferred_element_type=wide
+        ).astype(low)
+
+    for at in range(chunks):
+        inner[halo:, span(at, chunk)] = project(at)
+    pl.semaphore_wait(barrier, everyone - 1)
+    halo_copy = remote(
+        inner.at[steps : steps + halo, :],
+        inner.at[0:halo, :],
+        halo_wires.at[0, 0],
+        halo_wires.at[0, 1],
+        {"seq": partner("seq", 1)},
+    )
+
+    @pl.when(member < devices - 1)
+    def _():
+        halo_copy.start()
+
+    @pl.when(member == 0)
+    def _():
+        inner[0:halo, :] = jnp.zeros((halo, E), low)
+
+    row_copies = begin(
+        [
+            remote(
+                source.at[row],
+                source.at[row],
+                gather_wires.at[kind, 0, offset - 1],
+                gather_wires.at[kind, 1, offset - 1],
+                {"rows": partner("rows", offset)},
+            )
+            for kind, source in ((0, normed_rows), (1, cot_rows))
+            for offset in range(1, nrows)
+        ]
+    )
+    for at in range(chunks):
+        gates[:, span(at, chunk)] = project(chunks + at)
+    out_load.wait()
+    for at in range(chunks):
+        back[:, span(at, chunk)] = lax.dot_general(
+            cot_ref[...],
+            out_proj_buf[span(at, chunk), :],
+            (((1,), (1,)), ((), ())),
+            preferred_element_type=wide,
+        ).astype(low)
+
     gin[...] = jnp.zeros_like(gin)
     gout[...] = jnp.zeros_like(gout)
     rank_back[...] = jnp.zeros_like(rank_back)
     small[...] = jnp.zeros_like(small)
-    pl.semaphore_wait(barrier, len(greeted))
-
-    normed_copy = remote(
-        normed_ref, normed_sib, sib_wires.at[0], sib_wires.at[1], {"seq": 2 * level + 1 - side}
-    )
-    normed_copy.start()
+    norm_part[...] = jnp.zeros_like(norm_part)
+    proj[...] = jnp.zeros_like(proj)
+
+    @pl.when(member < devices - 1)
+    def _():
+        halo_copy.wait_send()
+
+    @pl.when(member > 0)
+    def _():
+        halo_copy.wait_recv()
+
+    for at in range(chunks):
+        lows = []
+        for group in range(4 * at, 4 * at + 4):
+            columns = span(group, LANES)
+            padded[...] = inner[halo - 8 :, columns].astype(wide)
+            value = cbias_ref[:, columns] + conv_ref[0:1, columns] * padded[8:, :]
+            for offset in range(1, K):
+                value = (
+                    value
+                    + conv_ref[offset : offset + 1, columns]
+                    * padded[8 - offset : 8 - offset + steps, :]
+                    * masks[offset, :steps, :]
+                )
+            pre_act[group] = value
+            act = silu(value)
+            drive[group] = act
+            lows.append(act.astype(low))
+        proj[...] += lax.dot_general(
+            jnp.concatenate(lows, axis=1),
+            x_proj_ref[:, span(at, chunk)],
+            (((1,), (1,)), ((), ())),
+            preferred_element_type=wide,
+        )
+    rank_low[...] = proj[:, :R].astype(low)
+    inb[...] = jnp.broadcast_to(proj[:, R : R + N][:, :, None], inb.shape)
+    outb[...] = jnp.broadcast_to(proj[:, R + N :][:, :, None], outb.shape)
+
+    def state_copy(direction, distance, at):
+        offset = distance if direction == 0 else devices - distance
+        return remote(
+            ends.at[direction, at],
+            ends_all.at[member, at],
+            state_wires.at[direction, 0, at, distance - 1],
+            state_wires.at[direction, 1, at, distance - 1],
+            {"seq": partner("seq", offset)},
+        )
+
+    def sum_copy(direction, distance):
+        offset = distance if direction == 0 else devices - distance
+        return remote(
+            sums_all.at[member],
+            sums_all.at[member],
+            sum_wires.at[direction, 0, distance - 1],
+            sum_wires.at[direction, 1, distance - 1],
+            {"seq": partner("seq", offset)},
+        )
+
+    def to_neighbours(make):
+        for distance in range(1, reach + 1):
+
+            @pl.when(member + distance < devices)
+            def _():
+                make(0, distance).start()
+
+            @pl.when(member >= distance)
+            def _():
+                make(1, distance).start()
+
+    def from_neighbours(make):
+        for distance in range(1, reach + 1):
+
+            @pl.when(member + distance < devices)
+            def _():
+                make(0, distance).wait_send()
+                make(1, distance).wait_recv()
+
+            @pl.when(member >= distance)
+            def _():
+                make(1, distance).wait_send()
+                make(0, distance).wait_recv()
+
+    for at in range(chunks):
+        pre = (
+            jnp.dot(rank_low[...], dt_proj_ref[:, span(at, chunk)], preferred_element_type=wide)
+            + dtbias_ref[:, span(at, chunk)]
+        )
+        for place in range(4):
+            group = 4 * at + place
+            columns = span(group, LANES)
+            here = pre[:, place * LANES : (place + 1) * LANES]
+            delta = softplus(here)
+            delta_pre[group] = here
+            drive[group] = drive[group] * delta
+            decaying = jnp.where(masks[0, :steps, :] > 0.0, RESET, delta)
+            ddec[group] = decaying
+            sums_all[member, group : group + 1, :] = column_sum(decaying)
+            grady[group] = back[:, columns].astype(wide) * silu(gates[:, columns].astype(wide))
+    to_neighbours(sum_copy)
+    zeros = [jnp.zeros((N, LANES), wide) for _ in range(4)]
+    ones = [jnp.ones((N, LANES), wide) for _ in range(4)]
+    for at in range(chunks):
+
+        def step(t, carry):
+            hidden, decayed, pulled = carry
+            in_row, out_row = inb[t], outb[t]
+            new = ([], [], [])
+            for place in range(4):
+                here = (4 * at + place, pl.ds(t, 1))
+                decay = jnp.exp2(ddec[here] * rates_ref[:, span(4 * at + place, LANES)])
+                new[0].append(decay * hidden[place] + drive[here] * in_row)
+                product = decay * decayed[place]
+                new[1].append(product)
+                new[2].append(pulled[place] + product * (grady[here] * out_row))
+            return new
+
+        hidden, _, pulled = lax.fori_loop(0, steps, step, (zeros, ones, zeros), unroll=4)
+        ends[0, at] = jnp.concatenate(hidden, axis=1).astype(low)
+        ends[1, at] = jnp.concatenate(pulled, axis=1).astype(low)
+        to_neighbours(lambda direction, distance: state_copy(direction, distance, at))
+    from_neighbours(sum_copy)
+    for at in range(chunks):
+        from_neighbours(lambda direction, distance: state_copy(direction, distance, at))
 
     def fold(values):
         return values[:half] + values[half:]
@@ -749,9 +947,6 @@
 
     def lanes(at, place):
         return share(4 * at + place, LANES)
-
-    def column_sum(values):
-        return jnp.sum(values, axis=0, keepdims=True)
 
     def trade(kind, source, at, turn):
         copies = []
@@ -774,167 +969,102 @@
                 )
         return begin(copies)
 
-    def gated_copy(target_member):
-        return remote(
-            gated.at[:, share(target_member, shard)],
-            gated_got.at[share(member, steps), :],
-            gated_wires.at[0, target_member],
-            gated_wires.at[1, member],
-            {"seq": target_member},
-        )
-
-    gate_moves = []
+    def trade_gated(at, turn):
+        copies = []
+        for jump in (turn % 2, turn % 2 + 2):
+            for other in range(2):
+                receiver = lax.rem(row + jump, nrows)
+                columns = share(
+                    4 * at + 2 * lax.rem(side + other, 2) + receiver // 2, LANES
+                )
+                target = gated_got.at[at // 2, other, row]
+                if jump == 0 and other == 0:
+                    copies.append(
+                        pltpu.make_async_copy(
+                            gated.at[:, columns], target, local.at[2 + turn // 2]
+                        )
+                    )
+                else:
+                    copies.append(
+                        remote(
+                            gated.at[:, columns],
+                            target,
+                            gated_wires.at[0, at // 2, 2 * jump + other],
+                            gated_wires.at[1, at // 2, 2 * jump + other],
+                            plane(jump, other),
+                        )
+                    )
+        return begin(copies)
+
+    gate_moves, gated_moves = [], []
     order = [(turn, lax.rem(row + turn, nrows)) for turn in [*range(1, nrows), 0]]
-    for turn, at in order:
+    leavings = []
+    for slot, (turn, at) in enumerate(order):
 
         def through(device, states):
             new = []
             for place in range(4):
-                total = sums_ref[device, pl.ds(4 * at + place, 1), :]
+                total = sums_all[device, pl.ds(4 * at + place, 1), :]
                 factor = jnp.exp2(total * rates_ref[:, lanes(at, place)])
                 new.append(
                     factor * states[place]
-                    + all_ref[device, at, :, place * LANES : (place + 1) * LANES].astype(wide)
+                    + ends_all[device, at, :, place * LANES : (place + 1) * LANES].astype(wide)
                 )
             return new
 
         def forward(t, hidden):
-            in_row, out_row = inb_ref[t], outb_ref[t]
+            in_row, out_row = inb[t], outb[t]
             new = []
             for place in range(4):
                 here = (4 * at + place, pl.ds(t, 1))
-                decay = jnp.exp2(ddec_ref[here] * rates_ref[:, lanes(at, place)])
-                state = decay * hidden[place] + drive_ref[here] * in_row
-                kept[t + 1, place] = state
+                decay = jnp.exp2(ddec[here] * rates_ref[:, lanes(at, place)])
+                state = decay * hidden[place] + drive[here] * in_row
+                kept[slot, t + 1, place] = state.astype(low)
                 first[place, share(t, half), :] = fold(state * out_row)
                 new.append(state)
             return new
 
-        def backward(back, carry):
-            later, grates = carry
-            t = steps - 1 - back
-            in_row, out_row = inb_ref[t], outb_ref[t]
-            gin_row, gout_row = gin[t], gout[t]
-            new = ([], [])
-            for place in range(4):
-                here = (4 * at + place, pl.ds(t, 1))
-                grady = grady_ref[here]
-                delta = ddec_ref[here]
-                rates = rates_ref[:, lanes(at, place)]
-                adjoint = grady * out_row + later[place]
-                gout_row = gout_row + grady * kept[t + 1, place]
-                gin_row = gin_row + adjoint * drive_ref[here]
-                first[place, share(t, half), :] = fold(adjoint * in_row)
-                passed = jnp.exp2(delta * rates) * adjoint
-                pulled = passed * kept[t, place]
-                second[place, share(t, half), :] = fold(pulled * rates)
-                new[0].append(passed)
-                new[1].append(grates[place] + pulled * delta)
-            gin[t] = gin_row
-            gout[t] = gout_row
-            return new
-
-        zeros = [jnp.zeros((N, LANES), wide) for _ in range(4)]
         entering = lax.fori_loop(jnp.maximum(member - reach, 0), member, through, zeros)
         last = jnp.minimum(member + reach, devices - 1)
-        leaving = lax.fori_loop(0, last - member, lambda d, s: through(last - d, s), zeros)
+        leavings.append(lax.fori_loop(0, last - member, lambda d, s: through(last - d, s), zeros))
         for place in range(4):
-            kept[0, place] = entering[place]
+            kept[slot, 0, place] = entering[place].astype(low)
         lax.fori_loop(0, steps, forward, entering, unroll=4)
         for place in range(4):
             group, columns = 4 * at + place, lanes(at, place)
-            act = silu(pre_act_ref[group])
+            act = silu(pre_act[group])
             y_full = collapse(first, place) + dskip_ref[:, columns] * act
-            gate, slope = silu_pair(gates_ref[:, columns].astype(wide))
+            gate, slope = silu_pair(gates[:, columns].astype(wide))
             gated[:, columns] = (y_full * gate).astype(low)
-            back_gates[:, columns] = (
-                back_ref[:, columns].astype(wide) * y_full * slope
-            ).astype(low)
-            small[spans[6][0] : spans[6][1], columns] = column_sum(grady_ref[group] * act)
+            back_gates[:, columns] = (back[:, columns].astype(wide) * y_full * slope).astype(low)
+            small[spans[6][0] : spans[6][1], columns] = column_sum(grady[group] * act)
         gate_moves += trade(1, back_gates, at, turn)
-        for core in range(2):
-
-            @pl.when(2 * at + core != member)
-            def _():
-                gated_copy(2 * at + core).start()
-
-        _, grates = lax.fori_loop(0, steps, backward, (leaving, zeros), unroll=4)
-        lows = []
-        for place in range(4):
-            group, columns = 4 * at + place, lanes(at, place)
-            along = collapse(first, place)
-            delta_pre = delta_pre_ref[group]
-            act = silu(pre_act_ref[group])
-            grad_delta = along * act + collapse(second, place) * math.log(2.0)
-            pre_low = (grad_delta * jax.nn.sigmoid(delta_pre)).astype(low)
-            lows.append(pre_low)
-            grad_act[group] = grady_ref[group] * dskip_ref[:, columns] + along * softplus(delta_pre)
-            small[spans[5][0] : spans[5][1], columns] = column_sum(pre_low.astype(wide))
-            small[spans[2][0] : spans[2][1], columns] = (
-                grates[place] * rates_ref[:, columns] * math.log(2.0)
+        gated_moves += trade_gated(at, turn)
+
+    settle(row_copies)
+    sib_moves = begin(
+        [
+            remote(
+                source,
+                target,
+                sib_wires.at[kind, 0],
+                sib_wires.at[kind, 1],
+                {"seq": 2 * level + 1 - side},
             )
-        lows = jnp.concatenate(lows, axis=1)
-        rank_back[...] += lax.dot_general(
-            lows,
-            dt_proj_ref[:, share(at, chunk)],
-            (((1,), (1,)), ((), ())),
-            preferred_element_type=wide,
-        )
-        small[spans[1][0] : spans[1][1], share(at, chunk)] = lax.dot_general(
-            rank_ref[...], lows, (((0,), (0,)), ((), ())), preferred_element_type=wide
-        )
-
-    gated_got[share(member, steps), :] = gated[:, share(member, shard)]
-    for offset in range(1, devices):
-        gated_copy(partner("seq", offset)).wait_send()
-        source = partner("seq", offset)
-        remote(
-            gated.at[:, share(member, shard)],
-            gated_got.at[share(source, steps), :],
-            gated_wires.at[0, member],
-            gated_wires.at[1, source],
-            {"seq": source},
-        ).wait_recv()
-
-    def to_rows(kind, make):
-        return begin(
-            [
-                remote(
-                    *make(partner("rows", offset), offset - 1),
-                    row_wires.at[kind, 0, offset - 1],
-                    row_wires.at[kind, 1, offset - 1],
-                    {"rows": partner("rows", offset)},
-                )
-                for offset in range(1, nrows)
-            ]
-        )
-
-    def to_seq(kind, make):
-        return begin(
-            [
-                remote(
-                    *make(partner("seq", offset), offset - 1),
-                    seq_wires.at[kind, 0, offset - 1],
-                    seq_wires.at[kind, 1, offset - 1],
-                    {"seq": partner("seq", offset)},
-                )
-                for offset in range(1, devices)
-            ]
-        )
-
-    def squares(values):
-        return jnp.sum(jnp.sum(values * values, axis=0, keepdims=True), axis=1, keepdims=True)
+            for kind, source, target in ((0, normed_rows, normed_sib), (1, cot_rows, cot_sib))
+        ]
+    )
 
     def in_grads(kind):
-        total = jnp.zeros((D, shard), wide)
-        for other, normed in ((0, normed_ref), (1, normed_sib)):
-            for source in range(nrows):
-                total = total + lax.dot_general(
-                    normed[source],
-                    back_got[kind, other, source],
-                    (((0,), (0,)), ((), ())),
-                    preferred_element_type=wide,
-                )
+        total = None
+        for other, normed in ((0, normed_rows), (1, normed_sib)):
+            part = lax.dot_general(
+                normed[...].reshape(nrows * steps, D),
+                back_got[kind, other].reshape(nrows * steps, shard),
+                (((0,), (0,)), ((), ())),
+                preferred_element_type=wide,
+            )
+            total = part if total is None else total + part
         gin_sum[kind] = total
         gin_low[kind] = total.astype(low)
         return begin(
@@ -950,6 +1080,9 @@
             ]
         )
 
+    def squares(values):
+        return jnp.sum(jnp.sum(values * values, axis=0, keepdims=True), axis=1, keepdims=True)
+
     def in_share(kind):
         total = gin_sum[kind, share(level, D // levels), :]
         for turn in range(levels - 1):
@@ -958,31 +1091,187 @@
         owned = D // devices
         columns = share(kind * devices + 2 * row + side, shard)
         gin_out[:, columns] = gin_pub[kind, share(side, owned), :]
-        copies = [
-            remote(
-                gin_pub.at[kind, share(lax.rem(side + other, 2), owned), :],
-                gin_out.at[:, columns],
-                plane_wires.at[kind, 0, 2 * turn + other],
-                plane_wires.at[kind, 1, 2 * turn + other],
-                plane(turn, other),
+        copies = begin(
+            [
+                remote(
+                    gin_pub.at[kind, share(lax.rem(side + other, 2), owned), :],
+                    gin_out.at[:, columns],
+                    plane_wires.at[kind, 0, 2 * turn + other],
+                    plane_wires.at[kind, 1, 2 * turn + other],
+                    plane(turn, other),
+                )
+                for turn in range(nrows)
+                for other in range(2)
+                if turn + other > 0
+            ]
+        )
+        norm_part[...] += squares(total)
+        return copies
+
+    summing = lax.rem(level, 2) == lax.rem(row, 2)
+    idle = lax.rem(level, 2) != lax.rem(row, 2)
+
+    def gout_copy(turn):
+        return remote(
+            gout_low.at[lax.rem(level + turn, levels) // 2],
+            gout_got.at[turn - 1],
+            gout_wires.at[0, turn - 1],
+            gout_wires.at[1, turn - 1],
+            line(turn),
+        )
+
+    def gout_share_copy(turn):
+        rows_of = gout_out.at[share(row // 2, LANES), :]
+        return remote(
+            rows_of,
+            rows_of,
+            row_wires.at[2, 0, turn - 1],
+            row_wires.at[2, 1, turn - 1],
+            {"rows": partner("rows", turn)},
+        )
+
+    def out_grads():
+        for piece in range(2):
+            total = None
+            for other, cots in ((0, cot_rows), (1, cot_sib)):
+                part = lax.dot_general(
+                    gated_got[piece, other].reshape(nrows * steps, LANES),
+                    cots[...].reshape(nrows * steps, D),
+                    (((0,), (0,)), ((), ())),
+                    preferred_element_type=wide,
+                )
+                total = part if total is None else total + part
+            gout_sum[piece] = total
+            gout_low[piece] = total.astype(low)
+
+        @pl.when(summing)
+        def _():
+            gout_copy(2).start()
+
+        @pl.when(idle)
+        def _():
+            gout_copy(1).start()
+            gout_copy(3).start()
+
+    def out_share():
+        @pl.when(idle)
+        def _():
+            gout_copy(1).wait_send()
+            gout_copy(3).wait_send()
+
+        @pl.when(summing)
+        def _():
+            gout_copy(2).wait_send()
+            for turn in range(1, levels):
+                gout_copy(turn).wait_recv()
+            total = gout_sum[level // 2]
+            for turn in range(levels - 1):
+                total = total + gout_got[turn].astype(wide)
+            gout_out[share(row // 2, LANES), :] = total.astype(low)
+            norm_part[...] += squares(total)
+            for turn in range(1, nrows):
+                gout_share_copy(turn).start()
+
+    def out_end():
+        @pl.when(summing)
+        def _():
+            for turn in range(1, nrows):
+                gout_share_copy(turn).wait_send()
+            gout_share_copy(2).wait_recv()
+
+        @pl.when(idle)
+        def _():
+            gout_share_copy(1).wait_recv()
+            gout_share_copy(3).wait_recv()
+
+    for slot, (turn, at) in enumerate(order):
+
+        def backward(back_step, carry):
+            later, grates, states = carry
+            t = steps - 1 - back_step
+            in_row, out_row = inb[t], outb[t]
+            gin_row, gout_row = gin[t], gout[t]
+            new = ([], [], [])
+            for place in range(4):
+                here = (4 * at + place, pl.ds(t, 1))
+                grad_y = grady[here]
+                delta = ddec[here]
+                rates = rates_ref[:, lanes(at, place)]
+                before = kept[slot, t, place].astype(wide)
+                adjoint = grad_y * out_row + later[place]
+                gout_row = gout_row + grad_y * states[place]
+                gin_row = gin_row + adjoint * drive[here]
+                first[place, share(t, half), :] = fold(adjoint * in_row)
+                passed = jnp.exp2(delta * rates) * adjoint
+                pulled = passed * before
+                second[place, share(t, half), :] = fold(pulled * rates)
+                new[0].append(passed)
+                new[1].append(grates[place] + pulled * delta)
+                new[2].append(before)
+            gin[t] = gin_row
+            gout[t] = gout_row
+            return new
+
+        ending = [kept[slot, steps, place].astype(wide) for place in range(4)]
+        _, grates, _ = lax.fori_loop(
+            0, steps, backward, (leavings[slot], zeros, ending), unroll=4
+        )
+        lows = []
+        for place in range(4):
+            group, columns = 4 * at + place, lanes(at, place)
+            along = collapse(first, place)
+            here = delta_pre[group]
+            act = silu(pre_act[group])
+            grad_delta = along * act + collapse(second, place) * math.log(2.0)
+            pre_low = (grad_delta * jax.nn.sigmoid(here)).astype(low)
+            lows.append(pre_low)
+            drive[group] = grady[group] * dskip_ref[:, columns] + along * softplus(here)
+            small[spans[5][0] : spans[5][1], columns] = column_sum(pre_low.astype(wide))
+            small[spans[2][0] : spans[2][1], columns] = (
+                grates[place] * rates_ref[:, columns] * math.log(2.0)
             )
-            for turn in range(nrows)
-            for other in range(2)
-            if turn + other > 0
-        ]
-        return begin(copies), squares(total)
-
-    outer = gout_out.shape[0] // nrows
-    gout_sum[...] = lax.dot_general(
-        gated_got[...], cot_all_ref[...], (((0,), (0,)), ((), ())), preferred_element_type=wide
-    )
-    gout_low[...] = gout_sum[...].astype(low)
-    gout_moves = to_rows(
-        0, lambda other, at: (gout_low.at[share(other, outer), :], gout_got.at[at])
-    )
-    normed_copy.wait()
-    settle(gate_moves)
-    gate_moves = in_grads(1)
+        lows = jnp.concatenate(lows, axis=1)
+        rank_back[...] += lax.dot_general(
+            lows,
+            dt_proj_ref[:, share(at, chunk)],
+            (((1,), (1,)), ((), ())),
+            preferred_element_type=wide,
+        )
+        small[spans[1][0] : spans[1][1], share(at, chunk)] = lax.dot_general(
+            rank_low[...], lows, (((0,), (0,)), ((), ())), preferred_element_type=wide
+        )
+        if slot == chunks - 2:
+            settle(gate_moves)
+            settle(sib_moves)
+            gate_moves = in_grads(1)
+            settle(gated_moves)
+            out_grads()
+
+    def to_rows(kind, make):
+        return begin(
+            [
+                remote(
+                    *make(partner("rows", offset), offset - 1),
+                    row_wires.at[kind, 0, offset - 1],
+                    row_wires.at[kind, 1, offset - 1],
+                    {"rows": partner("rows", offset)},
+                )
+                for offset in range(1, nrows)
+            ]
+        )
+
+    def to_seq(kind, make):
+        return begin(
+            [
+                remote(
+                    *make(partner("seq", offset), offset - 1),
+                    seq_wires.at[kind, 0, offset - 1],
+                    seq_wires.at[kind, 1, offset - 1],
+                    {"seq": partner("seq", offset)},
+                )
+                for offset in range(1, devices)
+            ]
+        )
 
     proj_back[:, :R] = rank_back[...].astype(low)
     proj_back[:, R : R + N] = jnp.sum(gin[...], axis=2).astype(low)
@@ -994,10 +1283,10 @@
         lows = []
         for place in range(4):
             group = 4 * at + place
-            act, slope = silu_pair(pre_act_ref[group])
+            act, slope = silu_pair(pre_act[group])
             lows.append(act.astype(low))
             grad_conv[group, :steps, :] = (
-                grad_act[group] + pulled[:, place * LANES : (place + 1) * LANES]
+                drive[group] + pulled[:, place * LANES : (place + 1) * LANES]
             ) * slope
         small[spans[0][0] : spans[0][1], span(at, chunk)] = lax.dot_general(
             proj_back[...],
@@ -1005,29 +1294,25 @@
             (((0,), (0,)), ((), ())),
             preferred_element_type=wide,
         )
-    halo_copy = remote(
+    halo_back = remote(
         grad_conv.at[:, 0:8, :],
         grad_conv.at[:, steps : steps + 8, :],
-        halo_wires.at[0],
-        halo_wires.at[1],
+        halo_wires.at[1, 0],
+        halo_wires.at[1, 1],
         {"seq": partner("seq", devices - 1)},
     )
 
     @pl.when(member > 0)
     def _():
-        halo_copy.start()
+        halo_back.start()
 
     @pl.when(member == devices - 1)
     def _():
         grad_conv[:, steps : steps + 8, :] = jnp.zeros((groups, 8, LANES), wide)
 
-    out_load.wait()
-    stream = tokens_ref[...].astype(wide)
     output_ref[...] = stream + jnp.dot(
         gated[...], out_proj_buf[...], preferred_element_type=wide
     )
-    for load in in_loads:
-        load.wait()
     grad_normed = jnp.zeros((steps, D), wide)
     for at in range(chunks):
         grad_normed = grad_normed + lax.dot_general(
@@ -1039,17 +1324,17 @@
 
     @pl.when(member > 0)
     def _():
-        halo_copy.wait_send()
+        halo_back.wait_send()
 
     @pl.when(member < devices - 1)
     def _():
-        halo_copy.wait_recv()
+        halo_back.wait_recv()
 
     inner_moves = []
     for turn, at in order:
         for place in range(4):
             group, columns = 4 * at + place, lanes(at, place)
-            padded[...] = inner_ref[halo - 8 :, columns].astype(wide)
+            padded[...] = inner[halo - 8 :, columns].astype(wide)
             here = grad_conv[group, :steps, :]
             pulled = conv_ref[0:1, columns] * here
             small[spans[4][0] : spans[4][1], columns] = column_sum(here)
@@ -1080,6 +1365,11 @@
         small[spans[7][0] : spans[7][1], index * shard : index * shard + owned] = grad_gain[
             :, index * owned : (index + 1) * owned
         ]
+    few = small_low.shape[0] // nrows
+    small_low[...] = small[...].astype(low)
+    small_moves = to_rows(
+        0, lambda other, at: (small_low.at[share(other, few), :], small_got.at[at])
+    )
     scaled = grad_normed * gain_ref[...]
     grad_ref[...] = (
         cot_ref[...].astype(wide)
@@ -1090,25 +1380,6 @@
         * inverse
         * jnp.mean(scaled * stream, axis=1, keepdims=True)
     )
-    few = small_low.shape[0] // nrows
-    small_low[...] = small[...].astype(low)
-    small_moves = to_rows(
-        1, lambda other, at: (small_low.at[share(other, few), :], small_got.at[at])
-    )
-
-    settle(gout_moves)
-    total = gout_sum[share(row, outer), :]
-    for at in range(nrows - 1):
-        total = total + gout_got[at].astype(wide)
-    gout_out[share(row, outer), :] = total.astype(low)
-    gout_moves = to_rows(
-        2,
-        lambda other, at: (
-            gout_out.at[share(row, outer), :],
-            gout_out.at[share(row, outer), :],
-        ),
-    )
-    norm = squares(total)
 
     settle(inner_moves)
     inner_moves = in_grads(0)
@@ -1121,10 +1392,9 @@
     small_moves = to_seq(
         0, lambda other, at: (small_part.at[:, share(other, shard)], small_seq.at[at])
     )
-
+    out_share()
     settle(gate_moves)
-    gate_moves, part = in_share(1)
-    norm = norm + part
+    gate_moves = in_share(1)
 
     settle(small_moves)
     total = small_part[:, share(member, shard)].astype(wide)
@@ -1132,34 +1402,47 @@
         total = total + small_seq[at].astype(wide)
     small_out[share(row, few), :] = total.astype(low)
     small_moves = to_rows(
-        3,
+        1,
         lambda other, at: (
             small_out.at[share(row, few), :],
             small_out.at[share(row, few), :],
         ),
     )
-    norm = norm + squares(total)
+    norm_part[...] += squares(total)
 
     settle(inner_moves)
-    inner_moves, part = in_share(0)
-    norm_seq[member] = jnp.broadcast_to(norm + part, (8, LANES))
-    settle(to_seq(1, lambda other, at: (norm_seq.at[member], norm_seq.at[member])))
-    norm_rows[row] = jnp.sum(norm_seq[...], axis=0)
-    settle(to_rows(4, lambda other, at: (norm_rows.at[row], norm_rows.at[row])))
-    norm_out[...] = jnp.sqrt(jnp.sum(norm_rows[...], axis=0))
-    settle(gout_moves)
+    inner_moves = in_share(0)
+    here = row * devices + member
+    norm_all[here] = jnp.broadcast_to(norm_part[...], (8, LANES))
+    norm_moves = begin(
+        [
+            remote(
+                norm_all.at[here],
+                norm_all.at[here],
+                norm_wires.at[0, offset - 1],
+                norm_wires.at[1, offset - 1],
+                other_device(offset),
+            )
+            for offset in range(1, everyone)
+        ]
+    )
+    settle(norm_moves)
+    norm_out[...] = jnp.sqrt(jnp.sum(norm_all[...], axis=0))
+    out_end()
     settle(gate_moves)
     settle(small_moves)
     settle(inner_moves)
 
 
-def core_of(operands, nrows, devices):
+def block_of(operands, nrows, devices):
     steps = operands[1].shape[0]
     groups = E // LANES
     chunk = 4 * LANES
     chunks = E // chunk
     levels = devices // 2
+    reach = devices // 2
     shard = E // devices
+    halo = 16
     low, wide = jnp.bfloat16, jnp.float32
     few = PACKED_ROWS // nrows
     vmem = pl.BlockSpec(memory_space=pltpu.VMEM)
@@ -1167,8 +1450,13 @@
     specs[0] = pl.BlockSpec(memory_space=pltpu.SMEM)
     specs[4] = specs[5] = pl.BlockSpec(memory_space=pl.ANY)
     dma = pltpu.SemaphoreType.DMA
+    grouped = pltpu.VMEM((groups, steps, LANES), wide)
+    flat = pltpu.VMEM((steps, E), low)
+    spread = pltpu.VMEM((steps, N, LANES), wide)
+    gathered = pltpu.VMEM((nrows, steps, D), low)
+    folded = pltpu.VMEM((4, steps * N // 2, LANES), wide)
     return pl.pallas_call(
-        functools.partial(core_kernel, nrows, devices),
+        functools.partial(block_kernel, nrows, devices),
         in_specs=specs,
         out_specs=[vmem] * 6,
         out_shape=[
@@ -1182,27 +1470,45 @@
         scratch_shapes=[
             pltpu.VMEM((2 * chunks, D, chunk), low),
             pltpu.VMEM((E, D), low),
+            pltpu.VMEM((N, E), wide),
+            gathered,
+            gathered,
+            gathered,
+            gathered,
+            pltpu.VMEM((steps + halo, E), low),
+            flat,
+            flat,
+            grouped,
+            grouped,
+            grouped,
+            grouped,
+            grouped,
+            pltpu.VMEM((steps, R + 2 * N), wide),
+            pltpu.VMEM((steps, R), low),
+            spread,
+            spread,
+            pltpu.VMEM((2, chunks, N, chunk), low),
+            pltpu.VMEM((devices, chunks, N, chunk), low),
+            pltpu.VMEM((devices, groups, LANES), wide),
             pltpu.VMEM((steps + 16, LANES), jnp.int32),
             pltpu.VMEM((K, steps + 8, LANES), wide),
-            pltpu.VMEM((steps + 1, 4, N, LANES), wide),
-            pltpu.VMEM((4, steps * N // 2, LANES), wide),
-            pltpu.VMEM((4, steps * N // 2, LANES), wide),
-            pltpu.VMEM((steps, N, LANES), wide),
-            pltpu.VMEM((steps, N, LANES), wide),
-            pltpu.VMEM((steps, E), low),
-            pltpu.VMEM((steps, E), low),
-            pltpu.VMEM((steps, E), low),
-            pltpu.VMEM((groups, steps, LANES), wide),
+            pltpu.VMEM((steps + 8, LANES), wide),
+            pltpu.VMEM((chunks, steps + 1, 4, N, LANES), low),
+            folded,
+            folded,
+            spread,
+            spread,
+            flat,
+            flat,
+            flat,
             pltpu.VMEM((groups, steps + 8, LANES), wide),
-            pltpu.VMEM((steps + 8, LANES), wide),
             pltpu.VMEM((steps, R), wide),
             pltpu.VMEM((steps, R + 2 * N), low),
-            pltpu.VMEM((nrows, steps, D), low),
-            pltpu.VMEM((steps * devices, shard), low),
+            pltpu.VMEM((2, 2, nrows, steps, LANES), low),
             pltpu.VMEM((2, 2, nrows, steps, shard), low),
-            pltpu.VMEM((shard, D), wide),
-            pltpu.VMEM((shard, D), low),
-            pltpu.VMEM((nrows - 1, shard // nrows, D), low),
+            pltpu.VMEM((2, LANES, D), wide),
+            pltpu.VMEM((2, LANES, D), low),
+            pltpu.VMEM((levels - 1, LANES, D), low),
             pltpu.VMEM((2, D, shard), wide),
             pltpu.VMEM((2, D, shard), low),
             pltpu.VMEM((2, levels - 1, D // levels, shard), low),
@@ -1212,23 +1518,28 @@
             pltpu.VMEM((nrows - 1, few, E), low),
             pltpu.VMEM((few, E), low),
             pltpu.VMEM((devices - 1, few, shard), low),
-            pltpu.VMEM((devices, 8, LANES), wide),
-            pltpu.VMEM((nrows, 8, LANES), wide),
+            pltpu.VMEM((1, 1), wide),
+            pltpu.VMEM((nrows * devices, 8, LANES), wide),
             dma((2 * chunks + 1,)),
-            dma((2,)),
-            dma((2,)),
-            dma((2, devices)),
+            dma((2, 2)),
+            dma((2, 2, chunks, reach)),
+            dma((2, 2, reach)),
+            dma((2, 2, nrows - 1)),
+            dma((2, 2)),
             dma((2, 2, 2 * nrows)),
+            dma((2, 2, 2 * nrows)),
+            dma((2, levels - 1)),
             dma((2, 2, levels - 1)),
             dma((2, 2, 2 * nrows)),
-            dma((5, 2, nrows - 1)),
-            dma((2, 2, devices - 1)),
-            dma((2,)),
+            dma((3, 2, nrows - 1)),
+            dma((1, 2, devices - 1)),
+            dma((2, nrows * devices - 1)),
+            dma((4,)),
         ],
         compiler_params=pltpu.CompilerParams(
-            collective_id=1, has_side_effects=True, vmem_limit_bytes=62 * 2**20
+            collective_id=1, has_side_effects=True, vmem_limit_bytes=63 * 2**20
         ),
-        name="core",
+        name="block",
     )(*operands)
 
 
@@ -1370,13 +1681,74 @@
     steps = stream.shape[0]
     length = steps * devices
     cot_low = cotangent[0]
+    nrows = lax.axis_size("rows")
+    direct = devices == 2 * nrows and nrows == 4 and E == nrows * 4 * LANES
+    member_word = jnp.reshape(member_id, (1,)).astype(jnp.int32)
+    moments = (
+        moment_norm_gain,
+        moment_in_proj,
+        moment_conv_weight,
+        moment_conv_bias,
+        moment_x_proj,
+        moment_dt_proj,
+        moment_dt_bias,
+        moment_a_log,
+        moment_d_skip,
+        moment_out_proj,
+    )
+    averages = (
+        average_norm_gain,
+        average_in_proj,
+        average_conv_weight,
+        average_conv_bias,
+        average_x_proj,
+        average_dt_proj,
+        average_dt_bias,
+        average_a_log,
+        average_d_skip,
+        average_out_proj,
+    )
+    if direct:
+        weights = (
+            norm_gain,
+            in_proj,
+            conv_weight,
+            conv_bias,
+            x_proj,
+            dt_proj,
+            dt_bias,
+            a_log,
+            d_skip,
+            out_proj,
+        )
+        block_output, input_grad, gin_share, gout_share, small, norm_tile = block_of(
+            (
+                doc_lengths,
+                tokens[0],
+                cot_low,
+                norm_gain[None],
+                in_proj,
+                out_proj,
+                conv_weight,
+                conv_bias[None],
+                x_proj.T,
+                dt_proj,
+                dt_bias[None],
+                a_log,
+                d_skip[None],
+            ),
+            nrows,
+            devices,
+        )
+        updated = update_of(
+            member_word, norm_tile, gin_share, gout_share, small, weights, moments, averages
+        )
+        return (block_output[None], input_grad[None], norm_tile[0, 0], *updated)
     inverse = lax.rsqrt(jnp.mean(stream * stream, axis=1, keepdims=True) + EPS)
     rates = -jnp.exp(a_log)
     scaled_rates = rates * (1.0 / math.log(2.0))
     lengths = doc_lengths[0]
     starts = (jnp.cumsum(lengths) - lengths).astype(jnp.int32)
-    nrows = lax.axis_size("rows")
-    direct = devices == 2 * nrows and E % (2 * nrows * LANES) == 0 and E == nrows * 4 * LANES
     (
         normed,
         inner_low,
@@ -1406,83 +1778,9 @@
         dt_bias[None],
         scaled_rates,
         devices,
-        nrows if direct else 1,
+        1,
     )
     cot_all = lax.all_gather(cot_low, "seq", axis=0, tiled=True)
-    member_word = jnp.reshape(member_id, (1,)).astype(jnp.int32)
-    moments = (
-        moment_norm_gain,
-        moment_in_proj,
-        moment_conv_weight,
-        moment_conv_bias,
-        moment_x_proj,
-        moment_dt_proj,
-        moment_dt_bias,
-        moment_a_log,
-        moment_d_skip,
-        moment_out_proj,
-    )
-    averages = (
-        average_norm_gain,
-        average_in_proj,
-        average_conv_weight,
-        average_conv_bias,
-        average_x_proj,
-        average_dt_proj,
-        average_dt_bias,
-        average_a_log,
-        average_d_skip,
-        average_out_proj,
-    )
-    if direct:
-        weights = (
-            norm_gain,
-            in_proj,
-            conv_weight,
-            conv_bias,
-            x_proj,
-            dt_proj,
-            dt_bias,
-            a_log,
-            d_skip,
-            out_proj,
-        )
-        block_output, input_grad, gin_share, gout_share, small, norm_tile = core_of(
-            (
-                starts,
-                tokens[0],
-                cot_low,
-                norm_gain[None],
-                in_proj,
-                out_proj,
-                conv_weight,
-                x_proj.T,
-                dt_proj,
-                d_skip[None],
-                scaled_rates,
-                normed,
-                inner_low,
-                gates_low,
-                back_gated,
-                pre_act,
-                delta_pre,
-                ddec,
-                drive,
-                grady_rows,
-                rank_low,
-                inb,
-                outb,
-                everyone,
-                all_sums,
-                cot_all,
-            ),
-            nrows,
-            devices,
-        )
-        updated = update_of(
-            member_word, norm_tile, gin_share, gout_share, small, weights, moments, averages
-        )
-        return (block_output[None], input_grad[None], norm_tile[0, 0], *updated)
     normed_all = lax.all_gather(normed[0], "seq", axis=0, tiled=True)
     positions = member_id * steps + jnp.arange(-8, steps + 8, dtype=jnp.int32)
     docid, starting = doc_tables(doc_lengths[0], positions)

time: 162 us -> 129 us (0.80)
  the two profiles are of different devices: /device:TPU:0 before, /device:TPU:9 now
where the time goes in v4:
time: 129 us
  Pallas kernels  124 us (96%)
  local copies, waits for them, and re-layouts  3.87 us (3%)
    pallas_call x1, Pallas kernels, block_of(): pl.pallas_call(functools.partial(block_kernel, nrows, devices), in_specs=...  113 us
    pallas_call x1, Pallas kernels, update_of(): pl.pallas_call(update_kernel, grid_spec=pltpu.PrefetchScalarGridSpec(num_...  11.4 us
    unnamed x4, local copies, waits for them, and re-layouts  2.68 us

profile of v4, /device:TPU:9, one launch (start us, length us, event | category | flops | bytes accessed | tf_op | source)
XLA Modules:
  0.0 128.9 jit_solution(3269227170009561040)
XLA Ops:
  0.7 112.9 %block.1 = (f32[128,1024]{1,0:T(8,128)}, f32[128,1024]{1,0:T(8,128)}, bf16[128,4096]{1,0:T(8,128)(2,1)}, bf16[256,1024]{1,0:T(8,128)(2,1)}, bf16[192,256]{1,0:T(8,128)(2,1)}, /*index=5*/f32[8,128]{1,0:T(8,128)}) custom-call(s32[1,8]{1,0:T(1,128)} %lengths_ref.1, bf16[128,1024]{1,0:T(8,128)(2,1)} %bitcast.40, bf16[128,1024]{1,0:T(8,128)(2,1)} %bitcast.41, ...), custom_call_target="tpu_custom_call" | custom-call | tf_op jit(solution)/shard_map/block/pallas_call | solution.py:1458
  113.6 0.0 copy-start
  113.6 11.4 %update.1 = (f32[1,128]{1,0:T(1,128)}, f32[1,128]{1,0:T(1,128)}, f32[1,128]{1,0:T(1,128)}, f32[128,4096]{1,0:T(8,128)}, f32[128,4096]{1,0:T(8,128)}, /*index=5*/...) custom-call(s32[1]{0:T(128)} %bitcast.10.member_ref, ...), custom_call_target="tpu_custom_call" | custom-call | tf_op jit(solution)/shard_map/update/pallas_call | solution.py:1611
  125.0 1.2 slice.3
  126.2 1.9 %copy.68 = f32[1,128,1024]{2,1,0:T(8,128)} copy(f32[1,128,1024]{2,1,0:T(8,128)} %bitcast.39) | data formatting | bytes 1048576
  128.1 0.0 copy-done
  128.1 0.8 copy.69
Async XLA Ops:
  113.6 14.5 %copy-start = (f32[128,1024]{1,0:T(8,128)S(1)}, f32[128,1024]{1,0:T(8,128)}, u32[]{:S(2)}) copy-start(f32[128,1024]{1,0:T(8,128)} %get-tuple-element.70) | copy-start | bytes 1572868

commit v5 on v4

--- a/solution.py
+++ b/solution.py
@@ -557,7 +557,7 @@
     )(starts, tokens, cot, gain, in_proj, out_proj, conv, cbias, x_proj, dt_proj, dtbias, rates)
 
 
-PACKED = (R + 2 * N, R, N, K, 1, 1, 1, 1)
+PACKED = (R, R + 2 * N, N, K, 1, 1, 1, 1)
 PACKED_ROWS = 192
 
 
@@ -602,7 +602,7 @@
     rates_ref,
     normed_rows,
     normed_sib,
-    cot_rows,
+    cot_half,
     cot_sib,
     inner,
     gates,
@@ -701,8 +701,10 @@
             "seq": 2 * level + lax.rem(side + other, 2),
         }
 
+    across = [levels - 1 - level, lax.rem(level + 2, levels), level + 1 - 2 * lax.rem(level, 2)]
+
     def line(turn):
-        return {"seq": 2 * lax.rem(level + turn, levels) + side}
+        return {"seq": 2 * across[turn - 1] + side}
 
     def remote(source, target, send, recv, device):
         return pltpu.make_async_remote_copy(
@@ -741,7 +743,7 @@
     stream = tokens_ref[...].astype(wide)
     inverse = lax.rsqrt(jnp.mean(stream * stream, axis=1, keepdims=True) + EPS)
     normed_rows[row] = (stream * inverse * gain_ref[...]).astype(low)
-    cot_rows[row] = cot_ref[...]
+    cot_half[row] = cot_ref[:, share(lax.rem(row, 2), D // 2)]
     rates_ref[...] = jnp.exp(alog_ref[...]) * (-1.0 / math.log(2.0))
 
     places = member * steps - 8 + lax.broadcasted_iota(jnp.int32, docid.shape, 0)
@@ -784,18 +786,36 @@
     def _():
         inner[0:halo, :] = jnp.zeros((halo, E), low)
 
-    row_copies = begin(
-        [
-            remote(
-                source.at[row],
-                source.at[row],
-                gather_wires.at[kind, 0, offset - 1],
-                gather_wires.at[kind, 1, offset - 1],
-                {"rows": partner("rows", offset)},
-            )
-            for kind, source in ((0, normed_rows), (1, cot_rows))
-            for offset in range(1, nrows)
-        ]
+    def gather_rows(kind, make, target):
+        return begin(
+            [
+                remote(
+                    make(partner("rows", offset)),
+                    target.at[row],
+                    gather_wires.at[kind, 0, offset - 1],
+                    gather_wires.at[kind, 1, offset - 1],
+                    {"rows": partner("rows", offset)},
+                )
+                for offset in range(1, nrows)
+            ]
+        )
+
+    def to_sibling(kind, source, target):
+        return begin(
+            [
+                remote(
+                    source,
+                    target,
+                    sib_wires.at[kind, 0],
+                    sib_wires.at[kind, 1],
+                    {"seq": 2 * level + 1 - side},
+                )
+            ]
+        )
+
+    normed_moves = gather_rows(0, lambda other: normed_rows.at[row], normed_rows)
+    cot_moves = gather_rows(
+        1, lambda other: cot_ref.at[:, share(lax.rem(other, 2), D // 2)], cot_half
     )
     for at in range(chunks):
         gates[:, span(at, chunk)] = project(chunks + at)
@@ -850,6 +870,9 @@
     inb[...] = jnp.broadcast_to(proj[:, R : R + N][:, :, None], inb.shape)
     outb[...] = jnp.broadcast_to(proj[:, R + N :][:, :, None], outb.shape)
 
+    def lanes(at, place):
+        return share(4 * at + place, LANES)
+
     def state_copy(direction, distance, at):
         offset = distance if direction == 0 else devices - distance
         return remote(
@@ -871,7 +894,7 @@
         )
 
     def to_neighbours(make):
-        for distance in range(1, reach + 1):
+        for distance in range(reach, 0, -1):
 
             @pl.when(member + distance < devices)
             def _():
@@ -913,7 +936,8 @@
     to_neighbours(sum_copy)
     zeros = [jnp.zeros((N, LANES), wide) for _ in range(4)]
     ones = [jnp.ones((N, LANES), wide) for _ in range(4)]
-    for at in range(chunks):
+    order = [(turn, lax.rem(row + turn, nrows)) for turn in [*range(1, nrows), 0]]
+    for _, at in order:
 
         def step(t, carry):
             hidden, decayed, pulled = carry
@@ -921,7 +945,7 @@
             new = ([], [], [])
             for place in range(4):
                 here = (4 * at + place, pl.ds(t, 1))
-                decay = jnp.exp2(ddec[here] * rates_ref[:, span(4 * at + place, LANES)])
+                decay = jnp.exp2(ddec[here] * rates_ref[:, lanes(at, place)])
                 new[0].append(decay * hidden[place] + drive[here] * in_row)
                 product = decay * decayed[place]
                 new[1].append(product)
@@ -933,8 +957,6 @@
         ends[1, at] = jnp.concatenate(pulled, axis=1).astype(low)
         to_neighbours(lambda direction, distance: state_copy(direction, distance, at))
     from_neighbours(sum_copy)
-    for at in range(chunks):
-        from_neighbours(lambda direction, distance: state_copy(direction, distance, at))
 
     def fold(values):
         return values[:half] + values[half:]
@@ -944,9 +966,6 @@
         for index in range(1, half):
             total = total + source[place, pl.ds(index, steps, stride=half), :]
         return total
-
-    def lanes(at, place):
-        return share(4 * at + place, LANES)
 
     def trade(kind, source, at, turn):
         copies = []
@@ -969,37 +988,34 @@
                 )
         return begin(copies)
 
-    def trade_gated(at, turn):
+    def trade_gated(at):
         copies = []
-        for jump in (turn % 2, turn % 2 + 2):
+        for turn in range(nrows):
             for other in range(2):
-                receiver = lax.rem(row + jump, nrows)
                 columns = share(
-                    4 * at + 2 * lax.rem(side + other, 2) + receiver // 2, LANES
+                    4 * at + 2 * lax.rem(side + other, 2) + partner("rows", turn) // 2, LANES
                 )
-                target = gated_got.at[at // 2, other, row]
-                if jump == 0 and other == 0:
+                target = gated_got.at[at, other, row]
+                if turn == 0 and other == 0:
                     copies.append(
-                        pltpu.make_async_copy(
-                            gated.at[:, columns], target, local.at[2 + turn // 2]
-                        )
+                        pltpu.make_async_copy(gated.at[:, columns], target, local.at[2 + at])
                     )
                 else:
                     copies.append(
                         remote(
                             gated.at[:, columns],
                             target,
-                            gated_wires.at[0, at // 2, 2 * jump + other],
-                            gated_wires.at[1, at // 2, 2 * jump + other],
-                            plane(jump, other),
+                            gated_wires.at[0, at, 2 * turn + other],
+                            gated_wires.at[1, at, 2 * turn + other],
+                            plane(turn, other),
                         )
                     )
         return begin(copies)
 
     gate_moves, gated_moves = [], []
-    order = [(turn, lax.rem(row + turn, nrows)) for turn in [*range(1, nrows), 0]]
     leavings = []
     for slot, (turn, at) in enumerate(order):
+        from_neighbours(lambda direction, distance: state_copy(direction, distance, at))
 
         def through(device, states):
             new = []
@@ -1039,21 +1055,7 @@
             back_gates[:, columns] = (back[:, columns].astype(wide) * y_full * slope).astype(low)
             small[spans[6][0] : spans[6][1], columns] = column_sum(grady[group] * act)
         gate_moves += trade(1, back_gates, at, turn)
-        gated_moves += trade_gated(at, turn)
-
-    settle(row_copies)
-    sib_moves = begin(
-        [
-            remote(
-                source,
-                target,
-                sib_wires.at[kind, 0],
-                sib_wires.at[kind, 1],
-                {"seq": 2 * level + 1 - side},
-            )
-            for kind, source, target in ((0, normed_rows, normed_sib), (1, cot_rows, cot_sib))
-        ]
-    )
+
 
     def in_grads(kind):
         total = None
@@ -1070,7 +1072,7 @@
         return begin(
             [
                 remote(
-                    gin_low.at[kind, share(lax.rem(level + turn, levels), D // levels), :],
+                    gin_low.at[kind, share(across[turn - 1], D // levels), :],
                     gin_got.at[kind, turn - 1],
                     line_wires.at[kind, 0, turn - 1],
                     line_wires.at[kind, 1, turn - 1],
@@ -1083,7 +1085,7 @@
     def squares(values):
         return jnp.sum(jnp.sum(values * values, axis=0, keepdims=True), axis=1, keepdims=True)
 
-    def in_share(kind):
+    def in_share(kind, before=None):
         total = gin_sum[kind, share(level, D // levels), :]
         for turn in range(levels - 1):
             total = total + gin_got[kind, turn].astype(wide)
@@ -1091,7 +1093,9 @@
         owned = D // devices
         columns = share(kind * devices + 2 * row + side, shard)
         gin_out[:, columns] = gin_pub[kind, share(side, owned), :]
-        copies = begin(
+        norm_part[...] += squares(total)
+        copies = [] if before is None else before()
+        copies += begin(
             [
                 remote(
                     gin_pub.at[kind, share(lax.rem(side + other, 2), owned), :],
@@ -1105,38 +1109,24 @@
                 if turn + other > 0
             ]
         )
-        norm_part[...] += squares(total)
         return copies
-
-    summing = lax.rem(level, 2) == lax.rem(row, 2)
-    idle = lax.rem(level, 2) != lax.rem(row, 2)
 
     def gout_copy(turn):
         return remote(
-            gout_low.at[lax.rem(level + turn, levels) // 2],
+            gout_low.at[across[turn - 1]],
             gout_got.at[turn - 1],
             gout_wires.at[0, turn - 1],
             gout_wires.at[1, turn - 1],
             line(turn),
         )
 
-    def gout_share_copy(turn):
-        rows_of = gout_out.at[share(row // 2, LANES), :]
-        return remote(
-            rows_of,
-            rows_of,
-            row_wires.at[2, 0, turn - 1],
-            row_wires.at[2, 1, turn - 1],
-            {"rows": partner("rows", turn)},
-        )
-
     def out_grads():
-        for piece in range(2):
+        for piece in range(levels):
             total = None
-            for other, cots in ((0, cot_rows), (1, cot_sib)):
+            for other, cots in ((0, cot_half), (1, cot_sib)):
                 part = lax.dot_general(
                     gated_got[piece, other].reshape(nrows * steps, LANES),
-                    cots[...].reshape(nrows * steps, D),
+                    cots[...].reshape(nrows * steps, D // 2),
                     (((0,), (0,)), ((), ())),
                     preferred_element_type=wide,
                 )
@@ -1144,45 +1134,25 @@
             gout_sum[piece] = total
             gout_low[piece] = total.astype(low)
 
-        @pl.when(summing)
-        def _():
-            gout_copy(2).start()
-
-        @pl.when(idle)
-        def _():
-            gout_copy(1).start()
-            gout_copy(3).start()
-
     def out_share():
-        @pl.when(idle)
-        def _():
-            gout_copy(1).wait_send()
-            gout_copy(3).wait_send()
-
-        @pl.when(summing)
-        def _():
-            gout_copy(2).wait_send()
-            for turn in range(1, levels):
-                gout_copy(turn).wait_recv()
-            total = gout_sum[level // 2]
-            for turn in range(levels - 1):
-                total = total + gout_got[turn].astype(wide)
-            gout_out[share(row // 2, LANES), :] = total.astype(low)
-            norm_part[...] += squares(total)
-            for turn in range(1, nrows):
-                gout_share_copy(turn).start()
-
-    def out_end():
-        @pl.when(summing)
-        def _():
-            for turn in range(1, nrows):
-                gout_share_copy(turn).wait_send()
-            gout_share_copy(2).wait_recv()
-
-        @pl.when(idle)
-        def _():
-            gout_share_copy(1).wait_recv()
-            gout_share_copy(3).wait_recv()
+        total = gout_sum[level]
+        for turn in range(levels - 1):
+            total = total + gout_got[turn].astype(wide)
+        mine = gout_out.at[share(row // 2, LANES), share(lax.rem(row, 2), D // 2)]
+        mine[...] = total.astype(low)
+        norm_part[...] += squares(total)
+        return begin(
+            [
+                remote(
+                    mine,
+                    mine,
+                    row_wires.at[2, 0, turn - 1],
+                    row_wires.at[2, 1, turn - 1],
+                    {"rows": partner("rows", turn)},
+                )
+                for turn in range(1, nrows)
+            ]
+        )
 
     for slot, (turn, at) in enumerate(order):
 
@@ -1237,42 +1207,83 @@
             (((1,), (1,)), ((), ())),
             preferred_element_type=wide,
         )
-        small[spans[1][0] : spans[1][1], share(at, chunk)] = lax.dot_general(
+        small[spans[0][0] : spans[0][1], share(at, chunk)] = lax.dot_general(
             rank_low[...], lows, (((0,), (0,)), ((), ())), preferred_element_type=wide
         )
-        if slot == chunks - 2:
+        if slot == 0:
+            settle(normed_moves)
+            normed_moves = to_sibling(0, normed_rows, normed_sib)
+            settle(cot_moves)
+            cot_moves = to_sibling(1, cot_half, cot_sib)
+            for _, chunk_at in order:
+                gated_moves += trade_gated(chunk_at)
+        if slot == chunks - 3:
+            settle(normed_moves)
             settle(gate_moves)
-            settle(sib_moves)
             gate_moves = in_grads(1)
-            settle(gated_moves)
-            out_grads()
-
-    def to_rows(kind, make):
+
+    parts = [(0, R // nrows), (R, (PACKED_ROWS - R) // nrows)]
+
+    def scatter_small(part):
+        begin_row, few = parts[part]
+        rows = pl.ds(begin_row, few * nrows)
+        small_low[rows, :] = small[rows, :].astype(low)
         return begin(
             [
                 remote(
-                    *make(partner("rows", offset), offset - 1),
-                    row_wires.at[kind, 0, offset - 1],
-                    row_wires.at[kind, 1, offset - 1],
-                    {"rows": partner("rows", offset)},
+                    small_low.at[pl.ds(begin_row + partner("rows", turn) * few, few), :],
+                    small_got.at[turn - 1, pl.ds(begin_row // nrows, few), :],
+                    row_wires.at[part, 0, turn - 1],
+                    row_wires.at[part, 1, turn - 1],
+                    {"rows": partner("rows", turn)},
                 )
-                for offset in range(1, nrows)
+                for turn in range(1, nrows)
             ]
         )
 
-    def to_seq(kind, make):
+    def trade_small(part):
+        begin_row, few = parts[part]
+        rows = pl.ds(begin_row // nrows, few)
+        total = small[pl.ds(pl.multiple_of(begin_row + row * few, few), few), :]
+        for turn in range(nrows - 1):
+            total = total + small_got[turn, rows, :].astype(wide)
+        small_part[rows, :] = total.astype(low)
         return begin(
             [
                 remote(
-                    *make(partner("seq", offset), offset - 1),
-                    seq_wires.at[kind, 0, offset - 1],
-                    seq_wires.at[kind, 1, offset - 1],
+                    small_part.at[rows, share(partner("seq", offset), shard)],
+                    small_seq.at[offset - 1, rows, :],
+                    seq_wires.at[part, 0, offset - 1],
+                    seq_wires.at[part, 1, offset - 1],
                     {"seq": partner("seq", offset)},
                 )
-                for offset in range(1, devices)
+                for offset in (4, 3, 5, 2, 6, 1, 7)
             ]
         )
 
+    def share_small(part):
+        begin_row, few = parts[part]
+        rows = pl.ds(begin_row // nrows, few)
+        total = small_part[rows, share(member, shard)].astype(wide)
+        for offset in range(devices - 1):
+            total = total + small_seq[offset, rows, :].astype(wide)
+        mine = pl.ds(pl.multiple_of(begin_row + row * few, few), few)
+        small_out[mine, :] = total.astype(low)
+        norm_part[...] += squares(total)
+        return begin(
+            [
+                remote(
+                    small_out.at[mine, :],
+                    small_out.at[mine, :],
+                    row_wires.at[3 + part, 0, turn - 1],
+                    row_wires.at[3 + part, 1, turn - 1],
+                    {"rows": partner("rows", turn)},
+                )
+                for turn in range(1, nrows)
+            ]
+        )
+
+    dt_moves = scatter_small(0)
     proj_back[:, :R] = rank_back[...].astype(low)
     proj_back[:, R : R + N] = jnp.sum(gin[...], axis=2).astype(low)
     proj_back[:, R + N :] = jnp.sum(gout[...], axis=2).astype(low)
@@ -1288,7 +1299,7 @@
             grad_conv[group, :steps, :] = (
                 drive[group] + pulled[:, place * LANES : (place + 1) * LANES]
             ) * slope
-        small[spans[0][0] : spans[0][1], span(at, chunk)] = lax.dot_general(
+        small[spans[1][0] : spans[1][1], span(at, chunk)] = lax.dot_general(
             proj_back[...],
             jnp.concatenate(lows, axis=1),
             (((0,), (0,)), ((), ())),
@@ -1310,6 +1321,9 @@
     def _():
         grad_conv[:, steps : steps + 8, :] = jnp.zeros((groups, 8, LANES), wide)
 
+    settle(cot_moves)
+    settle(gated_moves)
+    out_grads()
     output_ref[...] = stream + jnp.dot(
         gated[...], out_proj_buf[...], preferred_element_type=wide
     )
@@ -1330,6 +1344,7 @@
     def _():
         halo_back.wait_recv()
 
+    gout_moves = begin([gout_copy(turn) for turn in range(1, levels)])
     inner_moves = []
     for turn, at in order:
         for place in range(4):
@@ -1358,6 +1373,8 @@
             (((1,), (1,)), ((), ())),
             preferred_element_type=wide,
         )
+    settle(dt_moves)
+    dt_moves = trade_small(0)
     inverse = lax.rsqrt(jnp.mean(stream * stream, axis=1, keepdims=True) + EPS)
     grad_gain = column_sum(grad_normed * stream * inverse)
     owned = D // devices
@@ -1365,11 +1382,7 @@
         small[spans[7][0] : spans[7][1], index * shard : index * shard + owned] = grad_gain[
             :, index * owned : (index + 1) * owned
         ]
-    few = small_low.shape[0] // nrows
-    small_low[...] = small[...].astype(low)
-    small_moves = to_rows(
-        0, lambda other, at: (small_low.at[share(other, few), :], small_got.at[at])
-    )
+    small_moves = scatter_small(1)
     scaled = grad_normed * gain_ref[...]
     grad_ref[...] = (
         cot_ref[...].astype(wide)
@@ -1381,55 +1394,43 @@
         * jnp.mean(scaled * stream, axis=1, keepdims=True)
     )
 
+    settle(gate_moves)
+    gate_moves = in_share(1)
     settle(inner_moves)
     inner_moves = in_grads(0)
-
     settle(small_moves)
-    total = small[share(row, few), :]
-    for at in range(nrows - 1):
-        total = total + small_got[at].astype(wide)
-    small_part[...] = total.astype(low)
-    small_moves = to_seq(
-        0, lambda other, at: (small_part.at[:, share(other, shard)], small_seq.at[at])
-    )
-    out_share()
-    settle(gate_moves)
-    gate_moves = in_share(1)
-
+    small_moves = trade_small(1)
+    settle(gout_moves)
+    gout_moves = out_share()
+    settle(dt_moves)
+    dt_moves = share_small(0)
     settle(small_moves)
-    total = small_part[:, share(member, shard)].astype(wide)
-    for at in range(devices - 1):
-        total = total + small_seq[at].astype(wide)
-    small_out[share(row, few), :] = total.astype(low)
-    small_moves = to_rows(
-        1,
-        lambda other, at: (
-            small_out.at[share(row, few), :],
-            small_out.at[share(row, few), :],
-        ),
-    )
-    norm_part[...] += squares(total)
+    small_moves = share_small(1)
+
+    def spread_norm():
+        here = row * devices + member
+        norm_all[here] = jnp.broadcast_to(norm_part[...], (8, LANES))
+        return begin(
+            [
+                remote(
+                    norm_all.at[here],
+                    norm_all.at[here],
+                    norm_wires.at[0, offset - 1],
+                    norm_wires.at[1, offset - 1],
+                    other_device(offset),
+                )
+                for offset in range(1, everyone)
+            ]
+        )
 
     settle(inner_moves)
-    inner_moves = in_share(0)
-    here = row * devices + member
-    norm_all[here] = jnp.broadcast_to(norm_part[...], (8, LANES))
-    norm_moves = begin(
-        [
-            remote(
-                norm_all.at[here],
-                norm_all.at[here],
-                norm_wires.at[0, offset - 1],
-                norm_wires.at[1, offset - 1],
-                other_device(offset),
-            )
-            for offset in range(1, everyone)
-        ]
-    )
+    inner_moves = in_share(0, spread_norm)
+    norm_moves, inner_moves = inner_moves[: everyone - 1], inner_moves[everyone - 1 :]
     settle(norm_moves)
     norm_out[...] = jnp.sqrt(jnp.sum(norm_all[...], axis=0))
-    out_end()
+    settle(gout_moves)
     settle(gate_moves)
+    settle(dt_moves)
     settle(small_moves)
     settle(inner_moves)
 
@@ -1473,8 +1474,8 @@
             pltpu.VMEM((N, E), wide),
             gathered,
             gathered,
-            gathered,
-            gathered,
+            pltpu.VMEM((nrows, steps, D // 2), low),
+            pltpu.VMEM((nrows, steps, D // 2), low),
             pltpu.VMEM((steps + halo, E), low),
             flat,
             flat,
@@ -1504,11 +1505,11 @@
             pltpu.VMEM((groups, steps + 8, LANES), wide),
             pltpu.VMEM((steps, R), wide),
             pltpu.VMEM((steps, R + 2 * N), low),
-            pltpu.VMEM((2, 2, nrows, steps, LANES), low),
+            pltpu.VMEM((levels, 2, nrows, steps, LANES), low),
             pltpu.VMEM((2, 2, nrows, steps, shard), low),
-            pltpu.VMEM((2, LANES, D), wide),
-            pltpu.VMEM((2, LANES, D), low),
-            pltpu.VMEM((levels - 1, LANES, D), low),
+            pltpu.VMEM((levels, LANES, D // 2), wide),
+            pltpu.VMEM((levels, LANES, D // 2), low),
+            pltpu.VMEM((levels - 1, LANES, D // 2), low),
             pltpu.VMEM((2, D, shard), wide),
             pltpu.VMEM((2, D, shard), low),
             pltpu.VMEM((2, levels - 1, D // levels, shard), low),
@@ -1526,15 +1527,15 @@
             dma((2, 2, reach)),
             dma((2, 2, nrows - 1)),
             dma((2, 2)),
-            dma((2, 2, 2 * nrows)),
+            dma((2, levels, 2 * nrows)),
             dma((2, 2, 2 * nrows)),
             dma((2, levels - 1)),
             dma((2, 2, levels - 1)),
             dma((2, 2, 2 * nrows)),
-            dma((3, 2, nrows - 1)),
-            dma((1, 2, devices - 1)),
+            dma((5, 2, nrows - 1)),
+            dma((2, 2, devices - 1)),
             dma((2, nrows * devices - 1)),
-            dma((4,)),
+            dma((2 + levels,)),
         ],
         compiler_params=pltpu.CompilerParams(
             collective_id=1, has_side_effects=True, vmem_limit_bytes=63 * 2**20
@@ -1544,7 +1545,16 @@
 
 
 def update_kernel(member_ref, norm_ref, gin_ref, gout_ref, small_ref, *refs):
-    weights, moments, averages, outs = refs[:10], refs[10:20], refs[20:30], refs[30:]
+    passed, weights, moments, averages, outs = (
+        refs[:2],
+        refs[2:12],
+        refs[12:22],
+        refs[22:32],
+        refs[32:],
+    )
+    outs[30][...] = passed[0][...]
+    outs[31][...] = passed[1][...]
+    outs[32][...] = norm_ref[0:1, 0:1]
     shrink_by = 1.0 / jnp.maximum(norm_ref[0:1, 0:1], 1.0)
 
     def renew(ordinal, grad, at=Ellipsis):
@@ -1568,8 +1578,8 @@
             return small_ref[spans[index][0] : spans[index][1], :].astype(jnp.float32)
 
         small = small_ref[...].astype(jnp.float32)
-        renew(4, part(0))
-        renew(5, part(1))
+        renew(5, part(0))
+        renew(4, part(1))
         renew(7, part(2))
         renew(2, part(3))
         for ordinal, index in ((3, 4), (6, 5), (8, 6)):
@@ -1578,10 +1588,10 @@
         renew(0, gain)
 
 
-def update_of(member, norm_tile, gin, gout, small, weights, moments, averages):
+def update_of(member, norm_tile, gin, gout, small, passed, weights, moments, averages):
     inner = gin.shape[0]
     channels = gout.shape[0]
-    blocks = 8
+    blocks = 2
     outer = channels // blocks
     block = gin.shape[1] // blocks
     flat = (0, 3, 6, 8)
@@ -1608,6 +1618,8 @@
     averages = [rows_of(array, ordinal) for ordinal, array in enumerate(averages)]
     shapes = [array.shape for array in moments]
     shards = [shard(shape, ordinal) for ordinal, shape in enumerate(shapes)]
+    steps, depth = passed[0].shape
+    through = pl.BlockSpec((steps // blocks, depth), lambda j, m: (j, 0))
     outs = pl.pallas_call(
         update_kernel,
         grid_spec=pltpu.PrefetchScalarGridSpec(
@@ -1618,23 +1630,28 @@
                 pl.BlockSpec((inner, block), lambda j, m: (0, j)),
                 pl.BlockSpec((outer, gout.shape[1]), lambda j, m: (j, 0)),
                 pl.BlockSpec(small.shape, lambda j, m: (0, 0)),
+                through,
+                through,
             ]
             + [weight(shape, ordinal) for ordinal, shape in enumerate(shapes)]
             + shards
             + shards,
-            out_specs=[shards[ordinal] for ordinal in range(10) for _ in range(3)],
+            out_specs=[shards[ordinal] for ordinal in range(10) for _ in range(3)]
+            + [through, through, pl.BlockSpec((1, 1), lambda j, m: (0, 0))],
         ),
         out_shape=[
             jax.ShapeDtypeStruct(shapes[ordinal], jnp.float32)
             for ordinal in range(10)
             for _ in range(3)
-        ],
+        ]
+        + [jax.ShapeDtypeStruct(array.shape, array.dtype) for array in passed]
+        + [jax.ShapeDtypeStruct((1, 1), jnp.float32)],
         compiler_params=pltpu.CompilerParams(vmem_limit_bytes=63 * 2**20),
         name="update",
-    )(member, norm_tile, gin, gout, small, *weights, *moments, *averages)
-    return [
+    )(member, norm_tile, gin, gout, small, *passed, *weights, *moments, *averages)
+    return outs[30:], [
         out.reshape(-1) if index // 3 in flat else out.T if index // 3 == 4 else out
-        for index, out in enumerate(outs)
+        for index, out in enumerate(outs[:30])
     ]
 
 
@@ -1740,10 +1757,18 @@
             nrows,
             devices,
         )
-        updated = update_of(
-            member_word, norm_tile, gin_share, gout_share, small, weights, moments, averages
-        )
-        return (block_output[None], input_grad[None], norm_tile[0, 0], *updated)
+        (block_output, input_grad, grad_norm), updated = update_of(
+            member_word,
+            norm_tile,
+            gin_share,
+            gout_share,
+            small,
+            (block_output, input_grad),
+            weights,
+            moments,
+            averages,
+        )
+        return (block_output[None], input_grad[None], grad_norm.reshape(()), *updated)
     inverse = lax.rsqrt(jnp.mean(stream * stream, axis=1, keepdims=True) + EPS)
     rates = -jnp.exp(a_log)
     scaled_rates = rates * (1.0 / math.log(2.0))
@@ -1867,8 +1892,8 @@
     )
     small = jnp.concatenate(
         [
+            grad_dtproj,
             grad_xproj.T,
-            grad_dtproj,
             grad_alog,
             grad_convw,
             grad_conv_bias[None],
@@ -1908,8 +1933,8 @@
         gin_share.astype(jnp.float32),
         parts[3],
         parts[4][0],
-        parts[0].T,
-        parts[1],
+        parts[1].T,
+        parts[0],
         parts[5][0],
         parts[2],
         parts[6][0],

time: 129 us -> 101 us (0.78)
  the two profiles are of different devices: /device:TPU:9 before, /device:TPU:0 now
where the time goes in v5:
time: 101 us
  Pallas kernels  100 us (99%)
    pallas_call x1, Pallas kernels, block_of(): pl.pallas_call(functools.partial(block_kernel, nrows, devices), in_specs=...  91.5 us
    pallas_call x1, Pallas kernels, update_of(): pl.pallas_call(update_kernel, grid_spec=pltpu.PrefetchScalarGridSpec(num_...  8.79 us

profile of v5, /device:TPU:0, one launch (start us, length us, event | category | flops | bytes accessed | tf_op | source)
XLA Modules:
  0.0 101.2 jit_solution(13530838639114495318)
XLA Ops:
  0.7 91.5 %block.1 = (f32[128,1024]{1,0:T(8,128)}, f32[128,1024]{1,0:T(8,128)}, bf16[128,4096]{1,0:T(8,128)(2,1)}, bf16[256,1024]{1,0:T(8,128)(2,1)}, bf16[192,256]{1,0:T(8,128)(2,1)}, /*index=5*/f32[8,128]{1,0:T(8,128)}) custom-call(s32[1,8]{1,0:T(1,128)} %lengths_ref.1, bf16[128,1024]{1,0:T(8,128)(2,1)} %bitcast.38, bf16[128,1024]{1,0:T(8,128)(2,1)} %bitcast.39, ...), custom_call_target="tpu_custom_call" | custom-call | tf_op jit(solution)/shard_map/block/pallas_call | solution.py:1459
  92.2 8.8 %update.1 = (f32[1,128]{1,0:T(1,128)}, f32[1,128]{1,0:T(1,128)}, f32[1,128]{1,0:T(1,128)}, f32[128,4096]{1,0:T(8,128)}, f32[128,4096]{1,0:T(8,128)}, /*index=5*/...) custom-call(s32[1]{0:T(128)} %bitcast.member_ref, ...), custom_call_target="tpu_custom_call" | custom-call | tf_op jit(solution)/shard_map/update/pallas_call | solution.py:1623

commit v6 on v5

--- a/solution.py
+++ b/solution.py
@@ -952,7 +952,7 @@
                 new[2].append(pulled[place] + product * (grady[here] * out_row))
             return new
 
-        hidden, _, pulled = lax.fori_loop(0, steps, step, (zeros, ones, zeros), unroll=4)
+        hidden, _, pulled = lax.fori_loop(0, steps, step, (zeros, ones, zeros), unroll=8)
         ends[0, at] = jnp.concatenate(hidden, axis=1).astype(low)
         ends[1, at] = jnp.concatenate(pulled, axis=1).astype(low)
         to_neighbours(lambda direction, distance: state_copy(direction, distance, at))
@@ -1045,7 +1045,7 @@
         leavings.append(lax.fori_loop(0, last - member, lambda d, s: through(last - d, s), zeros))
         for place in range(4):
             kept[slot, 0, place] = entering[place].astype(low)
-        lax.fori_loop(0, steps, forward, entering, unroll=4)
+        lax.fori_loop(0, steps, forward, entering, unroll=8)
         for place in range(4):
             group, columns = 4 * at + place, lanes(at, place)
             act = silu(pre_act[group])
@@ -1184,7 +1184,7 @@
 
         ending = [kept[slot, steps, place].astype(wide) for place in range(4)]
         _, grates, _ = lax.fori_loop(
-            0, steps, backward, (leavings[slot], zeros, ending), unroll=4
+            0, steps, backward, (leavings[slot], zeros, ending), unroll=8
         )
         lows = []
         for place in range(4):
@@ -1324,6 +1324,7 @@
     settle(cot_moves)
     settle(gated_moves)
     out_grads()
+    gout_moves = begin([gout_copy(turn) for turn in range(1, levels)])
     output_ref[...] = stream + jnp.dot(
         gated[...], out_proj_buf[...], preferred_element_type=wide
     )
@@ -1344,7 +1345,6 @@
     def _():
         halo_back.wait_recv()
 
-    gout_moves = begin([gout_copy(turn) for turn in range(1, levels)])
     inner_moves = []
     for turn, at in order:
         for place in range(4):

time: 101 us -> 99.2 us (0.982)
  Pallas kernels: 100 us -> 98.2 us
    pallas_call x1, Pallas kernels: 91.5 us -> 89.4 us  [block_of(): pl.pallas_call(functools.partial(block_kernel, nrows, devices), in_specs=...]
where the time goes in v6:
time: 99.2 us; the launch traced here: 99.1 us
  Pallas kernels  98.2 us (99%)
    pallas_call x1, Pallas kernels, block_of(): pl.pallas_call(functools.partial(block_kernel, nrows, devices), in_specs=...  89.4 us
    pallas_call x1, Pallas kernels, update_of(): pl.pallas_call(update_kernel, grid_spec=pltpu.PrefetchScalarGridSpec(num_...  8.79 us

profile of v6, /device:TPU:0, one launch (start us, length us, event | category | flops | bytes accessed | tf_op | source)
XLA Modules:
  0.0 99.1 jit_solution(14357150379894077606)
XLA Ops:
  0.7 89.4 %block.1 = (f32[128,1024]{1,0:T(8,128)}, f32[128,1024]{1,0:T(8,128)}, bf16[128,4096]{1,0:T(8,128)(2,1)}, bf16[256,1024]{1,0:T(8,128)(2,1)}, bf16[192,256]{1,0:T(8,128)(2,1)}, /*index=5*/f32[8,128]{1,0:T(8,128)}) custom-call(s32[1,8]{1,0:T(1,128)} %lengths_ref.1, bf16[128,1024]{1,0:T(8,128)(2,1)} %bitcast.38, bf16[128,1024]{1,0:T(8,128)(2,1)} %bitcast.39, ...), custom_call_target="tpu_custom_call" | custom-call | tf_op jit(solution)/shard_map/block/pallas_call | solution.py:1459
  90.1 8.8 %update.1 = (f32[1,128]{1,0:T(1,128)}, f32[1,128]{1,0:T(1,128)}, f32[1,128]{1,0:T(1,128)}, f32[128,4096]{1,0:T(8,128)}, f32[128,4096]{1,0:T(8,128)}, /*index=5*/...) custom-call(s32[1]{0:T(128)} %bitcast.member_ref, ...), custom_call_target="tpu_custom_call" | custom-call | tf_op jit(solution)/shard_map/update/pallas_call | solution.py:1623

commit v7 on v6

--- a/solution.py
+++ b/solution.py
@@ -591,12 +591,14 @@
     dtbias_ref,
     alog_ref,
     dskip_ref,
-    output_ref,
-    grad_ref,
+    output_out,
+    grad_out,
     gin_out,
     gout_out,
     small_out,
     norm_out,
+    output_ref,
+    grad_ref,
     in_proj_buf,
     out_proj_buf,
     rates_ref,
@@ -1396,6 +1398,12 @@
 
     settle(gate_moves)
     gate_moves = in_share(1)
+    position_moves = begin(
+        [
+            pltpu.make_async_copy(output_ref, output_out, local.at[2 + levels]),
+            pltpu.make_async_copy(grad_ref, grad_out, local.at[3 + levels]),
+        ]
+    )
     settle(inner_moves)
     inner_moves = in_grads(0)
     settle(small_moves)
@@ -1426,6 +1434,7 @@
     settle(inner_moves)
     inner_moves = in_share(0, spread_norm)
     norm_moves, inner_moves = inner_moves[: everyone - 1], inner_moves[everyone - 1 :]
+    settle(position_moves)
     settle(norm_moves)
     norm_out[...] = jnp.sqrt(jnp.sum(norm_all[...], axis=0))
     settle(gout_moves)
@@ -1459,7 +1468,7 @@
     return pl.pallas_call(
         functools.partial(block_kernel, nrows, devices),
         in_specs=specs,
-        out_specs=[vmem] * 6,
+        out_specs=[pl.BlockSpec(memory_space=pl.ANY)] * 2 + [vmem] * 4,
         out_shape=[
             jax.ShapeDtypeStruct((steps, D), wide),
             jax.ShapeDtypeStruct((steps, D), wide),
@@ -1469,6 +1478,8 @@
             jax.ShapeDtypeStruct((8, LANES), wide),
         ],
         scratch_shapes=[
+            pltpu.VMEM((steps, D), wide),
+            pltpu.VMEM((steps, D), wide),
             pltpu.VMEM((2 * chunks, D, chunk), low),
             pltpu.VMEM((E, D), low),
             pltpu.VMEM((N, E), wide),
@@ -1535,7 +1546,7 @@
             dma((5, 2, nrows - 1)),
             dma((2, 2, devices - 1)),
             dma((2, nrows * devices - 1)),
-            dma((2 + levels,)),
+            dma((4 + levels,)),
         ],
         compiler_params=pltpu.CompilerParams(
             collective_id=1, has_side_effects=True, vmem_limit_bytes=63 * 2**20

time: 99.2 us -> 98.9 us (level)
  no operation moved by 1% of the time
where the time goes in v7:
time: 98.9 us; the launch traced here: 98.7 us
  Pallas kernels  97.9 us (99%)
    pallas_call x1, Pallas kernels, block_of(): pl.pallas_call(functools.partial(block_kernel, nrows, devices), in_specs=...  89.1 us
    pallas_call x1, Pallas kernels, update_of(): pl.pallas_call(update_kernel, grid_spec=pltpu.PrefetchScalarGridSpec(num_...  8.79 us

profile of v7, /device:TPU:0, one launch (start us, length us, event | category | flops | bytes accessed | tf_op | source)
XLA Modules:
  0.0 98.7 jit_solution(14657354071822099518)
XLA Ops:
  0.7 89.1 %block.1 = (f32[128,1024]{1,0:T(8,128)}, f32[128,1024]{1,0:T(8,128)}, bf16[128,4096]{1,0:T(8,128)(2,1)}, bf16[256,1024]{1,0:T(8,128)(2,1)}, bf16[192,256]{1,0:T(8,128)(2,1)}, /*index=5*/f32[8,128]{1,0:T(8,128)}) custom-call(s32[1,8]{1,0:T(1,128)} %lengths_ref.1, bf16[128,1024]{1,0:T(8,128)(2,1)} %bitcast.38, bf16[128,1024]{1,0:T(8,128)(2,1)} %bitcast.39, ...), custom_call_target="tpu_custom_call" | custom-call | tf_op jit(solution)/shard_map/block/pallas_call | solution.py:1468
  89.8 8.8 %update.1 = (f32[1,128]{1,0:T(1,128)}, f32[1,128]{1,0:T(1,128)}, f32[1,128]{1,0:T(1,128)}, f32[128,4096]{1,0:T(8,128)}, f32[128,4096]{1,0:T(8,128)}, /*index=5*/...) custom-call(s32[1]{0:T(128)} %bitcast.member_ref, ...), custom_call_target="tpu_custom_call" | custom-call | tf_op jit(solution)/shard_map/update/pallas_call | solution.py:1634
